TPU v7x, 128 devices: a whole 4x4x4 slice. The times are simulated.
128 devices in a mesh: grp: 2 (over x_lo), row: 8 (over y, core), col: 8 (over x_hi, z).
Axes of the slice: x: 4 (x_hi: 2, x_lo: 2; x = x_hi * 2 + x_lo), y: 4, z: 4, core: 2. Of those that a mesh axis runs over, the one named last changes fastest.
Arguments:
- pair_state: bfloat16 [768, 768, 128], P(('grp', 'row'), 'col'), may hold values from -6 to 6
- pair_mask: int32 [768], replicated, may hold values 0 or 1
- chain_ids: int32 [768], replicated, may hold values from 0 to 3, never falling along the last dimension, each value on 1 to 384 neighbouring positions
- tokens: bfloat16 [48, 768, 768], P(('grp', 'row')), may hold values from -6 to 6
- grad_attn: bfloat16 [48, 768, 768], P(('grp', 'row')), may hold values from -192 to 192
- norm_pair: bfloat16 [128], replicated, may hold values from 0.099609375 to 1.8984375
- proj_left: bfloat16 [128, 128], replicated, may hold values from -0.5 to 0.5
- gate_left: bfloat16 [128, 128], replicated, may hold values from -0.5 to 0.5
- proj_right: bfloat16 [128, 128], replicated, may hold values from -0.5 to 0.5
- gate_right: bfloat16 [128, 128], replicated, may hold values from -0.5 to 0.5
- gate_out: bfloat16 [128, 128], replicated, may hold values from -0.5 to 0.5
- norm_tri: bfloat16 [128], replicated, may hold values from 0.099609375 to 1.8984375
- tri_out: bfloat16 [128, 128], replicated, may hold values from -1.0546875 to 1.0546875
- norm_bias: bfloat16 [128], replicated, may hold values from 0.099609375 to 1.8984375
- bias_proj: bfloat16 [128, 16], replicated, may hold values from -0.5 to 0.5
- chain_weight: float32 [16], replicated, may hold values from -2 to 2
- norm_tokens: bfloat16 [768], replicated, may hold values from 0.099609375 to 1.8984375
- w_query: bfloat16 [768, 768], P(None, 'col'), may hold values from -0.21875 to 0.21875
- w_key: bfloat16 [768, 768], P(None, 'col'), may hold values from -0.21875 to 0.21875
- w_value: bfloat16 [768, 768], P(None, 'col'), may hold values from -0.21875 to 0.21875
- w_out: bfloat16 [768, 768], P('col'), may hold values from -0.21875 to 0.21875
- norm_ff: bfloat16 [768], replicated, may hold values from 0.099609375 to 1.8984375
- ff_gate: bfloat16 [768, 1536], replicated, may hold values from -0.21875 to 0.21875
- ff_up: bfloat16 [768, 1536], replicated, may hold values from -0.21875 to 0.21875
- ff_down: bfloat16 [1536, 768], replicated, may hold values from -0.15625 to 0.15625
Outputs:
- pair_out: float32 [768, 768, 128], P(('grp', 'row'), 'col')
- refined: float32 [48, 768, 768], P(('grp', 'row'), 'col')
- pair_grad: float32 [768, 768, 128], P(('grp', 'row'), 'col')
All inputs are finite; a program needn't handle non-finite values.
Results may differ from a plain program's by a relative error of at most 0.03.
Values may be sent and summed in bfloat16 or wider, within the bound.
No kernel may reach another device: no remote copies, remote signals or barrier semaphores. Data moves between devices by JAX's collectives and lax.ppermute only.
A program may use at most 192 MiB of HBM per device.

v0:
```python
import jax
import jax.numpy as jnp
from jax import lax
from jax.sharding import PartitionSpec as P

HD = 48


def layer_norm(value_rows, gain_vec):
    middle = value_rows - jnp.mean(value_rows, axis=-1, keepdims=True)
    spread = jnp.mean(middle * middle, axis=-1, keepdims=True)
    return middle * lax.rsqrt(spread + 1e-05) * gain_vec.astype(jnp.float32)


def matmul(left_side, right_side):
    return jnp.dot(left_side, right_side, preferred_element_type=jnp.float32)


def gated(flat_normed, proj_weight, gate_weight, tile_mask, tile_shape):
    gated_rows = jax.nn.sigmoid(matmul(flat_normed, gate_weight)) * matmul(flat_normed, proj_weight)
    return (gated_rows.reshape(tile_shape) * tile_mask).astype(jnp.bfloat16)


def body(
    pair_state,
    pair_mask,
    chain_ids,
    tokens,
    grad_attn,
    norm_pair,
    proj_left,
    gate_left,
    proj_right,
    gate_right,
    gate_out,
    norm_tri,
    tri_out,
    norm_bias,
    bias_proj,
    chain_weight,
    norm_tokens,
    w_query,
    w_key,
    w_value,
    w_out,
    norm_ff,
    ff_gate,
    ff_up,
    ff_down,
):
    tile_rows, tile_cols, channels = pair_state.shape
    head_count = bias_proj.shape[1]
    row_start = lax.axis_index(("grp", "row")) * tile_rows
    col_index = lax.axis_index("col")
    col_start = col_index * tile_cols
    mask_float = pair_mask.astype(jnp.float32)
    row_mask = lax.dynamic_slice_in_dim(mask_float, row_start, tile_rows)
    col_mask = lax.dynamic_slice_in_dim(mask_float, col_start, tile_cols)
    tile_mask = (row_mask[:, None] * col_mask[None, :])[:, :, None]
    pair_float = pair_state.astype(jnp.float32)
    normed = (
        layer_norm(pair_float, norm_pair)
        .astype(jnp.bfloat16)
        .reshape(tile_rows * tile_cols, channels)
    )
    left_tile = gated(normed, proj_left, gate_left, tile_mask, pair_state.shape)
    right_tile = gated(normed, proj_right, gate_right, tile_mask, pair_state.shape)
    right_all = lax.all_gather(right_tile, ("grp", "row"), axis=0, tiled=True)
    tri_flip = lax.psum_scatter(
        jnp.einsum("jkc,ikc->jic", right_all, left_tile, preferred_element_type=jnp.float32).astype(
            jnp.bfloat16
        ),
        "col",
        scatter_dimension=0,
        tiled=True,
    ).astype(jnp.float32)
    tri_total = jnp.transpose(tri_flip, (1, 0, 2))
    tri_normed = (
        layer_norm(tri_total, norm_tri)
        .astype(jnp.bfloat16)
        .reshape(tile_rows * tile_cols, channels)
    )
    update = jax.nn.sigmoid(matmul(normed, gate_out)) * matmul(tri_normed, tri_out)
    pair_out = pair_float + update.reshape(pair_state.shape)
    bias_in = (
        layer_norm(pair_out, norm_bias)
        .astype(jnp.bfloat16)
        .reshape(tile_rows * tile_cols, channels)
    )
    bias_tile = (
        matmul(bias_in, bias_proj).astype(jnp.bfloat16).reshape(tile_rows, tile_cols, head_count)
    )
    bias_part = lax.all_to_all(bias_tile, "col", split_axis=2, concat_axis=1, tiled=True)
    bias_full = lax.all_gather(bias_part, ("grp", "row"), axis=0, tiled=True)
    samples, seq_len, model_width = tokens.shape
    share_len = seq_len // lax.axis_size("col")
    local_heads = w_query.shape[1] // HD
    head_weight = lax.dynamic_slice_in_dim(chain_weight, col_index * local_heads, local_heads)
    same_chain = (chain_ids[:, None] == chain_ids[None, :]).astype(jnp.float32)
    extra_terms = (
        jnp.transpose(bias_full.astype(jnp.float32), (2, 0, 1))
        + head_weight[:, None, None] * same_chain[None]
    )
    token_float = tokens.astype(jnp.float32)
    token_norm = (
        layer_norm(token_float, norm_tokens)
        .astype(jnp.bfloat16)
        .reshape(samples * seq_len, model_width)
    )

    def heads_of(weight):
        return (
            matmul(token_norm, weight)
            .astype(jnp.bfloat16)
            .reshape(samples, seq_len, local_heads, HD)
        )

    query_rows = heads_of(w_query)
    key_rows = heads_of(w_key)
    value_rows = heads_of(w_value)
    logit_scores = (
        jnp.einsum("snhd,smhd->shnm", query_rows, key_rows, preferred_element_type=jnp.float32)
        * HD ** (-0.5)
        + extra_terms[None]
    )
    weights = jnp.exp(logit_scores)
    probabilities = weights / jnp.sum(weights, axis=-1, keepdims=True)
    mixed_output = jnp.einsum(
        "shnm,smhd->snhd",
        probabilities.astype(jnp.bfloat16),
        value_rows,
        preferred_element_type=jnp.float32,
    )
    mixed_output = mixed_output.astype(jnp.bfloat16).reshape(samples, seq_len, local_heads * HD)
    attn_part = matmul(mixed_output.reshape(samples * seq_len, local_heads * HD), w_out).reshape(
        samples, seq_len, model_width
    )
    attn_all = lax.psum(attn_part.astype(jnp.bfloat16), "col").astype(jnp.float32)
    attn_share = lax.dynamic_slice_in_dim(attn_all, col_index * share_len, share_len, 1)
    token_share = lax.dynamic_slice_in_dim(token_float, col_index * share_len, share_len, 1)
    state = token_share + attn_share
    ff_in = (
        layer_norm(state, norm_ff).astype(jnp.bfloat16).reshape(samples * share_len, model_width)
    )
    hidden = (jax.nn.silu(matmul(ff_in, ff_gate)) * matmul(ff_in, ff_up)).astype(jnp.bfloat16)
    refined = state + matmul(hidden, ff_down).reshape(samples, share_len, model_width)
    grad_flat = grad_attn.reshape(samples * seq_len, model_width)
    head_gradient = jnp.dot(grad_flat, w_out.T, preferred_element_type=jnp.float32)
    head_gradient = head_gradient.astype(jnp.bfloat16).reshape(samples, seq_len, local_heads, HD)
    probability_gradient = jnp.einsum(
        "snhd,smhd->shnm", head_gradient, value_rows, preferred_element_type=jnp.float32
    )
    score_grad = probabilities * (
        probability_gradient - jnp.sum(probabilities * probability_gradient, axis=-1, keepdims=True)
    )
    bias_grad = jnp.transpose(jnp.sum(score_grad, axis=0), (1, 2, 0))
    swapped = lax.all_to_all(
        bias_grad.astype(jnp.bfloat16), "col", split_axis=1, concat_axis=2, tiled=True
    ).astype(bias_grad.dtype)
    tile_grad = lax.psum_scatter(
        swapped.astype(jnp.bfloat16), ("grp", "row"), scatter_dimension=0, tiled=True
    ).astype(jnp.float32)
    pair_grad = jnp.dot(
        tile_grad.reshape(tile_rows * tile_cols, head_count),
        bias_proj.astype(jnp.float32).T,
        precision=lax.Precision.HIGHEST,
    )
    pair_grad = pair_grad.reshape(tile_rows, tile_cols, channels)
    return (pair_out, refined, pair_grad)


def solution(mesh):
    return jax.shard_map(
        body,
        mesh=mesh,
        in_specs=(
            P(("grp", "row"), "col", None),
            P(),
            P(),
            P(("grp", "row"), None, None),
            P(("grp", "row"), None, None),
            P(),
            P(),
            P(),
            P(),
            P(),
            P(),
            P(),
            P(),
            P(),
            P(),
            P(),
            P(),
            P(None, "col"),
            P(None, "col"),
            P(None, "col"),
            P("col", None),
            P(),
            P(),
            P(),
            P(),
        ),
        out_specs=(
            P(("grp", "row"), "col", None),
            P(("grp", "row"), "col", None),
            P(("grp", "row"), "col", None),
        ),
        check_vma=False,
    )
```

profile of v0, /device:TPU:1, one launch (start us, length us, event | category | flops | bytes accessed | tf_op | source)
XLA Modules:
  0.0 598.7 jit_solution(14858763261334845973)
XLA Ops:
  7.2 0.8 convert_element_type.106
  8.2 1.9 convert_reduce_fusion.1
  10.1 2.7 fusion.18
  12.9 1.5 fusion.20
  14.4 0.8 fusion.14
  15.4 1.9 convolution_multiply_fusion.1
  17.2 3.5 copy.91
  20.8 0.6 copy-done.18
  21.4 3.3 multiply_convert_fusion.1
  24.8 2.1 fusion.13
  26.9 1.9 convolution_multiply_fusion.2
  28.8 3.5 copy.90
  32.2 127.3 %all-gather.3.cloned.1.call-done = bf16[768,96,128]{1,0,2:T(8,128)(2,1)} async-done(((bf16[48,96,128]{1,0,2:T(8,128)(2,1)}), bf16[768,96,128]{1,0,2:T(8,128)(2,1)}) %all-gather.3.cloned.1.call-update) | async-done | bytes 18874384 | tf_op jit(solution)/shard_map/all_gather | solution.py:68
  159.5 17.8 %convert_bitcast_fusion = bf16[768,48,128]{0,1,2:T(8,128)(2,1)} fusion(bf16[768,96,128]{1,0,2:T(8,128)(2,1)} %all-gather.3.cloned.1.call-done, f32[48,96,128]{1,0,2:T(8,128)} %copy.90, f32[48,96]{1,0:T(8,128)} %copy-done.18), kind=kOutput, calls=%fused_computation.7 | convolution fusion | flops 911867904 | bytes 30689280 | tf_op jit(solution)/shard_map/jkc,ikc->jic/dot_general | solution.py:70
  177.3 14.0 %copy.92 = bf16[768,48,128]{2,1,0:T(8,128)(2,1)} copy(bf16[768,48,128]{0,1,2:T(8,128)(2,1)} %convert_bitcast_fusion) | data formatting | bytes 18874368 | tf_op jit(solution)/shard_map/convert_element_type | solution.py:70
  192.0 3.5 fusion.12
  195.4 120.6 %reduce-scatter.3.cloned.1.call-done = bf16[96,48,128]{2,1,0:T(8,128)(2,1)} async-done(((bf16[768,48,128]{2,1,0:T(8,128)(2,1)}), bf16[96,48,128]{2,1,0:T(8,128)(2,1)}) %reduce-scatter.3.cloned.1.call-update) | async-done | bytes 1179664 | tf_op jit(solution)/shard_map/reduce_scatter | solution.py:69
  316.0 2.3 bitcast_reduce_fusion
  318.3 2.7 fusion.23
  321.1 1.7 fusion.25
  322.8 0.5 convolution_multiply_fusion
  323.3 0.8 copy-done.8
  324.1 0.9 fusion.55
  325.0 1.7 multiply_reduce_fusion.3
  326.7 1.5 multiply_convert_fusion.3
  328.2 1.1 convolution_convert_fusion
  329.3 1.8 reshape.192
  331.0 10.6 %all_to_all.36 = bf16[48,96,16]{1,0,2:T(8,128)(2,1)S(1)} all-to-all(bf16[48,96,16]{1,0,2:T(8,128)(2,1)} %reshape.192), channel_id=1, replica_groups=mesh['grp'=2,'row'=8,'col'=8] {'col'}, dimensions={2} | all-to-all | bytes 294912 | tf_op jit(solution)/shard_map/all_to_all | solution.py:93
  341.6 0.8 copy.139
  342.4 1.9 all_to_all.29
  344.4 2.7 convert_reduce_fusion
  347.4 1.2 multiply_reduce_fusion.2
  348.7 1.7 multiply_convert_fusion
  350.4 1.7 copy-done.2
  352.1 2.0 convolution_convert_fusion.3
  354.1 2.3 reshape.189
  356.4 4.0 convolution_convert_fusion.2
  360.4 2.2 reshape.190
  362.6 4.0 convolution_convert_fusion.4
  366.6 2.2 reshape.188
  368.9 2.9 convolution_convert_fusion.1
  371.8 1.6 reshape.196
  373.7 7.1 %fusion.32 = f32[3,2,768,768]{2,3,1,0:T(8,128)} fusion(bf16[3,768,2,48]{1,0,3,2:T(4,128)(2,1)S(1)} %reshape.196, bf16[3,768,2,48]{1,0,3,2:T(4,128)(2,1)S(1)} %copy-done.14), kind=kOutput, calls=%fused_computation.65 | convolution fusion | flops 339738624 | bytes 15040512 | tf_op jit(solution)/shard_map/snhd,smhd->shnm/dot_general | solution.py:150
  380.8 4.2 bitcast_add_fusion
  385.1 6.2 %copy.98 = f32[2,768,768]{1,2,0:T(8,128)} copy(f32[2,768,768]{2,1,0:T(8,128)} %bitcast_add_fusion) | data formatting | bytes 9437184 | tf_op jit(solution)/shard_map/add | solution.py:101
  391.2 5.7 fusion.3
  396.9 3.2 fusion.27
  400.2 1.9 copy-done.9
  402.1 2.9 convolution_convert_fusion.5
  405.0 21.6 %multiply_reduce_fusion = bf16[2,768,768]{1,2,0:T(8,128)(2,1)} fusion(f32[3,2,768,768]{2,3,1,0:T(8,128)} %fusion.32, f32[3,2,768]{2,1,0:T(2,128)S(1)} %get-tuple-element.5, f32[2,768,768]{1,2,0:T(8,128)} %copy.98, f32[3,2,768,768]{2,3,1,0:T(8,128)} %copy-done.9, bf16[3,768,2,48]{1,0,3,2:T(4,128)(2,1)S(1)} %copy-done.16, ...), kind=kOutput, calls=%fused_computation.1 | convolution fusion | flops 373953792 | bytes 36292608 | tf_op jit(solution)/shard_map/sub | solution.py:154
  426.6 4.1 copy.103
  430.8 47.4 %all_to_all.37 = bf16[768,768,2]{0,2,1:T(2,128)(2,1)S(1)} all-to-all(bf16[768,768,2]{0,2,1:T(2,128)(2,1)S(1)} %copy.103), channel_id=1, replica_groups=mesh['grp'=2,'row'=8,'col'=8] {'col'}, dimensions={1} | all-to-all | bytes 4718592 | tf_op jit(solution)/shard_map/all_to_all | solution.py:157
  478.4 1.6 copy.105
  480.0 5.1 copy.106
  485.2 3.5 convert_element_type.113
  488.7 35.1 %all-reduce.2.cloned.1.call-done = bf16[3,768,768]{2,1,0:T(8,128)(2,1)} async-done(((bf16[3,768,768]{2,1,0:T(8,128)(2,1)}), bf16[3,768,768]{2,1,0:T(8,128)(2,1)}) %all-reduce.2.cloned.1.call-update) | async-done | bytes 3538960 | tf_op jit(solution)/shard_map/psum | solution.py:138
  523.8 1.5 fusion.44
  525.3 1.6 multiply_reduce_fusion.4
  526.9 1.5 multiply_convert_fusion.5
  528.4 2.1 fusion.60
  530.5 5.5 fusion.30
  536.0 2.8 fusion.43
  538.8 50.3 %reduce-scatter.5.cloned.1.call-done = bf16[48,96,16]{1,2,0:T(8,128)(2,1)} async-done(((bf16[768,96,16]{1,2,0:T(8,128)(2,1)}), bf16[48,96,16]{1,2,0:T(8,128)(2,1)}) %reduce-scatter.5.cloned.1.call-update) | async-done | bytes 147472 | tf_op jit(solution)/shard_map/reduce_scatter | solution.py:160
  589.1 2.9 fusion.40
  (94 shorter events, 2.5 us)
Async XLA Ops:
  7.2 361.7 %copy-start = (bf16[3,768,768]{2,1,0:T(8,128)(2,1)S(1)}, bf16[3,768,768]{2,1,0:T(8,128)(2,1)}, u32[]{:S(2)}) copy-start(bf16[3,768,768]{2,1,0:T(8,128)(2,1)} %param.29) | copy-start | bytes 10616836
  7.2 5.7 copy-start.29
  7.2 152.3 %all-gather.3.cloned.1.call-start = ((), (), s32[]{:S(2)}) async-start(), calls=%async_computation.4 | async-start | bytes 26738688 | tf_op jit(solution)/shard_map/all_gather | solution.py:68
  8.2 4.7 copy-start.7
  8.2 6.1 %copy-start.28 = (bf16[128,128]{1,0:T(8,128)(2,1)S(1)}, bf16[128,128]{1,0:T(8,128)(2,1)}, u32[]{:S(2)}) copy-start(bf16[128,128]{1,0:T(8,128)(2,1)} %param.34) | copy-start | bytes 98308
  14.4 1.0 copy-start.11
  14.4 1.0 copy-start.20
  20.8 0.6 copy-start.18
  24.7 291.3 %reduce-scatter.3.cloned.1.call-start = ((), (), s32[]{:S(2)}) async-start(), calls=%async_computation.5 | async-start | bytes 10616832 | tf_op jit(solution)/shard_map/reduce_scatter | solution.py:69
  24.7 2.2 copy-start.12
  24.7 2.2 copy-start.21
  191.3 0.7 copy-start.30
  191.3 0.7 copy-start.31
  191.3 189.5 %all-gather.5.cloned.1.call-start = ((), (), s32[]{:S(2)}) async-start(), calls=%async_computation.6 | async-start | bytes 2506752 | tf_op jit(solution)/shard_map/all_gather | solution.py:94
  316.0 5.1 copy-start.10
  316.0 6.8 %copy-start.13 = (f32[4608,128]{1,0:T(8,128)S(1)}, f32[4608,128]{1,0:T(8,128)}, u32[]{:S(2)}) copy-start(f32[4608,128]{1,0:T(8,128)} %fusion.12) | copy-start | bytes 7077892
  316.0 6.8 %copy-start.22 = (bf16[128,128]{1,0:T(8,128)(2,1)S(1)}, bf16[128,128]{1,0:T(8,128)(2,1)}, u32[]{:S(2)}) copy-start(bf16[128,128]{1,0:T(8,128)(2,1)} %param.37) | copy-start | bytes 98308
  322.8 1.3 copy-start.8
  325.0 3.2 copy-start.6
  326.6 1.5 copy-start.24
  328.1 16.2 %copy-start.25 = (bf16[768]{0:T(1024)(128)(2,1)S(1)}, bf16[768]{0:T(1024)(128)(2,1)}, u32[]{:S(2)}) copy-start(bf16[768]{0:T(1024)(128)(2,1)} %param.41) | copy-start | bytes 4612
  344.3 179.5 %all-reduce.2.cloned.1.call-start = ((), (), s32[]{:S(2)}) async-start(), calls=%async_computation.7 | async-start | bytes 7077888 | tf_op jit(solution)/shard_map/psum | solution.py:138
  344.4 3.1 copy-start.4
  348.6 3.5 copy-start.19
  350.4 1.7 copy-start.2
  368.9 4.5 copy-start.32
  368.9 4.6 copy-start.23
  371.8 2.0 copy-start.14
  385.1 6.2 %copy-start.15 = (bf16[3,768,2,48]{1,0,3,2:T(4,128)(2,1)S(1)}, bf16[3,768,2,48]{1,0,3,2:T(4,128)(2,1)}, u32[]{:S(2)}) copy-start(bf16[3,768,2,48]{1,0,3,2:T(4,128)(2,1)} %reshape.189) | copy-start | bytes 1327108
  385.1 6.2 %copy-start.16 = (bf16[3,768,2,48]{1,0,3,2:T(4,128)(2,1)S(1)}, bf16[3,768,2,48]{1,0,3,2:T(4,128)(2,1)}, u32[]{:S(2)}) copy-start(bf16[3,768,2,48]{1,0,3,2:T(4,128)(2,1)} %reshape.190) | copy-start | bytes 1327108
  391.2 5.7 copy-start.3
  396.9 5.1 copy-start.9
  396.9 5.1 copy-start.17
  405.0 184.1 %reduce-scatter.5.cloned.1.call-start = ((), (), s32[]{:S(2)}) async-start(), calls=%async_computation.8 | async-start | bytes 3342336 | tf_op jit(solution)/shard_map/reduce_scatter | solution.py:160
  480.0 5.1 copy-start.5
  485.2 3.5 copy-start.26
  488.7 39.7 %copy-start.27 = (bf16[768,1536]{1,0:T(8,128)(2,1)S(1)}, bf16[768,1536]{1,0:T(8,128)(2,1)}, u32[]{:S(2)}) copy-start(bf16[768,1536]{1,0:T(8,128)(2,1)} %param.47) | copy-start | bytes 7077892
  536.0 56.0 %copy-start.1 = (bf16[3,768,768]{2,1,0:T(8,128)(2,1)S(1)}, bf16[3,768,768]{2,1,0:T(8,128)(2,1)}, u32[]{:S(2)}) copy-start(bf16[3,768,768]{2,1,0:T(8,128)(2,1)} %param.29) | copy-start | bytes 10616836
Sparse Core Ops, SparseCore 0:
  24.8 134.6 all-gather.2
  191.4 124.5 reduce-scatter.2
  344.4 33.6 all-gather.4
  405.1 118.6 all-reduce.1
  526.2 62.8 reduce-scatter.4
where the time goes:
time: 609 us; the launch traced here: 599 us
  waiting for transfers between devices  333 us (55%)
  matrix products  93.2 us (15%)
  blocking collectives  57.9 us (10%)
  local copies, waits for them, and re-layouts  57.2 us (9%)
  other arithmetic  42 us (7%)
  between operations  14.5 us (2%)
    all_gather x1, waiting for transfers between devices, body(): right_all = lax.all_gather(right_tile, ('grp', 'row'), axis=0, tiled=True)  127 us
    reduce_scatter x1, waiting for transfers between devices, body(): lax.psum_scatter(jnp.einsum('jkc,ikc->jic', right_all, left_tile, preferr...  121 us
    reduce_scatter x1, waiting for transfers between devices, body(): lax.psum_scatter(swapped.astype(jnp.bfloat16), ('grp', 'row'), scatter_di...  50.3 us
    all_to_all x1, blocking collectives, body(): lax.all_to_all(bias_grad.astype(jnp.bfloat16), 'col', split_axis=1, conca...  47.4 us
    psum x1, waiting for transfers between devices, body(): lax.psum(attn_part.astype(jnp.bfloat16), 'col').astype(jnp.float32)  35.1 us
    dot_general x13, matrix products, matmul(): return jnp.dot(left_side, right_side, preferred_element_type=jnp.float32)  32 us
    sub x1, matrix products, body(): probability_gradient - jnp.sum(probabilities * probability_gradient, axis...  21.6 us
    dot_general x1, matrix products, body(): jnp.einsum('jkc,ikc->jic', right_all, left_tile, preferred_element_type=j...  17.8 us
  transfers between devices with their start and end apart: 5, of which 4 were waited for; matrix products, arithmetic and copies ran while one was open for 16% of the time, Pallas kernels for 0%

commit v1 on v0

v1 whole, which is shorter than its diff:
```python
import functools
import jax
import jax.numpy as jnp
from jax import lax
from jax.experimental import pallas as pl
from jax.experimental.pallas import tpu as pltpu
from jax.sharding import Mesh, PartitionSpec as P

HD = 48
F32 = jnp.float32
BF16 = jnp.bfloat16
ROWS = ("grp", "y", "core")
COLS = ("xh", "z")
ALL = ROWS + COLS
LOG2E = 1.4426950408889634
VMEM_LIMIT = 44 * 1024 * 1024


def layer_norm(value_rows, gain_vec):
    middle = value_rows - jnp.mean(value_rows, axis=-1, keepdims=True)
    spread = jnp.mean(middle * middle, axis=-1, keepdims=True)
    return middle * lax.rsqrt(spread + 1e-05) * gain_vec.astype(F32)


def matmul(left_side, right_side):
    return jnp.dot(left_side, right_side, preferred_element_type=F32)


def dot_nt(a, b):
    return lax.dot_general(a, b, (((1,), (1,)), ((), ())), preferred_element_type=F32)


def dot_tn(a, b):
    return lax.dot_general(a, b, (((0,), (0,)), ((), ())), preferred_element_type=F32)


def lanes_of(rows):
    return lax.broadcasted_iota(jnp.int32, (rows, 128), 1)


def roll(value, shift):
    shift = shift % 128
    return value if shift == 0 else pltpu.roll(value, shift, 1)


def call(kernel, outs, args, scratch, name, flops=0, nbytes=0):
    return pl.pallas_call(
        kernel,
        out_shape=outs,
        in_specs=[pl.BlockSpec(memory_space=pltpu.VMEM)] * len(args),
        out_specs=jax.tree.map(lambda _: pl.BlockSpec(memory_space=pltpu.VMEM), outs),
        scratch_shapes=scratch,
        compiler_params=pltpu.CompilerParams(vmem_limit_bytes=VMEM_LIMIT),
        cost_estimate=pl.CostEstimate(flops=flops, bytes_accessed=nbytes, transcendentals=0),
        name=name,
    )(*args)


def project_kernel(pair_ref, gain_ref, w_ref, mask_ref, out_ref, normed_ref, scr):
    gain = gain_ref[...]

    def norm_block(block, carry):
        rows = pl.ds(pl.multiple_of(block * 512, 512), 512)
        normed_ref[rows, :] = layer_norm(pair_ref[rows, :].astype(F32), gain).astype(BF16)
        return carry

    lax.fori_loop(0, 9, norm_block, 0)
    low = lanes_of(128) < 64
    weights = w_ref[...]

    def rows_at(i, start, size):
        return normed_ref[pl.ds(pl.multiple_of(i * 96 + start, 32), size), :]

    def chunk(i, carry):
        wide = [rows_at(i, 0, 64), rows_at(i + 24, 0, 64)]
        thin = [rows_at(i, 64, 32), rows_at(i + 24, 64, 32)]
        y = dot_nt(weights, jnp.concatenate(wide + thin + thin, axis=0))
        left = y[0:128, 0:128] * jax.nn.sigmoid(y[256:384, 0:128])
        right = y[128:256, 0:128] * jax.nn.sigmoid(y[384:512, 0:128])
        both_p = jnp.where(low, y[0:128, 128:256], y[128:256, 128:256])
        both_g = jnp.where(low, y[256:384, 128:256], y[384:512, 128:256])
        scr[pl.ds(i, 128, stride=72), :] = left
        scr[pl.ds(i + 24, 128, stride=72), :] = right
        scr[pl.ds(i + 48, 128, stride=72), :] = both_p * jax.nn.sigmoid(both_g)
        return carry

    lax.fori_loop(0, 24, chunk, 0)
    mask = mask_ref[...]

    def write(c, carry):
        rows = pl.ds(pl.multiple_of(c * 576, 576), 576)
        out_ref[pl.ds(c * 8, 8)] = (scr[rows, :].reshape(8, 72, 128) * mask[None]).astype(BF16)
        return carry

    lax.fori_loop(0, 16, write, 0)


def unpack_wide(first, second, low):
    top = jnp.where(low, first, roll(second, 64))
    bottom = jnp.where(low, roll(first, 64), second)
    return top, bottom


def product_kernel(in_ref, out_ref, l_scr, r_scr):
    lane = lanes_of(384)
    low = lane < 64

    def put(dst, column, full):
        full = full.reshape(768, 128).astype(BF16)
        if dst is l_scr:
            dst[:, column : column + 128] = full
        else:
            for q in range(8):
                dst[64 * q : 64 * q + 64, column : column + 128] = full[96 * q : 96 * q + 64]
                dst[512 + 32 * q : 544 + 32 * q, column : column + 128] = full[96 * q + 64 : 96 * q + 96]

    def stack(halves):
        return jnp.concatenate([h.reshape(16, 24, 128) for h in halves], axis=1)

    def part(value, start):
        return value[:, start : start + 24].reshape(384, 128)

    for u in range(2):
        blocks = [in_ref[:, 4 * u + v].astype(F32) for v in range(4)]
        for p in range(2):
            for dst, start in ((l_scr, 0), (r_scr, 24)):
                halves = unpack_wide(part(blocks[2 * p], start), part(blocks[2 * p + 1], start), low)
                put(dst, (2 * u + p) * 128, stack(halves))
        thin = [part(b, 48) for b in blocks]
        for dst, base in ((l_scr, 0), (r_scr, 2)):
            halves = []
            for a in range(2):
                parts = [roll(thin[v], 32 * (v - base - a)) for v in range(4)]
                lower = jnp.where(lane < 32, parts[0], parts[1])
                upper = jnp.where(lane < 96, parts[2], parts[3])
                halves.append(jnp.where(low, lower, upper))
            put(dst, 512 + u * 128, stack(halves))
    for b in range(4):
        product = dot_nt(l_scr[192 * b : 192 * b + 192, :], r_scr[...])
        pack_rows(product, out_ref, 4 * b, 4)


def pack_rows(full, out_ref, first, count):
    low = lanes_of(count * 24) < 64
    lane = lanes_of(count * 16)
    for q in range(8):
        tile = full[:, 128 * (q // 2) : 128 * (q // 2) + 128].reshape(count, 48, 128)
        top = tile[:, 0:24].reshape(count * 24, 128)
        bottom = tile[:, 24:48].reshape(count * 24, 128)
        if q % 2 == 0:
            wide = jnp.where(low, top, roll(bottom, 64))
        else:
            wide = jnp.where(low, roll(top, 64), bottom)
        tile = full[:, 512 + 128 * (q // 4) : 640 + 128 * (q // 4)].reshape(count, 48, 128)
        thin = [
            roll(tile[:, 16 * m : 16 * m + 16].reshape(count * 16, 128), 32 * (m - q % 4))
            for m in range(3)
        ]
        thin = jnp.where(lane < 32, thin[0], jnp.where(lane < 64, thin[1], thin[2]))
        piece = jnp.concatenate(
            [wide.reshape(count, 24, 128), thin.reshape(count, 16, 128)], axis=1
        )
        out_ref[pl.ds(first, count), q] = piece.astype(BF16)


def update_kernel(
    t_ref, pair_ref, gate_ref, w_ref, tri_gain_ref, bias_gain_ref, bp_ref, out_ref, bias_ref, scr, b_scr
):
    def spread(c, carry):
        rows = pl.ds(pl.multiple_of(c * 640, 640), 640)
        scr[rows, :] = t_ref[pl.ds(c * 16, 16)].astype(F32).reshape(640, 128)
        return carry

    lax.fori_loop(0, 8, spread, 0)
    weight = w_ref[...]
    tri_gain = tri_gain_ref[...]
    bias_gain = bias_gain_ref[...]
    bias_proj = bp_ref[...]

    def step(position, places):
        tri = scr[pl.ds(position, 128, stride=40), :]
        middle = tri - jnp.mean(tri, axis=0, keepdims=True)
        spread_of = jnp.mean(middle * middle, axis=0, keepdims=True)
        tri_normed = (middle * lax.rsqrt(spread_of + 1e-05) * tri_gain).astype(BF16)
        update = dot_tn(tri_normed, weight)
        fed = []
        at = 0
        for start, size in places:
            rows = pl.ds(pl.multiple_of(start, 32), size)
            new = pair_ref[rows, :].astype(F32) + gate_ref[rows, :] * update[at : at + size]
            out_ref[rows, :] = new
            fed.append(layer_norm(new, bias_gain).astype(BF16))
            at += size
        if at < 128:
            fed.append(fed[-1])
        b_scr[pl.ds(position, 16, stride=40), :] = dot_nt(bias_proj, jnp.concatenate(fed, axis=0))

    def wide(i, carry):
        step(i, [(96 * i, 64), (96 * (i + 24), 64)])
        return carry

    def thin(i, carry):
        step(i + 24, [(96 * (i + 16 * m) + 64, 32) for m in range(3)])
        return carry

    lax.fori_loop(0, 24, wide, 0)
    lax.fori_loop(0, 16, thin, 0)
    bias = b_scr[...].reshape(16, 40, 128).astype(BF16)
    for copy in range(8):
        bias_ref[copy] = bias


def attention_kernel(
    bias_ref, q_ref, k_ref, v_ref, g_ref, chain_row_ref, chain_col_ref, weight_ref,
    mixed_ref, grad_ref, bias_scr, acc,
):
    low = lanes_of(384) < 64
    lane = lanes_of(256)
    head_weight = weight_ref[...] * LOG2E

    def put(column, full):
        same = chain_row_ref[...] == chain_col_ref[:, column : column + 128]
        bias_scr[:, column : column + 128] = full.reshape(768, 128) * LOG2E + jnp.where(
            same, head_weight, 0.0
        )

    for u in range(2):
        blocks = [bias_ref[:, 4 * u + v].astype(F32) for v in range(4)]
        for p in range(2):
            halves = unpack_wide(
                blocks[2 * p][:, 0:24].reshape(384, 128),
                blocks[2 * p + 1][:, 0:24].reshape(384, 128),
                low,
            )
            put((2 * u + p) * 128, jnp.concatenate([h.reshape(16, 24, 128) for h in halves], axis=1))
        thin = [b[:, 24:40].reshape(256, 128) for b in blocks]
        thirds = []
        for m in range(3):
            parts = [roll(thin[v], 32 * (v - m)) for v in range(4)]
            lower = jnp.where(lane < 32, parts[0], parts[1])
            upper = jnp.where(lane < 96, parts[2], parts[3])
            thirds.append(jnp.where(lane < 64, lower, upper).reshape(16, 16, 128))
        put(512 + u * 128, jnp.concatenate(thirds, axis=1))

    scale = HD ** (-0.5) * LOG2E
    block = acc.shape[0]

    def row_block(b, carry):
        rows = pl.ds(pl.multiple_of(b * block, block), block)

        def sample(s, inner):
            values = v_ref[s]
            grads = g_ref[s, rows, :]
            weights = jnp.exp2(dot_nt(q_ref[s, rows, :], k_ref[s]) * scale + bias_scr[rows, :])
            probs = weights * (1.0 / jnp.sum(weights, axis=-1, keepdims=True))
            mixed = matmul(probs.astype(BF16), values)
            mixed_ref[s, rows, :] = mixed.astype(BF16)
            center = jnp.sum(grads.astype(F32) * mixed, axis=-1, keepdims=True)
            score_grad = probs * (dot_nt(grads, values) - center)
            acc[...] = jnp.where(s == 0, score_grad, acc[...] + score_grad)
            return inner

        lax.fori_loop(0, 6, sample, 0)
        pack_rows(acc[...], grad_ref, b * (block // 48), block // 48)
        return carry

    lax.fori_loop(0, 768 // block, row_block, 0)


def pair_grad_kernel(in_ref, w_ref, out_ref, scr):
    total = in_ref[0].astype(F32)
    for part in range(1, 8):
        total = total + in_ref[part].astype(F32)
    scr[...] = total.reshape(640, 128)
    weight = w_ref[...]

    def step(position, places):
        grad = scr[pl.ds(position, 16, stride=40), :]
        high = grad.astype(BF16)
        rest = grad - high.astype(F32)
        middle = rest.astype(BF16)
        least = (rest - middle.astype(F32)).astype(BF16)
        rows = dot_tn(jnp.concatenate([high, middle, least], axis=0), weight)
        at = 0
        for start, size in places:
            out_ref[pl.ds(pl.multiple_of(start, 32), size), :] = rows[at : at + size]
            at += size

    def wide(i, carry):
        step(i, [(96 * i, 64), (96 * (i + 24), 64)])
        return carry

    def thin(i, carry):
        step(i + 24, [(96 * (i + 16 * m) + 64, 32) for m in range(3)])
        return carry

    lax.fori_loop(0, 24, wide, 0)
    lax.fori_loop(0, 16, thin, 0)


def column_order(value, axis):
    shape = value.shape
    split = value.reshape(shape[:axis] + (8, 96) + shape[axis + 1 :])
    wide = lax.slice_in_dim(split, 0, 64, axis=axis + 1).reshape(shape[:axis] + (512,) + shape[axis + 1 :])
    thin = lax.slice_in_dim(split, 64, 96, axis=axis + 1).reshape(shape[:axis] + (256,) + shape[axis + 1 :])
    return jnp.concatenate([wide, thin], axis=axis)


def exchange(value, axes):
    return lax.all_to_all(value, axes, 0, 0, tiled=True)


def body(
    pair_state,
    pair_mask,
    chain_ids,
    tokens,
    grad_attn,
    norm_pair,
    proj_left,
    gate_left,
    proj_right,
    gate_right,
    gate_out,
    norm_tri,
    tri_out,
    norm_bias,
    bias_proj,
    chain_weight,
    norm_tokens,
    w_query,
    w_key,
    w_value,
    w_out,
    norm_ff,
    ff_gate,
    ff_up,
    ff_down,
):
    tile_rows, tile_cols, channels = pair_state.shape
    tile_size = tile_rows * tile_cols
    row_start = lax.axis_index(ROWS) * tile_rows
    col_index = lax.axis_index(COLS)
    col_start = col_index * tile_cols
    pair_flat = pair_state.reshape(tile_size, channels)

    mask_float = pair_mask.astype(F32)
    row_mask = lax.dynamic_slice_in_dim(mask_float, row_start, tile_rows)
    col_mask = lax.dynamic_slice_in_dim(mask_float, col_start, tile_cols)
    tile_mask = row_mask[:, None] * col_mask[None, :]
    wide_mask = jnp.concatenate([tile_mask[:24, :64], tile_mask[24:, :64]], axis=1)
    thin_mask = jnp.concatenate([tile_mask[:24, 64:], tile_mask[24:, 64:]], axis=1)
    packed_mask = jnp.concatenate(
        [wide_mask, wide_mask, jnp.concatenate([thin_mask, thin_mask], axis=1)], axis=0
    )
    pair_weights = jnp.concatenate([proj_left, proj_right, gate_left, gate_right], axis=1).T
    sides, normed = call(
        project_kernel,
        (jax.ShapeDtypeStruct((128, 72, 128), BF16), jax.ShapeDtypeStruct((tile_size, 128), BF16)),
        (pair_flat, norm_pair.astype(F32)[None], pair_weights, packed_mask),
        [pltpu.VMEM((128 * 72, 128), F32)],
        "project",
        flops=2 * 512 * 128 * 6144,
        nbytes=5_000_000,
    )
    sides_in = exchange(sides, ALL).reshape(16, 8, 72, 128)
    products = call(
        product_kernel,
        jax.ShapeDtypeStruct((16, 8, 40, 128), BF16),
        (sides_in,),
        [pltpu.VMEM((768, 768), BF16), pltpu.VMEM((768, 768), BF16)],
        "product",
        flops=2 * 768**3,
        nbytes=4_000_000,
    )
    tri_in = exchange(products.reshape(128, 40, 128), ALL)

    samples, seq_len, model_width = tokens.shape
    token_flat = tokens.reshape(samples * seq_len, model_width)
    token_norm = layer_norm(token_flat.astype(F32), norm_tokens).astype(BF16)

    def heads_of(rows, weight):
        value = matmul(rows, weight).astype(BF16).reshape(samples, seq_len, 2, HD)
        return jnp.transpose(value, (2, 0, 1, 3))

    query = heads_of(token_norm, w_query)
    key = column_order(heads_of(token_norm, w_key), 2)
    value = column_order(heads_of(token_norm, w_value), 2)
    head_grad = heads_of(grad_attn.reshape(samples * seq_len, model_width), w_out.T)
    swapped = exchange(jnp.concatenate([query, key, value, head_grad], axis=3), "core")
    swapped = swapped.reshape(2 * samples, seq_len, 4 * HD)
    query, key, value, head_grad = [swapped[:, :, HD * n : HD * n + HD] for n in range(4)]
    w_out_all = lax.all_gather(w_out, COLS, axis=0, tiled=True)

    gate = jax.nn.sigmoid(matmul(normed, gate_out))
    heads_first = jnp.transpose(bias_proj.T.reshape(8, 2, 128), (1, 0, 2)).reshape(16, 128)
    pair_out, bias = call(
        update_kernel,
        (jax.ShapeDtypeStruct((tile_size, 128), F32), jax.ShapeDtypeStruct((8, 16, 40, 128), BF16)),
        (
            tri_in,
            pair_flat,
            gate,
            tri_out,
            jnp.broadcast_to(norm_tri.astype(F32)[:, None], (128, 128)),
            norm_bias.astype(F32)[None],
            heads_first,
        ),
        [pltpu.VMEM((128 * 40, 128), F32), pltpu.VMEM((16 * 40, 128), F32)],
        "update",
        flops=2 * 128 * 128 * 5120,
        nbytes=9_000_000,
    )
    bias_in = exchange(bias.reshape(128, 40, 128), ALL).reshape(16, 8, 40, 128)

    head_index = 2 * col_index + lax.axis_index("core")
    head_weight = lax.dynamic_slice_in_dim(chain_weight, head_index, 1)[None]
    mixed, bias_grad = call(
        attention_kernel,
        (
            jax.ShapeDtypeStruct((2 * samples, seq_len, HD), BF16),
            jax.ShapeDtypeStruct((16, 8, 40, 128), BF16),
        ),
        (
            bias_in,
            query,
            key,
            value,
            head_grad,
            chain_ids[:, None],
            column_order(chain_ids[None], 1),
            head_weight,
        ),
        [pltpu.VMEM((768, 768), F32), pltpu.VMEM((192, 768), F32)],
        "attention",
        flops=6 * 6 * 768 * 768 * 128,
        nbytes=12_000_000,
    )

    share_len = seq_len // 8
    mixed_out = jnp.transpose(mixed.reshape(2, samples, 8, share_len, HD), (0, 2, 1, 3, 4))
    mixed_in = exchange(mixed_out.reshape(16, samples, share_len, HD), ("core",) + COLS)
    mixed_rows = jnp.transpose(mixed_in.reshape(2, 8, samples, share_len, HD), (2, 3, 1, 0, 4))
    attn = matmul(mixed_rows.reshape(samples * share_len, model_width), w_out_all)
    token_share = lax.dynamic_slice_in_dim(tokens, col_index * share_len, share_len, 1)
    state = token_share.reshape(samples * share_len, model_width).astype(F32) + attn
    ff_in = layer_norm(state, norm_ff).astype(BF16)
    hidden = (jax.nn.silu(matmul(ff_in, ff_gate)) * matmul(ff_in, ff_up)).astype(BF16)
    refined = (state + matmul(hidden, ff_down)).reshape(samples, share_len, model_width)

    grad_in = exchange(bias_grad.reshape(128, 40, 128), ALL).reshape(8, 16, 40, 128)
    pair_grad = call(
        pair_grad_kernel,
        jax.ShapeDtypeStruct((tile_size, 128), F32),
        (grad_in, jnp.concatenate([heads_first] * 3, axis=0)),
        [pltpu.VMEM((16 * 40, 128), F32)],
        "pair_grad",
        flops=2 * 48 * 128 * 5120,
        nbytes=4_000_000,
    )
    return (pair_out.reshape(pair_state.shape), refined, pair_grad.reshape(pair_state.shape))


def solution(mesh):
    fine = Mesh(mesh.devices.reshape(2, 4, 2, 2, 4), ALL)
    pair = P(ROWS, COLS, None)
    sample_rows = P(ROWS, None, None)
    return jax.shard_map(
        body,
        mesh=fine,
        in_specs=(pair, P(), P(), sample_rows, sample_rows)
        + (P(),) * 12
        + (P(None, COLS),) * 3
        + (P(COLS, None),)
        + (P(),) * 4,
        out_specs=(pair, pair, pair),
        check_vma=False,
    )
```

time: 609 us -> 265 us (0.44); the launches traced: 599 us -> 264 us
  waiting for transfers between devices: 333 us -> 44.9 us
  matrix products: 93.2 us -> 23.8 us
  Pallas kernels: 0 us -> 68.1 us
  blocking collectives: 57.9 us -> 0 us
  starting transfers between devices: 0.5 us -> 42.5 us
  other arithmetic: 42 us -> 13.8 us
    reduce_scatter x2 -> x0, waiting for transfers between devices: 171 us -> none  [the longest x1 121 us: body(): lax.psum_scatter(jnp.einsum('jkc,ikc->jic', right_all, left_tile, preferr...]
    all_gather x2 -> x1, waiting for transfers between devices: 127 us -> 0.02 us  [body(): w_out_all = lax.all_gather(w_out, COLS, axis=0, tiled=True)]
    pallas_call x0 -> x5, Pallas kernels: none -> 68.1 us  [call(): pl.pallas_call(kernel, out_shape=outs, in_specs=[pl.BlockSpec(memory_spac...]
    all_to_all x2 -> x0, blocking collectives: 57.9 us -> none  [the longest x1 47.4 us: body(): lax.all_to_all(bias_grad.astype(jnp.bfloat16), 'col', split_axis=1, conca...]
    dot_general x19 -> x8, matrix products: 71.6 us -> 23.8 us  [matmul(): return jnp.dot(left_side, right_side, preferred_element_type=F32)]
    all_to_all x0 -> x6, waiting for transfers between devices: none -> 44.2 us  [exchange(): return lax.all_to_all(value, axes, 0, 0, tiled=True)]
    all_to_all x0 -> x6, starting transfers between devices: none -> 42.4 us  [exchange(): return lax.all_to_all(value, axes, 0, 0, tiled=True)]
    psum x1 -> x0, waiting for transfers between devices: 35.1 us -> none  [body(): lax.psum(attn_part.astype(jnp.bfloat16), 'col').astype(jnp.float32)]
  transfers between devices with their start and end apart: 5 -> 7, of which waited for: 4 -> 4; matrix products, arithmetic and copies ran while one was open for 16% -> 26% of each run, Pallas kernels for 0% -> 19%
where the time goes in v1:
time: 265 us; the launch traced here: 264 us
  Pallas kernels  68.1 us (26%)
  local copies, waits for them, and re-layouts  55.9 us (21%)
  waiting for transfers between devices  44.9 us (17%)
  starting transfers between devices  42.5 us (16%)
  matrix products  23.8 us (9%)
  between operations  14.6 us (6%)
  other arithmetic  13.8 us (5%)
    pallas_call x5, Pallas kernels, call(): pl.pallas_call(kernel, out_shape=outs, in_specs=[pl.BlockSpec(memory_spac...  68.1 us
    all_to_all x6, waiting for transfers between devices, exchange(): return lax.all_to_all(value, axes, 0, 0, tiled=True)  44.2 us
    all_to_all x6, starting transfers between devices, exchange(): return lax.all_to_all(value, axes, 0, 0, tiled=True)  42.4 us
    dot_general x8, matrix products, matmul(): return jnp.dot(left_side, right_side, preferred_element_type=F32)  23.8 us
    unnamed x86, local copies, waits for them, and re-layouts  20.1 us
    slice x1, local copies, waits for them, and re-layouts, body(): swapped[:, :, HD * n:HD * n + HD]  6.24 us
  transfers between devices with their start and end apart: 7, of which 4 were waited for; matrix products, arithmetic and copies ran while one was open for 26% of the time, Pallas kernels for 19%

profile of v1, /device:TPU:1, one launch (start us, length us, event | category | flops | bytes accessed | tf_op | source)
XLA Modules:
  0.0 263.5 jit_solution(11799843305383357283)
XLA Ops:
  7.2 0.8 convert_element_type.51
  8.3 0.7 fusion.21
  9.5 0.7 bitcast_convert_fusion.1.gain_ref
  10.2 1.5 copy.72
  11.7 1.5 copy.71
  13.2 1.5 copy.70
  14.6 1.5 copy.69
  16.1 0.8 maximum_bitcast_fusion.w_ref
  16.9 0.9 maximum_maximum_fusion.mask_ref
  17.8 1.3 copy-done.9
  19.1 8.2 %project.1 = (bf16[128,72,128]{2,1,0:T(8,128)(2,1)S(1)}, bf16[4608,128]{1,0:T(8,128)(2,1)S(1)}) custom-call(bf16[4608,128]{1,0:T(8,128)(2,1)S(1)} %bitcast.106, f32[1,128]{1,0:T(1,128)S(1)} %bitcast_convert_fusion.1.gain_ref, bf16[512,128]{1,0:T(8,128)(2,1)S(1)} %maximum_bitcast_fusion.w_ref, f32[72,128]{1,0:T(8,128)S(1)} %maximum_maximum_fusion.mask_ref), custom_call_target="tpu_custom_call" | custom-call | flops 805306368 | bytes 5000000 | tf_op jit(solution)/shard_map/project/pallas_call | solution.py:47
  27.3 1.4 copy-done.2
  28.7 1.1 copy-done.12
  29.9 11.9 %all-to-all-start = ((bf16[128,72,128]{2,1,0:T(8,128)(2,1)}), bf16[128,72,128]{2,1,0:T(8,128)(2,1)}, u32[]{:S(2)}, u32[]{:S(2)}) async-start(bf16[128,72,128]{2,1,0:T(8,128)(2,1)} %copy-done.2), calls=%async_computation | async-start | bytes 4718592 | tf_op jit(solution)/shard_map/all_to_all | solution.py:310
  41.8 0.7 all-gather.2.cloned.1.call-update
  42.5 2.5 convert_reduce_fusion
  45.7 3.2 %multiply_reduce_fusion = f32[3,768]{1,0:T(4,128)S(1)} fusion(bf16[3,768,768]{2,1,0:T(8,128)(2,1)} %param.28, f32[3,768]{1,0:T(4,128)S(1)} %broadcast_multiply_fusion.1), kind=kLoop, calls=%fused_computation.4 | loop fusion | flops 7075584 | bytes 3557376 | tf_op jit(solution)/shard_map/reduce_sum | solution.py:21
  49.5 3.0 %convolution_convert_fusion = bf16[2304,96]{0,1:T(8,128)(2,1)} fusion(bf16[2304,768]{1,0:T(8,128)(2,1)S(1)} %bitcast.103, bf16[96,768]{1,0:T(8,128)(2,1)} %param.45), kind=kOutput, calls=%fused_computation.10 | convolution fusion | flops 339959808 | bytes 4128768 | tf_op jit(solution)/shard_map/dot_general | solution.py:26
  52.5 1.5 fusion.2
  54.1 2.0 convolution_convert_fusion.1
  56.1 2.0 convolution_convert_fusion.2
  58.1 16.2 %all-to-all-done = bf16[128,72,128]{2,1,0:T(8,128)(2,1)} async-done(((bf16[128,72,128]{2,1,0:T(8,128)(2,1)}), bf16[128,72,128]{2,1,0:T(8,128)(2,1)}, u32[]{:S(2)}, u32[]{:S(2)}) %all-to-all-start) | async-done | bytes 2359328 | tf_op jit(solution)/shard_map/all_to_all | solution.py:310
  74.2 5.7 %product.1 = bf16[16,8,40,128]{3,2,1,0:T(8,128)(2,1)} custom-call(bf16[16,8,72,128]{3,2,1,0:T(8,128)(2,1)} %bitcast.3.in_ref), custom_call_target="tpu_custom_call" | custom-call | flops 905969664 | bytes 4000000 | tf_op jit(solution)/shard_map/product/pallas_call | solution.py:47
  79.9 5.9 %all-to-all-start.1 = ((bf16[128,40,128]{2,1,0:T(8,128)(2,1)}), bf16[128,40,128]{2,1,0:T(8,128)(2,1)S(1)}, u32[]{:S(2)}, u32[]{:S(2)}) async-start(bf16[128,40,128]{2,1,0:T(8,128)(2,1)} %bitcast.4), calls=%async_computation.1 | async-start | bytes 2621440 | tf_op jit(solution)/shard_map/all_to_all | solution.py:310
  85.9 3.3 %convolution_convert_fusion.3 = bf16[2304,96]{0,1:T(8,128)(2,1)S(1)} fusion(bf16[2304,768]{1,0:T(8,128)(2,1)} %copy-done.14, bf16[768,96]{0,1:T(8,128)(2,1)S(1)} %copy-done.28), kind=kOutput, calls=%fused_computation.13 | convolution fusion | flops 339959808 | bytes 4128768 | tf_op jit(solution)/shard_map/dot_general | solution.py:26
  89.2 1.0 reshape.169
  90.4 0.8 copy.77
  91.2 1.7 reshape.165
  93.5 0.8 copy.79
  94.6 1.0 copy.78
  96.6 1.0 slice.61
  97.6 2.2 reshape.163
  99.8 1.7 copy.76
  101.5 1.1 reshape.162
  102.5 2.0 copy.75
  104.5 1.0 reshape.159
  105.5 3.1 %fusion.5.gate_ref = f32[4608,128]{1,0:T(8,128)} fusion(bf16[4608,128]{1,0:T(8,128)(2,1)S(1)} %copy-done.13, bf16[128,128]{1,0:T(8,128)(2,1)} %param.35), kind=kOutput, calls=%fused_computation.8 | convolution fusion | flops 152764416 | bytes 3571712 | tf_op jit(solution)/shard_map/dot_general | solution.py:26
  108.7 3.0 %pad_maximum_fusion = bf16[2,3,768,192]{2,1,3,0:T(4,128)(2,1)S(1)} fusion(bf16[2,3,768,48]{2,1,3,0:T(4,128)(2,1)S(1)} %bitcast.114, bf16[2,3,256,48]{2,1,3,0:T(4,128)(2,1)S(1)} %copy-done.24, bf16[2,3,512,48]{2,1,3,0:T(4,128)(2,1)S(1)} %copy-done.22, bf16[2,3,256,48]{2,1,3,0:T(4,128)(2,1)S(1)} %copy-done.25, bf16[2,3,512,48]{2,1,3,0:T(4,128)(2,1)S(1)} %copy-done.23, ...), kind=kLoop, calls=%fused_computation.16 | loop fusion | flops 10616832 | bytes 3538944 | tf_op jit(solution)/shard_map/concatenate | solution.py:390
  111.7 1.5 copy.80
  113.2 6.1 %all-to-all-start.3 = ((bf16[2,3,768,192]{2,3,1,0:T(8,128)(2,1)}), bf16[2,3,768,192]{2,3,1,0:T(8,128)(2,1)}, u32[]{:S(2)}, u32[]{:S(2)}) async-start(bf16[2,3,768,192]{2,3,1,0:T(8,128)(2,1)} %copy.80), calls=%async_computation.3 | async-start | bytes 3538944 | tf_op jit(solution)/shard_map/all_to_all | solution.py:310
  119.3 1.7 copy-done.3
  121.0 1.3 copy-done.10
  122.3 23.7 %update.1 = (f32[4608,128]{1,0:T(8,128)}, bf16[8,16,40,128]{3,2,1,0:T(8,128)(2,1)}) custom-call(bf16[128,40,128]{2,1,0:T(8,128)(2,1)S(1)} %all-to-all-done.1.t_ref, bf16[4608,128]{1,0:T(8,128)(2,1)S(1)} %bitcast.107, f32[4608,128]{1,0:T(8,128)S(1)} %copy-done.3, bf16[128,128]{1,0:T(8,128)(2,1)S(1)} %copy-done.11, ...), custom_call_target="tpu_custom_call" | custom-call | flops 167772160 | bytes 9000000 | tf_op jit(solution)/shard_map/update/pallas_call | solution.py:47
  146.0 8.7 %all-to-all-start.2 = ((bf16[128,40,128]{2,1,0:T(8,128)(2,1)}), bf16[128,40,128]{2,1,0:T(8,128)(2,1)S(1)}, u32[]{:S(2)}, u32[]{:S(2)}) async-start(bf16[128,40,128]{2,1,0:T(8,128)(2,1)} %bitcast.12), calls=%async_computation.2 | async-start | bytes 2621440 | tf_op jit(solution)/shard_map/all_to_all | solution.py:310
  155.7 4.0 %copy.81 = bf16[2,3,768,192]{3,2,1,0:T(8,128)(2,1)} copy(bf16[2,3,768,192]{2,3,1,0:T(8,128)(2,1)} %all-to-all-done.3) | data formatting | bytes 3538944 | tf_op jit(solution)/shard_map/all_to_all | solution.py:310
  159.7 6.2 %fusion.19 = (bf16[6,768,48]{2,1,0:T(8,128)(2,1)}, bf16[6,768,48]{2,1,0:T(8,128)(2,1)}, bf16[6,768,48]{2,1,0:T(8,128)(2,1)}, bf16[6,768,48]{2,1,0:T(8,128)(2,1)}) fusion(bf16[6,768,192]{2,1,0:T(8,128)(2,1)} %bitcast.110), kind=kLoop, calls=%fused_computation.44 | loop fusion | bytes 3538944 | tf_op jit(solution)/shard_map/slice | solution.py:392
  166.0 9.1 %all-to-all-done.2 = bf16[128,40,128]{2,1,0:T(8,128)(2,1)S(1)} async-done(((bf16[128,40,128]{2,1,0:T(8,128)(2,1)}), bf16[128,40,128]{2,1,0:T(8,128)(2,1)S(1)}, u32[]{:S(2)}, u32[]{:S(2)}) %all-to-all-start.2) | async-done | bytes 1310752 | tf_op jit(solution)/shard_map/all_to_all | solution.py:310
  175.1 1.3 copy-done.4
  176.3 1.3 copy-done.5
  177.6 1.3 copy-done.6
  178.9 1.3 copy-done.7
  180.1 20.0 %attention.1 = (bf16[6,768,48]{2,1,0:T(8,128)(2,1)S(1)}, bf16[16,8,40,128]{3,2,1,0:T(8,128)(2,1)}) custom-call(bf16[16,8,40,128]{3,2,1,0:T(8,128)(2,1)S(1)} %bitcast.104, bf16[6,768,48]{2,1,0:T(8,128)(2,1)S(1)} %copy-done.7, bf16[6,768,48]{2,1,0:T(8,128)(2,1)S(1)} %copy-done.6, bf16[6,768,48]{2,1,0:T(8,128)(2,1)S(1)} %copy-done.5, ...), custom_call_target="tpu_custom_call" | custom-call | flops 2717908992 | bytes 12000000 | tf_op jit(solution)/shard_map/attention/pallas_call | solution.py:47
  200.1 1.0 copy-done.8
  201.1 2.2 copy.83
  203.3 5.1 %all-to-all-start.4 = ((bf16[16,3,96,48]{2,3,1,0:T(8,128)(2,1)}), bf16[16,3,96,48]{2,3,1,0:T(8,128)(2,1)S(1)}, u32[]{:S(2)}, u32[]{:S(2)}) async-start(bf16[16,3,96,48]{2,3,1,0:T(8,128)(2,1)} %bitcast.24), calls=%async_computation.4 | async-start | bytes 1179648 | tf_op jit(solution)/shard_map/all_to_all | solution.py:310
  208.5 1.1 constant_dynamic-slice_fusion
  209.5 11.7 %all-to-all-done.4 = bf16[16,3,96,48]{2,3,1,0:T(8,128)(2,1)S(1)} async-done(((bf16[16,3,96,48]{2,3,1,0:T(8,128)(2,1)}), bf16[16,3,96,48]{2,3,1,0:T(8,128)(2,1)S(1)}, u32[]{:S(2)}, u32[]{:S(2)}) %all-to-all-start.4) | async-done | bytes 442400 | tf_op jit(solution)/shard_map/all_to_all | solution.py:310
  221.2 4.8 %all-to-all-start.5 = ((bf16[128,40,128]{2,1,0:T(8,128)(2,1)}), bf16[128,40,128]{2,1,0:T(8,128)(2,1)}, u32[]{:S(2)}, u32[]{:S(2)}) async-start(bf16[128,40,128]{2,1,0:T(8,128)(2,1)} %bitcast.28), calls=%async_computation.5 | async-start | bytes 2621440 | tf_op jit(solution)/shard_map/all_to_all | solution.py:310
  227.0 2.1 fusion.22
  229.3 0.7 copy-done.16
  230.6 2.1 fusion.8
  232.7 6.2 %convolution_add_fusion.1 = f32[288,768]{1,0:T(8,128)} fusion(f32[288,768]{1,0:T(8,128)} %copy-done.16, bf16[1536,768]{1,0:T(8,128)(2,1)} %param.49, bf16[768,1536]{1,0:T(8,128)(2,1)} %param.48, f32[288,1536]{1,0:T(8,128)} %fusion.8, f32[768]{0:T(1024)} %copy-done.32, f32[288]{0:T(512)} %copy-done.36, f32[288]{0:T(512)S(1)} %broadcast_multiply_fusion.2), kind=kOutput, calls=%fused_computation.18 | convolution fusion | flops 1362714624 | bytes 8262912 | tf_op jit(solution)/shard_map/dot_general | solution.py:26
  238.9 7.2 %all-to-all-done.5 = bf16[128,40,128]{2,1,0:T(8,128)(2,1)} async-done(((bf16[128,40,128]{2,1,0:T(8,128)(2,1)}), bf16[128,40,128]{2,1,0:T(8,128)(2,1)}, u32[]{:S(2)}, u32[]{:S(2)}) %all-to-all-start.5) | async-done | bytes 1310752 | tf_op jit(solution)/shard_map/all_to_all | solution.py:310
  246.1 10.6 %pair_grad.1 = f32[4608,128]{1,0:T(8,128)} custom-call(bf16[8,16,40,128]{3,2,1,0:T(8,128)(2,1)} %bitcast.29.in_ref, bf16[48,128]{1,0:T(8,128)(2,1)S(1)} %pad_maximum_fusion.1.w_ref), custom_call_target="tpu_custom_call" | custom-call | flops 62914560 | bytes 4000000 | tf_op jit(solution)/shard_map/pair_grad/pallas_call | solution.py:47
  (108 shorter events, 7.2 us)
Async XLA Ops:
  7.2 42.3 %copy-start = (bf16[3,768,768]{2,1,0:T(8,128)(2,1)S(1)}, bf16[3,768,768]{2,1,0:T(8,128)(2,1)}, u32[]{:S(2)}) copy-start(bf16[3,768,768]{2,1,0:T(8,128)(2,1)} %param.29) | copy-start | bytes 10616836
  17.8 1.3 copy-start.9
  27.3 1.4 copy-start.2
  28.7 1.1 copy-start.12
  29.8 12.6 %copy-start.34 = (bf16[768]{0:T(1024)(128)(2,1)S(1)}, bf16[768]{0:T(1024)(128)(2,1)}, u32[]{:S(2)}) copy-start(bf16[768]{0:T(1024)(128)(2,1)} %param.41) | copy-start | bytes 4612
  29.9 44.4 %all-to-all-start = ((bf16[128,72,128]{2,1,0:T(8,128)(2,1)}), bf16[128,72,128]{2,1,0:T(8,128)(2,1)}, u32[]{:S(2)}, u32[]{:S(2)}) async-start(bf16[128,72,128]{2,1,0:T(8,128)(2,1)} %copy-done.2), calls=%async_computation | async-start | bytes 4718592 | tf_op jit(solution)/shard_map/all_to_all | solution.py:310
  41.8 185.2 %all-gather.2.cloned.1.call-start = ((), (), s32[]{:S(2)}) async-start(), calls=%async_computation.6 | async-start | bytes 1327104 | tf_op jit(solution)/shard_map/all_gather | solution.py:393
  49.5 3.0 %copy-start.15 = (bf16[3,768,768]{2,1,0:T(8,128)(2,1)S(1)}, bf16[3,768,768]{2,1,0:T(8,128)(2,1)}, u32[]{:S(2)}) copy-start(bf16[3,768,768]{2,1,0:T(8,128)(2,1)} %param.28) | copy-start | bytes 10616836
  49.5 3.0 %copy-start.29 = (f32[2304]{0:T(1024)S(1)}, f32[2304]{0:T(1024)}, u32[]{:S(2)}) copy-start(f32[2304]{0:T(1024)} %div.23) | copy-start | bytes 27652
  49.5 3.0 %copy-start.30 = (f32[2304]{0:T(1024)S(1)}, f32[2304]{0:T(1024)}, u32[]{:S(2)}) copy-start(f32[2304]{0:T(1024)} %rsqrt.20) | copy-start | bytes 27652
  52.5 1.5 copy-start.26
  54.1 2.0 copy-start.14
  54.1 2.0 copy-start.27
  74.2 11.6 %copy-start.28 = (bf16[768,96]{0,1:T(8,128)(2,1)S(1)}, bf16[768,96]{0,1:T(8,128)(2,1)}, u32[]{:S(2)}) copy-start(bf16[768,96]{0,1:T(8,128)(2,1)} %param.42) | copy-start | bytes 442372
  79.9 33.3 %all-to-all-start.1 = ((bf16[128,40,128]{2,1,0:T(8,128)(2,1)}), bf16[128,40,128]{2,1,0:T(8,128)(2,1)S(1)}, u32[]{:S(2)}, u32[]{:S(2)}) async-start(bf16[128,40,128]{2,1,0:T(8,128)(2,1)} %bitcast.4), calls=%async_computation.1 | async-start | bytes 2621440 | tf_op jit(solution)/shard_map/all_to_all | solution.py:310
  85.9 3.3 %copy-start.18 = (bf16[2304,96]{0,1:T(8,128)(2,1)S(1)}, bf16[2304,96]{0,1:T(8,128)(2,1)}, u32[]{:S(2)}) copy-start(bf16[2304,96]{0,1:T(8,128)(2,1)} %convolution_convert_fusion) | copy-start | bytes 1327108
  85.9 4.3 %copy-start.19 = (bf16[2304,96]{0,1:T(8,128)(2,1)S(1)}, bf16[2304,96]{0,1:T(8,128)(2,1)}, u32[]{:S(2)}) copy-start(bf16[2304,96]{0,1:T(8,128)(2,1)} %convolution_convert_fusion.1) | copy-start | bytes 1327108
  91.2 4.5 %copy-start.17 = (bf16[2304,96]{0,1:T(8,128)(2,1)S(1)}, bf16[2304,96]{0,1:T(8,128)(2,1)}, u32[]{:S(2)}) copy-start(bf16[2304,96]{0,1:T(8,128)(2,1)} %convolution_convert_fusion.2) | copy-start | bytes 1327108
  96.6 8.9 %copy-start.13 = (bf16[4608,128]{1,0:T(8,128)(2,1)S(1)}, bf16[4608,128]{1,0:T(8,128)(2,1)}, u32[]{:S(2)}) copy-start(bf16[4608,128]{1,0:T(8,128)(2,1)} %copy-done.12) | copy-start | bytes 3538948
  105.5 3.1 %copy-start.20 = (bf16[3,768,2,48]{1,0,3,2:T(4,128)(2,1)S(1)}, bf16[3,768,2,48]{1,0,3,2:T(4,128)(2,1)}, u32[]{:S(2)}) copy-start(bf16[3,768,2,48]{1,0,3,2:T(4,128)(2,1)} %reshape.169) | copy-start | bytes 1327108
  105.5 3.1 %copy-start.21 = (bf16[3,768,2,48]{1,0,3,2:T(4,128)(2,1)S(1)}, bf16[3,768,2,48]{1,0,3,2:T(4,128)(2,1)}, u32[]{:S(2)}) copy-start(bf16[3,768,2,48]{1,0,3,2:T(4,128)(2,1)} %reshape.159) | copy-start | bytes 1327108
  105.5 3.1 %copy-start.22 = (bf16[2,3,512,48]{2,1,3,0:T(4,128)(2,1)S(1)}, bf16[2,3,512,48]{2,1,3,0:T(4,128)(2,1)}, u32[]{:S(2)}) copy-start(bf16[2,3,512,48]{2,1,3,0:T(4,128)(2,1)} %copy.78) | copy-start | bytes 884740
  105.5 3.1 %copy-start.23 = (bf16[2,3,512,48]{2,1,3,0:T(4,128)(2,1)S(1)}, bf16[2,3,512,48]{2,1,3,0:T(4,128)(2,1)}, u32[]{:S(2)}) copy-start(bf16[2,3,512,48]{2,1,3,0:T(4,128)(2,1)} %copy.75) | copy-start | bytes 884740
  105.5 3.1 %copy-start.24 = (bf16[2,3,256,48]{2,1,3,0:T(4,128)(2,1)S(1)}, bf16[2,3,256,48]{2,1,3,0:T(4,128)(2,1)}, u32[]{:S(2)}) copy-start(bf16[2,3,256,48]{2,1,3,0:T(4,128)(2,1)} %copy.79) | copy-start | bytes 442372
  105.5 3.1 %copy-start.25 = (bf16[2,3,256,48]{2,1,3,0:T(4,128)(2,1)S(1)}, bf16[2,3,256,48]{2,1,3,0:T(4,128)(2,1)}, u32[]{:S(2)}) copy-start(bf16[2,3,256,48]{2,1,3,0:T(4,128)(2,1)} %copy.76) | copy-start | bytes 442372
  108.7 3.0 %copy-start.39 = (bf16[128]{0:T(256)(128)(2,1)S(1)}, bf16[128]{0:T(256)(128)(2,1)}, u32[]{:S(2)}) copy-start(bf16[128]{0:T(256)(128)(2,1)} %param.38) | copy-start | bytes 772
  108.7 3.0 %copy-start.33 = (bf16[128,16]{0,1:T(8,128)(2,1)S(1)}, bf16[128,16]{0,1:T(8,128)(2,1)}, u32[]{:S(2)}) copy-start(bf16[128,16]{0,1:T(8,128)(2,1)} %param.39) | copy-start | bytes 12292
  113.2 6.1 %copy-start.37 = (bf16[128]{0:T(256)(128)(2,1)S(1)}, bf16[128]{0:T(256)(128)(2,1)}, u32[]{:S(2)}) copy-start(bf16[128]{0:T(256)(128)(2,1)} %param.36) | copy-start | bytes 772
  113.2 6.1 %copy-start.11 = (bf16[128,128]{1,0:T(8,128)(2,1)S(1)}, bf16[128,128]{1,0:T(8,128)(2,1)}, u32[]{:S(2)}) copy-start(bf16[128,128]{1,0:T(8,128)(2,1)} %w_ref.1) | copy-start | bytes 98308
  113.2 32.8 %all-to-all-start.3 = ((bf16[2,3,768,192]{2,3,1,0:T(8,128)(2,1)}), bf16[2,3,768,192]{2,3,1,0:T(8,128)(2,1)}, u32[]{:S(2)}, u32[]{:S(2)}) async-start(bf16[2,3,768,192]{2,3,1,0:T(8,128)(2,1)} %copy.80), calls=%async_computation.3 | async-start | bytes 3538944 | tf_op jit(solution)/shard_map/all_to_all | solution.py:310
  119.3 1.7 copy-start.3
  121.0 1.3 copy-start.10
  146.0 8.7 %copy-start.31 = (s32[768]{0:T(1024)S(1)}, s32[768]{0:T(1024)}, u32[]{:S(2)}) copy-start(s32[768]{0:T(1024)} %param.27) | copy-start | bytes 9220
  146.0 9.1 %copy-start.40 = (f32[16]{0:T(128)S(1)}, f32[16]{0:T(128)}, u32[]{:S(2)}) copy-start(f32[16]{0:T(128)} %param.40) | copy-start | bytes 196
  146.0 29.1 %all-to-all-start.2 = ((bf16[128,40,128]{2,1,0:T(8,128)(2,1)}), bf16[128,40,128]{2,1,0:T(8,128)(2,1)S(1)}, u32[]{:S(2)}, u32[]{:S(2)}) async-start(bf16[128,40,128]{2,1,0:T(8,128)(2,1)} %bitcast.12), calls=%async_computation.2 | async-start | bytes 2621440 | tf_op jit(solution)/shard_map/all_to_all | solution.py:310
  175.1 1.3 copy-start.4
  176.3 1.3 copy-start.5
  177.6 1.3 copy-start.6
  178.9 1.3 copy-start.7
  200.1 1.0 copy-start.8
  201.1 7.3 %copy-start.35 = (bf16[768]{0:T(1024)(128)(2,1)S(1)}, bf16[768]{0:T(1024)(128)(2,1)}, u32[]{:S(2)}) copy-start(bf16[768]{0:T(1024)(128)(2,1)} %param.46) | copy-start | bytes 4612
  203.3 17.9 %all-to-all-start.4 = ((bf16[16,3,96,48]{2,3,1,0:T(8,128)(2,1)}), bf16[16,3,96,48]{2,3,1,0:T(8,128)(2,1)S(1)}, u32[]{:S(2)}, u32[]{:S(2)}) async-start(bf16[16,3,96,48]{2,3,1,0:T(8,128)(2,1)} %bitcast.24), calls=%async_computation.4 | async-start | bytes 1179648 | tf_op jit(solution)/shard_map/all_to_all | solution.py:310
  208.4 20.9 %copy-start.32 = (f32[768]{0:T(1024)}, f32[768]{0:T(1024)S(1)}, u32[]{:S(2)}) copy-start(f32[768]{0:T(1024)S(1)} %convert_element_type.64) | copy-start | bytes 9220
  221.2 24.9 %all-to-all-start.5 = ((bf16[128,40,128]{2,1,0:T(8,128)(2,1)}), bf16[128,40,128]{2,1,0:T(8,128)(2,1)}, u32[]{:S(2)}, u32[]{:S(2)}) async-start(bf16[128,40,128]{2,1,0:T(8,128)(2,1)} %bitcast.28), calls=%async_computation.5 | async-start | bytes 2621440 | tf_op jit(solution)/shard_map/all_to_all | solution.py:310
  226.9 3.6 %copy-start.38 = (bf16[768,1536]{1,0:T(8,128)(2,1)S(1)}, bf16[768,1536]{1,0:T(8,128)(2,1)}, u32[]{:S(2)}) copy-start(bf16[768,1536]{1,0:T(8,128)(2,1)} %param.47) | copy-start | bytes 7077892
  229.0 0.9 copy-start.16
  230.0 0.6 copy-start.36
  232.7 24.0 %copy-start.1 = (bf16[3,768,768]{2,1,0:T(8,128)(2,1)S(1)}, bf16[3,768,768]{2,1,0:T(8,128)(2,1)}, u32[]{:S(2)}) copy-start(bf16[3,768,768]{2,1,0:T(8,128)(2,1)} %param.29) | copy-start | bytes 10616836
Sparse Core Ops, SparseCore 0:
  44.9 64.7 all-gather.1

commit v2 on v1

v2 whole, which is shorter than its diff:
```python
import functools
import jax
import jax.numpy as jnp
from jax import lax
from jax.experimental import pallas as pl
from jax.experimental.pallas import tpu as pltpu
from jax.sharding import Mesh, PartitionSpec as P

HD = 48
F32 = jnp.float32
BF16 = jnp.bfloat16
ROWS = ("grp", "y", "core")
COLS = ("xh", "z")
ALL = ROWS + COLS
LOG2E = 1.4426950408889634
SCALE = HD ** (-0.5) * LOG2E
VMEM_LIMIT = 60 * 1024 * 1024
FORWARD_ROWS = 384
PROJECT_PAR = 2
UPDATE_PAR = 4
BACKWARD_ROWS = 192


def layer_norm(value_rows, gain_vec):
    middle = value_rows - jnp.mean(value_rows, axis=-1, keepdims=True)
    spread = jnp.mean(middle * middle, axis=-1, keepdims=True)
    return middle * lax.rsqrt(spread + 1e-05) * gain_vec.astype(F32)


def matmul(left_side, right_side):
    return jnp.dot(left_side, right_side, preferred_element_type=F32)


def dot_nt(a, b):
    return lax.dot_general(a, b, (((1,), (1,)), ((), ())), preferred_element_type=F32)


def dot_tn(a, b):
    return lax.dot_general(a, b, (((0,), (0,)), ((), ())), preferred_element_type=F32)


def lanes_of(rows):
    return lax.broadcasted_iota(jnp.int32, (rows, 128), 1)


def roll(value, shift):
    shift = shift % 128
    return value if shift == 0 else pltpu.roll(value, shift, 1)


def call(kernel, outs, args, scratch, name, flops=0, nbytes=0, spaces=None, grid=None, out_specs=None):
    vmem = pl.BlockSpec(memory_space=pltpu.VMEM)
    return pl.pallas_call(
        kernel,
        out_shape=outs,
        in_specs=spaces or [vmem] * len(args),
        out_specs=out_specs or jax.tree.map(lambda _: vmem, outs),
        scratch_shapes=scratch,
        compiler_params=pltpu.CompilerParams(vmem_limit_bytes=VMEM_LIMIT),
        cost_estimate=pl.CostEstimate(flops=flops, bytes_accessed=nbytes, transcendentals=0),
        name=name,
        **({} if grid is None else {"grid": grid}),
    )(*args)


def start_all(copies):
    for copy in copies:
        copy.start()
    return copies


def wait_all(copies):
    for copy in copies:
        copy.wait()


def project_kernel(
    pair_hbm, gain_ref, pl_hbm, pr_hbm, gl_hbm, gr_hbm, mask_hbm, place_ref, out_hbm, normed_hbm,
    scr, pair_ref, normed_ref, w_ref, out_ref, mask_ref, pair_sems, w_sems, out_sems,
):
    blocks = [pl.ds(512 * n, 512) for n in range(9)]
    pair_copies = start_all(
        [pltpu.make_async_copy(pair_hbm.at[b], pair_ref.at[b], pair_sems.at[n]) for n, b in enumerate(blocks)]
    )
    w_copies = start_all(
        [
            pltpu.make_async_copy(src, w_ref.at[n], w_sems.at[n])
            for n, src in enumerate((pl_hbm, pr_hbm, gl_hbm, gr_hbm))
        ]
        + [pltpu.make_async_copy(mask_hbm, mask_ref, w_sems.at[4])]
    )
    gain = gain_ref[...]
    normed_copies = []
    for n, block in enumerate(blocks):
        pair_copies[n].wait()
        normed_ref[block, :] = layer_norm(pair_ref[block, :].astype(F32), gain).astype(BF16)
        copy = pltpu.make_async_copy(normed_ref.at[block], normed_hbm.at[block], out_sems.at[n])
        copy.start()
        normed_copies.append(copy)
    wait_all(w_copies)
    lane = lanes_of(1)
    row_start = place_ref[0]
    col_start = place_ref[1]
    wide_cols = jnp.zeros((1, 128), F32)
    thin_cols = jnp.zeros((1, 128), F32)
    for k in range(64):
        wide_cols = jnp.where(lane % 64 == k, mask_ref[col_start + k].astype(F32), wide_cols)
    for k in range(32):
        thin_cols = jnp.where(lane % 32 == k, mask_ref[col_start + 64 + k].astype(F32), thin_cols)
    low = lanes_of(128) < 64
    weights = jnp.concatenate([w_ref[n].astype(F32).T.astype(BF16) for n in range(4)], axis=0)

    def rows_at(i, start, size):
        return normed_ref[pl.ds(pl.multiple_of(i * 96 + start, 32), size), :]

    def one(i):
        wide = [rows_at(i, 0, 64), rows_at(i + 24, 0, 64)]
        thin = [rows_at(i, 64, 32), rows_at(i + 24, 64, 32)]
        y = dot_nt(weights, jnp.concatenate(wide + thin + thin, axis=0))
        first = mask_ref[row_start + i].astype(F32)
        second = mask_ref[row_start + i + 24].astype(F32)
        wide_mask = jnp.where(lane < 64, first, second) * wide_cols
        thin_mask = jnp.where(lane % 64 < 32, first, second) * thin_cols
        left = y[0:128, 0:128] * jax.nn.sigmoid(y[256:384, 0:128])
        right = y[128:256, 0:128] * jax.nn.sigmoid(y[384:512, 0:128])
        both_p = jnp.where(low, y[0:128, 128:256], y[128:256, 128:256])
        both_g = jnp.where(low, y[256:384, 128:256], y[384:512, 128:256])
        scr[pl.ds(i, 128, stride=72), :] = left * wide_mask
        scr[pl.ds(i + 24, 128, stride=72), :] = right * wide_mask
        scr[pl.ds(i + 48, 128, stride=72), :] = both_p * jax.nn.sigmoid(both_g) * thin_mask

    def chunk(i, carry):
        for k in range(PROJECT_PAR):
            one(PROJECT_PAR * i + k)
        return carry

    lax.fori_loop(0, 24 // PROJECT_PAR, chunk, 0)
    out_copies = []
    for n in range(8):
        part = scr[1152 * n : 1152 * n + 1152, :].reshape(16, 72, 128)
        out_ref[16 * n : 16 * n + 16] = part.astype(BF16)
        copy = pltpu.make_async_copy(
            out_ref.at[pl.ds(16 * n, 16)], out_hbm.at[pl.ds(16 * n, 16)], out_sems.at[9 + n]
        )
        copy.start()
        out_copies.append(copy)
    wait_all(normed_copies + out_copies)


def token_kernel(
    tokens_ref, grad_ref, gain_ref, wq_ref, wk_ref, wv_ref, wo_ref, core_ref, keep_ref, send_ref, w_scr, wo_scr, norm_scr
):
    even = core_ref[0] == 0

    @pl.when(pl.program_id(0) == 0)
    def _():
        gap = jnp.zeros((768, 16), F32)
        for n, ref in enumerate((wq_ref, wk_ref, wv_ref)):
            w = ref[...].astype(F32)
            w = jnp.concatenate([w[:, 0:48], gap, w[:, 48:96], gap], axis=1)
            w_scr[:, 128 * n : 128 * n + 128] = jnp.where(even, w, roll(w, 64)).astype(BF16)
        first, second = wo_ref[0:48, :], wo_ref[48:96, :]
        wo_scr[0:48, :] = jnp.where(even, first, second)
        wo_scr[64:112, :] = jnp.where(even, second, first)
        wo_scr[48:64, :] = jnp.zeros((16, 768), BF16)
        wo_scr[112:128, :] = jnp.zeros((16, 768), BF16)

    gain = gain_ref[...]

    def norm_block(block, carry):
        rows = pl.ds(pl.multiple_of(block * 96, 32), 96)
        norm_scr[rows, :] = layer_norm(tokens_ref[0, rows, :].astype(F32), gain).astype(BF16)
        return carry

    lax.fori_loop(0, 8, norm_block, 0)
    low = lanes_of(768) < 64
    query = matmul(norm_scr[...], w_scr[:, 0:128])
    grads = dot_nt(grad_ref[0], wo_scr[...])
    keep_ref[0, 0] = jnp.where(low, query, roll(grads, 64)).astype(BF16)
    send_ref[0, 0] = jnp.where(low, roll(query, 64), grads).astype(BF16)
    key = matmul(norm_scr[...], w_scr[:, 128:256])
    value = matmul(norm_scr[...], w_scr[:, 256:384])
    for ref, full in (
        (keep_ref, jnp.where(low, key, roll(value, 64))),
        (send_ref, jnp.where(low, roll(key, 64), value)),
    ):
        full = full.astype(BF16)
        for q in range(8):
            ref[0, 1, 64 * q : 64 * q + 64] = full[96 * q : 96 * q + 64]
            ref[0, 1, 512 + 32 * q : 544 + 32 * q] = full[96 * q + 64 : 96 * q + 96]


def unpack_wide(first, second, low):
    top = jnp.where(low, first, roll(second, 64))
    bottom = jnp.where(low, roll(first, 64), second)
    return top, bottom


def product_kernel(in_hbm, out_hbm, in_ref, out_ref, l_scr, r_scr, in_sems, out_sems):
    copies = start_all(
        [
            pltpu.make_async_copy(
                in_hbm.at[:, pl.ds(4 * u, 4)], in_ref.at[:, pl.ds(4 * u, 4)], in_sems.at[u]
            )
            for u in range(2)
        ]
    )
    lane = lanes_of(384)
    low = lane < 64

    def put(dst, column, full):
        full = full.reshape(768, 128).astype(BF16)
        if dst is l_scr:
            dst[:, column : column + 128] = full
        else:
            for q in range(8):
                dst[64 * q : 64 * q + 64, column : column + 128] = full[96 * q : 96 * q + 64]
                dst[512 + 32 * q : 544 + 32 * q, column : column + 128] = full[96 * q + 64 : 96 * q + 96]

    def stack(halves):
        return jnp.concatenate([h.reshape(16, 24, 128) for h in halves], axis=1)

    def part(value, start):
        return value[:, start : start + 24].reshape(384, 128)

    for u in range(2):
        copies[u].wait()
        blocks = [in_ref[:, 4 * u + v].astype(F32) for v in range(4)]
        for p in range(2):
            for dst, start in ((l_scr, 0), (r_scr, 24)):
                halves = unpack_wide(part(blocks[2 * p], start), part(blocks[2 * p + 1], start), low)
                put(dst, (2 * u + p) * 128, stack(halves))
        thin = [part(b, 48) for b in blocks]
        for dst, base in ((l_scr, 0), (r_scr, 2)):
            halves = []
            for a in range(2):
                parts = [roll(thin[v], 32 * (v - base - a)) for v in range(4)]
                lower = jnp.where(lane < 32, parts[0], parts[1])
                upper = jnp.where(lane < 96, parts[2], parts[3])
                halves.append(jnp.where(low, lower, upper))
            put(dst, 512 + u * 128, stack(halves))
    out_copies = []
    for b in range(4):
        product = dot_nt(l_scr[192 * b : 192 * b + 192, :], r_scr[...])
        pack_rows(product, out_ref, 4 * b, 4)
        copy = pltpu.make_async_copy(
            out_ref.at[pl.ds(4 * b, 4)], out_hbm.at[pl.ds(4 * b, 4)], out_sems.at[b]
        )
        copy.start()
        out_copies.append(copy)
    wait_all(out_copies)


def pack_rows(full, out_ref, first, count):
    low = lanes_of(count * 24) < 64
    lane = lanes_of(count * 16)
    for q in range(8):
        tile = full[:, 128 * (q // 2) : 128 * (q // 2) + 128].reshape(count, 48, 128)
        top = tile[:, 0:24].reshape(count * 24, 128)
        bottom = tile[:, 24:48].reshape(count * 24, 128)
        if q % 2 == 0:
            wide = jnp.where(low, top, roll(bottom, 64))
        else:
            wide = jnp.where(low, roll(top, 64), bottom)
        tile = full[:, 512 + 128 * (q // 4) : 640 + 128 * (q // 4)].reshape(count, 48, 128)
        thin = [
            roll(tile[:, 16 * m : 16 * m + 16].reshape(count * 16, 128), 32 * (m - q % 4))
            for m in range(3)
        ]
        thin = jnp.where(lane < 32, thin[0], jnp.where(lane < 64, thin[1], thin[2]))
        piece = jnp.concatenate(
            [wide.reshape(count, 24, 128), thin.reshape(count, 16, 128)], axis=1
        )
        out_ref[pl.ds(first, count), q] = piece.astype(BF16)


def wide_places(i):
    return [(i, 0, 64), (i + 24, 0, 64)]


def thin_places(i):
    return [(i + 16 * m, 64, 32) for m in range(3)]


def update_kernel(
    t_hbm, pair_hbm, gate_hbm, w_ref, tri_gain_ref, bias_gain_ref, bp_ref, out_hbm, bias_hbm,
    scr, b_scr, t_ref, pair_ref, gate_ref, out_ref, bias_ref, t_sems, sems, out_sems,
):
    t_copies = start_all(
        [
            pltpu.make_async_copy(t_hbm.at[pl.ds(32 * n, 32)], t_ref.at[pl.ds(32 * n, 32)], t_sems.at[n])
            for n in range(4)
        ]
    )
    copies = start_all(
        [
            pltpu.make_async_copy(pair_hbm, pair_ref, sems.at[0]),
            pltpu.make_async_copy(gate_hbm, gate_ref, sems.at[1]),
        ]
    )
    for n in range(4):
        t_copies[n].wait()
        scr[1280 * n : 1280 * n + 1280, :] = t_ref[32 * n : 32 * n + 32].astype(F32).reshape(1280, 128)
    wait_all(copies)
    weight = w_ref[...]
    tri_gain = tri_gain_ref[...]
    bias_gain = bias_gain_ref[...]
    bias_proj = bp_ref[...]

    def group(positions, places):
        normed = []
        for position in positions:
            tri = scr[pl.ds(position, 128, stride=40), :]
            middle = tri - jnp.mean(tri, axis=0, keepdims=True)
            spread_of = jnp.mean(middle * middle, axis=0, keepdims=True)
            normed.append((middle * lax.rsqrt(spread_of + 1e-05) * tri_gain).astype(BF16))
        update = dot_tn(jnp.concatenate(normed, axis=1), weight)
        fed = []
        for n, spots in enumerate(places):
            at = 128 * n
            for row, start, size in spots:
                cols = pl.ds(start, size)
                new = pair_ref[row, cols, :].astype(F32) + gate_ref[row, cols, :] * update[at : at + size]
                out_ref[row, cols, :] = new
                fed.append(layer_norm(new, bias_gain).astype(BF16))
                at += size
            if len(spots) == 3:
                fed.append(fed[-1])
        bias = dot_nt(bias_proj, jnp.concatenate(fed, axis=0))
        for n, position in enumerate(positions):
            b_scr[pl.ds(position, 16, stride=40), :] = bias[:, 128 * n : 128 * n + 128]

    par = UPDATE_PAR

    def wide(i, carry):
        group([par * i + n for n in range(par)], [wide_places(par * i + n) for n in range(par)])
        return carry

    def thin(i, carry):
        group([24 + par * i + n for n in range(par)], [thin_places(par * i + n) for n in range(par)])
        return carry

    lax.fori_loop(0, 24 // par, wide, 0)
    out_copies = [
        pltpu.make_async_copy(out_ref.at[:, pl.ds(c, n)], out_hbm.at[:, pl.ds(c, n)], out_sems.at[8 + k])
        for k, (c, n) in enumerate(((0, 64), (64, 32)))
    ]
    out_copies[0].start()
    lax.fori_loop(0, 16 // par, thin, 0)
    out_copies[1].start()
    bias_ref[...] = b_scr[...].reshape(16, 40, 128).astype(BF16)
    out_copies += start_all(
        [pltpu.make_async_copy(bias_ref, bias_hbm.at[n], out_sems.at[n]) for n in range(8)]
    )
    wait_all(out_copies)


def unpack_bias(bias_ref, copies, put):
    low = lanes_of(384) < 64
    lane = lanes_of(256)
    for u in range(2):
        copies[u].wait()
        blocks = [bias_ref[:, 4 * u + v].astype(F32) for v in range(4)]
        for p in range(2):
            halves = unpack_wide(
                blocks[2 * p][:, 0:24].reshape(384, 128),
                blocks[2 * p + 1][:, 0:24].reshape(384, 128),
                low,
            )
            put((2 * u + p) * 128, jnp.concatenate([h.reshape(16, 24, 128) for h in halves], axis=1))
        thin = [b[:, 24:40].reshape(256, 128) for b in blocks]
        thirds = []
        for m in range(3):
            parts = [roll(thin[v], 32 * (v - m)) for v in range(4)]
            lower = jnp.where(lane < 32, parts[0], parts[1])
            upper = jnp.where(lane < 96, parts[2], parts[3])
            thirds.append(jnp.where(lane < 64, lower, upper).reshape(16, 16, 128))
        put(512 + u * 128, jnp.concatenate(thirds, axis=1))


def pair_copies(keep_hbm, recv_hbm, pairs, sems):
    return start_all(
        [
            pltpu.make_async_copy(src, pairs.at[pl.ds(3 * n, 3)], sems.at[n])
            for n, src in enumerate((keep_hbm, recv_hbm))
        ]
    )


def forward_kernel(
    bias_hbm, keep_hbm, recv_hbm, chain_row_ref, chain_col_ref, place_ref, weight_ref,
    mixed_hbm, full_hbm, stats_hbm, pairs, bias_ref, mixed_ref, full_ref, stats_ref, sems, in_sems, out_sems,
):
    bias_copies = start_all(
        [
            pltpu.make_async_copy(
                bias_hbm.at[:, pl.ds(4 * u, 4)], bias_ref.at[:, pl.ds(4 * u, 4)], in_sems.at[u]
            )
            for u in range(2)
        ]
    )
    copies = pair_copies(keep_hbm, recv_hbm, pairs, sems)
    core = place_ref[2]
    head_weight = weight_ref[place_ref[3]] * LOG2E

    def put(column, full):
        same = chain_row_ref[...] == chain_col_ref[:, column : column + 128]
        full_ref[:, column : column + 128] = full.reshape(768, 128) * LOG2E + jnp.where(
            same, head_weight, 0.0
        )

    unpack_bias(bias_ref, bias_copies, put)
    full_copy = pltpu.make_async_copy(full_ref, full_hbm, out_sems.at[0])
    full_copy.start()
    stats_ref[...] = jnp.zeros_like(stats_ref)
    wait_all(copies)
    low_all = lanes_of(768) < 64
    lane = lanes_of(FORWARD_ROWS)
    low = lane < 64
    thin_low = lanes_of(48) < 64
    blocks = 768 // FORWARD_ROWS
    shares = FORWARD_ROWS // 96

    def block(s, b, owner, slot):
        both = pairs[s, 1]
        keys = jnp.where(low_all, both, jnp.zeros_like(both))
        rows = pl.ds(pl.multiple_of(b * FORWARD_ROWS, 32), FORWARD_ROWS)
        asked = pairs[s, 0, rows, :]
        weights = jnp.exp2(dot_nt(asked, keys) * SCALE + full_ref[rows, :])
        inverse = 1.0 / jnp.sum(weights, axis=-1, keepdims=True)
        mixed = matmul((weights * inverse).astype(BF16), both)
        center = jnp.sum(jnp.where(low, 0.0, asked.astype(F32) * mixed), axis=-1, keepdims=True)
        stats_ref[rows, :] = jnp.where(
            lane == s, inverse, jnp.where(lane == s + 64, center, stats_ref[rows, :])
        )
        for n in range(shares):
            mixed_ref[owner * 8 + b * shares + n, slot] = jnp.where(
                thin_low, roll(mixed[96 * n : 96 * n + 48], 64), mixed[96 * n + 48 : 96 * n + 96]
            ).astype(BF16)

    def step(i, carry):
        half = i // blocks
        owner = jnp.where(half == 0, core, 1 - core)
        for n in range(3):
            block(3 * half + n, i % blocks, owner, n)
        return carry

    def mixed_copy(owner, sem):
        part = pl.ds(owner * 8, 8)
        return pltpu.make_async_copy(mixed_ref.at[part], mixed_hbm.at[part], out_sems.at[sem])

    lax.fori_loop(0, blocks, step, 0)
    mixed_copy(core, 1).start()
    lax.fori_loop(blocks, 2 * blocks, step, 0)
    mixed_copy(1 - core, 2).start()
    stats_copy = pltpu.make_async_copy(stats_ref, stats_hbm, out_sems.at[3])
    stats_copy.start()
    mixed_copy(core, 1).wait()
    mixed_copy(1 - core, 2).wait()
    full_copy.wait()
    stats_copy.wait()


def backward_kernel(
    full_hbm, stats_hbm, keep_hbm, recv_hbm, grad_hbm, pairs, full_ref, stats_ref, grad_ref, sems, in_sems, out_sems
):
    copies = pair_copies(keep_hbm, recv_hbm, pairs, sems)
    copies += start_all([pltpu.make_async_copy(stats_hbm, stats_ref, in_sems.at[0])])
    copies += start_all([pltpu.make_async_copy(full_hbm, full_ref, in_sems.at[1])])
    wait_all(copies)
    low_all = lanes_of(768) < 64

    def row_block(b, carry):
        rows = pl.ds(pl.multiple_of(b * BACKWARD_ROWS, 32), BACKWARD_ROWS)
        total = None
        for s in range(6):
            both = pairs[s, 1]
            keys = jnp.where(low_all, both, jnp.zeros_like(both))
            values = jnp.where(low_all, jnp.zeros_like(both), both)
            asked = pairs[s, 0, rows, :]
            inverse = stats_ref[rows, s : s + 1]
            center = stats_ref[rows, s + 64 : s + 65]
            probs = jnp.exp2(dot_nt(asked, keys) * SCALE + full_ref[rows, :]) * inverse
            score_grad = probs * (dot_nt(asked, values) - center)
            total = score_grad if total is None else total + score_grad
        pack_rows(total, grad_ref, b * (BACKWARD_ROWS // 48), BACKWARD_ROWS // 48)
        grad_copy(b).start()
        return carry

    def grad_copy(b):
        part = pl.ds(b * (BACKWARD_ROWS // 48), BACKWARD_ROWS // 48)
        return pltpu.make_async_copy(grad_ref.at[part], grad_hbm.at[part], out_sems.at[b])

    lax.fori_loop(0, 768 // BACKWARD_ROWS, row_block, 0)
    wait_all([grad_copy(b) for b in range(768 // BACKWARD_ROWS)])


def pair_grad_kernel(in_hbm, w_ref, out_hbm, scr, in_ref, out_ref, in_sems, out_sems):
    copies = start_all([pltpu.make_async_copy(in_hbm.at[n], in_ref.at[n], in_sems.at[n]) for n in range(8)])
    total = None
    for n in range(8):
        copies[n].wait()
        part = in_ref[n].astype(F32)
        total = part if total is None else total + part
    scr[...] = total.reshape(640, 128)
    weight = w_ref[...]

    def group(positions, places):
        grad = jnp.concatenate([scr[pl.ds(p, 16, stride=40), :] for p in positions], axis=1)
        high = grad.astype(BF16)
        rest = grad - high.astype(F32)
        middle = rest.astype(BF16)
        least = (rest - middle.astype(F32)).astype(BF16)
        rows = dot_tn(jnp.concatenate([high, middle, least], axis=0), weight)
        for n, spots in enumerate(places):
            at = 128 * n
            for row, start, size in spots:
                out_ref[row, pl.ds(start, size), :] = rows[at : at + size]
                at += size

    par = UPDATE_PAR

    def wide(i, carry):
        group([par * i + n for n in range(par)], [wide_places(par * i + n) for n in range(par)])
        return carry

    def thin(i, carry):
        group([24 + par * i + n for n in range(par)], [thin_places(par * i + n) for n in range(par)])
        return carry

    lax.fori_loop(0, 24 // par, wide, 0)
    out_copies = [
        pltpu.make_async_copy(out_ref.at[:, pl.ds(c, n)], out_hbm.at[:, pl.ds(c, n)], out_sems.at[k])
        for k, (c, n) in enumerate(((0, 64), (64, 32)))
    ]
    out_copies[0].start()
    lax.fori_loop(0, 16 // par, thin, 0)
    out_copies[1].start()
    wait_all(out_copies)


def column_order(value, axis):
    shape = value.shape
    split = value.reshape(shape[:axis] + (8, 96) + shape[axis + 1 :])
    wide = lax.slice_in_dim(split, 0, 64, axis=axis + 1).reshape(shape[:axis] + (512,) + shape[axis + 1 :])
    thin = lax.slice_in_dim(split, 64, 96, axis=axis + 1).reshape(shape[:axis] + (256,) + shape[axis + 1 :])
    return jnp.concatenate([wide, thin], axis=axis)


def exchange(value, axes):
    return lax.all_to_all(value, axes, 0, 0, tiled=True)


def body(
    pair_state,
    pair_mask,
    chain_ids,
    tokens,
    grad_attn,
    norm_pair,
    proj_left,
    gate_left,
    proj_right,
    gate_right,
    gate_out,
    norm_tri,
    tri_out,
    norm_bias,
    bias_proj,
    chain_weight,
    norm_tokens,
    w_query,
    w_key,
    w_value,
    w_out,
    norm_ff,
    ff_gate,
    ff_up,
    ff_down,
):
    tile_rows, tile_cols, channels = pair_state.shape
    tile_size = tile_rows * tile_cols
    row_start = lax.axis_index(ROWS) * tile_rows
    col_index = lax.axis_index(COLS)
    col_start = col_index * tile_cols
    pair_flat = pair_state.reshape(tile_size, channels)

    vmem = pl.BlockSpec(memory_space=pltpu.VMEM)
    smem = pl.BlockSpec(memory_space=pltpu.SMEM)
    hbm = pl.BlockSpec(memory_space=pltpu.HBM)
    core_index = lax.axis_index("core")
    place = jnp.stack([row_start, col_start, core_index, 2 * col_index + core_index]).astype(jnp.int32)

    sides, normed = call(
        project_kernel,
        (jax.ShapeDtypeStruct((128, 72, 128), BF16), jax.ShapeDtypeStruct((tile_size, 128), BF16)),
        (
            pair_flat, norm_pair.astype(F32)[None], proj_left, proj_right, gate_left, gate_right,
            pair_mask, place,
        ),
        [
            pltpu.VMEM((128 * 72, 128), F32),
            pltpu.VMEM((tile_size, 128), BF16),
            pltpu.VMEM((tile_size, 128), BF16),
            pltpu.VMEM((4, 128, 128), BF16),
            pltpu.VMEM((128, 72, 128), BF16),
            pltpu.SMEM((768,), jnp.int32),
            pltpu.SemaphoreType.DMA((9,)),
            pltpu.SemaphoreType.DMA((5,)),
            pltpu.SemaphoreType.DMA((17,)),
        ],
        "project",
        flops=2 * 512 * 128 * 6144,
        nbytes=5_000_000,
        spaces=[hbm, vmem] + [hbm] * 5 + [smem],
        out_specs=(hbm, hbm),
    )
    sides_in = exchange(sides, ALL)

    samples, seq_len, model_width = tokens.shape
    part = jax.ShapeDtypeStruct((samples, 2, seq_len, 128), BF16)
    token_block = pl.BlockSpec((1, seq_len, model_width), lambda s: (s, 0, 0))
    part_block = pl.BlockSpec((1, 2, seq_len, 128), lambda s: (s, 0, 0, 0))
    keep, send = call(
        token_kernel,
        (part, part),
        (
            tokens, grad_attn, norm_tokens.astype(F32)[None], w_query, w_key, w_value, w_out, place[2:3],
        ),
        [pltpu.VMEM((768, 384), BF16), pltpu.VMEM((128, 768), BF16), pltpu.VMEM((768, 768), BF16)],
        "tokens",
        flops=2 * 2304 * 768 * 512,
        nbytes=12_000_000,
        spaces=[token_block, token_block] + [vmem] * 5 + [smem],
        grid=(samples,),
        out_specs=(part_block, part_block),
    )
    sides_in, keep, send = lax.optimization_barrier((sides_in, keep, send))
    recv = lax.ppermute(send, "core", [(0, 1), (1, 0)])
    w_out_all = lax.all_gather(w_out, COLS, axis=0, tiled=True)

    products = call(
        product_kernel,
        jax.ShapeDtypeStruct((16, 8, 40, 128), BF16),
        (sides_in.reshape(16, 8, 72, 128),),
        [
            pltpu.VMEM((16, 8, 72, 128), BF16),
            pltpu.VMEM((16, 8, 40, 128), BF16),
            pltpu.VMEM((768, 768), BF16),
            pltpu.VMEM((768, 768), BF16),
            pltpu.SemaphoreType.DMA((2,)),
            pltpu.SemaphoreType.DMA((4,)),
        ],
        "product",
        flops=2 * 768**3,
        nbytes=4_000_000,
        spaces=[hbm],
        out_specs=hbm,
    )
    tri_in = exchange(products.reshape(128, 40, 128), ALL)
    share_len = seq_len // 8
    token_share = lax.dynamic_slice_in_dim(tokens, col_index * share_len, share_len, 1)
    tri_in, recv, token_share = lax.optimization_barrier((tri_in, recv, token_share))

    gate = jax.nn.sigmoid(matmul(normed, gate_out))
    heads_first = jnp.transpose(bias_proj.T.reshape(8, 2, 128), (1, 0, 2)).reshape(16, 128)
    pair_out, bias = call(
        update_kernel,
        (jax.ShapeDtypeStruct(pair_state.shape, F32), jax.ShapeDtypeStruct((8, 16, 40, 128), BF16)),
        (
            tri_in,
            pair_state,
            gate.reshape(pair_state.shape),
            tri_out,
            jnp.broadcast_to(norm_tri.astype(F32)[:, None], (128, 128)),
            norm_bias.astype(F32)[None],
            heads_first,
        ),
        [
            pltpu.VMEM((128 * 40, 128), F32),
            pltpu.VMEM((16 * 40, 128), F32),
            pltpu.VMEM((128, 40, 128), BF16),
            pltpu.VMEM(pair_state.shape, BF16),
            pltpu.VMEM(pair_state.shape, F32),
            pltpu.VMEM(pair_state.shape, F32),
            pltpu.VMEM((16, 40, 128), BF16),
            pltpu.SemaphoreType.DMA((4,)),
            pltpu.SemaphoreType.DMA((2,)),
            pltpu.SemaphoreType.DMA((10,)),
        ],
        "update",
        flops=2 * 128 * 128 * 5120,
        nbytes=9_000_000,
        spaces=[hbm, hbm, hbm] + [vmem] * 4,
        out_specs=(hbm, hbm),
    )
    bias_in = exchange(bias.reshape(128, 40, 128), ALL).reshape(16, 8, 40, 128)

    pair_scratch = pltpu.VMEM((2 * samples, 2, seq_len, 128), BF16)
    mixed, full_bias, stats = call(
        forward_kernel,
        (
            jax.ShapeDtypeStruct((16, samples, 48, 128), BF16),
            jax.ShapeDtypeStruct((seq_len, seq_len), F32),
            jax.ShapeDtypeStruct((seq_len, 128), F32),
        ),
        (
            bias_in, keep, recv, chain_ids[:, None], column_order(chain_ids[None], 1), place, chain_weight,
        ),
        [
            pair_scratch,
            pltpu.VMEM((16, 8, 40, 128), BF16),
            pltpu.VMEM((16, samples, 48, 128), BF16),
            pltpu.VMEM((seq_len, seq_len), F32),
            pltpu.VMEM((seq_len, 128), F32),
            pltpu.SemaphoreType.DMA((2,)),
            pltpu.SemaphoreType.DMA((2,)),
            pltpu.SemaphoreType.DMA((4,)),
        ],
        "forward",
        flops=6 * 4 * 768 * 768 * 128,
        nbytes=12_000_000,
        spaces=[hbm, hbm, hbm, vmem, vmem, smem, smem],
        out_specs=(hbm, hbm, hbm),
    )
    mixed_in = exchange(mixed, ("core",) + COLS)
    bias_grad = call(
        backward_kernel,
        jax.ShapeDtypeStruct((16, 8, 40, 128), BF16),
        (full_bias, stats, keep, recv),
        [
            pair_scratch,
            pltpu.VMEM((seq_len, seq_len), F32),
            pltpu.VMEM((seq_len, 128), F32),
            pltpu.VMEM((16, 8, 40, 128), BF16),
            pltpu.SemaphoreType.DMA((2,)),
            pltpu.SemaphoreType.DMA((2,)),
            pltpu.SemaphoreType.DMA((768 // BACKWARD_ROWS,)),
        ],
        "backward",
        flops=6 * 4 * 768 * 768 * 128,
        nbytes=12_000_000,
        spaces=[hbm] * 4,
        out_specs=hbm,
    )
    grad_in = exchange(bias_grad.reshape(128, 40, 128), ALL).reshape(8, 16, 40, 128)

    mixed_rows = jnp.concatenate([mixed_in[..., 0:HD], mixed_in[..., 64 : 64 + HD]], axis=2)
    mixed_rows = jnp.transpose(mixed_rows.reshape(2, 8, samples, share_len, HD), (2, 3, 1, 0, 4))
    attn = matmul(mixed_rows.reshape(samples * share_len, model_width), w_out_all)
    state = token_share.reshape(samples * share_len, model_width).astype(F32) + attn
    ff_in = layer_norm(state, norm_ff).astype(BF16)
    hidden = (jax.nn.silu(matmul(ff_in, ff_gate)) * matmul(ff_in, ff_up)).astype(BF16)
    refined = (state + matmul(hidden, ff_down)).reshape(samples, share_len, model_width)

    pair_grad = call(
        pair_grad_kernel,
        jax.ShapeDtypeStruct(pair_state.shape, F32),
        (grad_in, jnp.concatenate([heads_first] * 3, axis=0)),
        [
            pltpu.VMEM((16 * 40, 128), F32),
            pltpu.VMEM((8, 16, 40, 128), BF16),
            pltpu.VMEM(pair_state.shape, F32),
            pltpu.SemaphoreType.DMA((8,)),
            pltpu.SemaphoreType.DMA((2,)),
        ],
        "pair_grad",
        flops=2 * 48 * 128 * 5120,
        nbytes=4_000_000,
        spaces=[hbm, vmem],
        out_specs=hbm,
    )
    return (pair_out, refined, pair_grad)


def solution(mesh):
    fine = Mesh(mesh.devices.reshape(2, 4, 2, 2, 4), ALL)
    pair = P(ROWS, COLS, None)
    sample_rows = P(ROWS, None, None)
    return jax.shard_map(
        body,
        mesh=fine,
        in_specs=(pair, P(), P(), sample_rows, sample_rows)
        + (P(),) * 12
        + (P(None, COLS),) * 3
        + (P(COLS, None),)
        + (P(),) * 4,
        out_specs=(pair, pair, pair),
        check_vma=False,
    )
```

time: 265 us -> 203 us (0.77)
  local copies, waits for them, and re-layouts: 55.9 us -> 11.9 us
  waiting for transfers between devices: 44.9 us -> 58 us
  matrix products: 23.8 us -> 13.7 us
  other arithmetic: 13.8 us -> 4.18 us
  starting transfers between devices: 42.5 us -> 36.4 us
  Pallas kernels: 68.1 us -> 63.9 us
    unnamed x86 -> x31, local copies, waits for them, and re-layouts: 20.1 us -> 3.12 us
    all_to_all x6 -> x5, waiting for transfers between devices: 44.2 us -> 57.5 us  [exchange(): return lax.all_to_all(value, axes, 0, 0, tiled=True)]
    dot_general x8 -> x4, matrix products: 23.8 us -> 13.7 us  [matmul(): return jnp.dot(left_side, right_side, preferred_element_type=F32)]
    all_to_all x6 -> x5, starting transfers between devices: 42.4 us -> 35 us  [exchange(): return lax.all_to_all(value, axes, 0, 0, tiled=True)]
    slice x3 -> x1, local copies, waits for them, and re-layouts: 7.52 us -> 0.23 us  [body(): mixed_in[..., 0:HD]]
    reshape x8 -> x1, local copies, waits for them, and re-layouts: 7.27 us -> 1.46 us  [body(): mixed_rows.reshape(2, 8, samples, share_len, HD)]
    reshape x5 -> x1, local copies, waits for them, and re-layouts: 5.1 us -> 0.08 us  [column_order(): lax.slice_in_dim(split, 64, 96, axis=axis + 1)]
    reshape x5 -> x1, local copies, waits for them, and re-layouts: 4.47 us -> 0.08 us  [column_order(): lax.slice_in_dim(split, 0, 64, axis=axis + 1)]
  transfers between devices with their start and end apart: 7 -> 7, of which waited for: 4 -> 5; matrix products, arithmetic and copies ran while one was open for 26% -> 13% of each run, Pallas kernels for 19% -> 16%
where the time goes in v2:
time: 203 us; the launch traced here: 202 us
  Pallas kernels  63.9 us (31%)
  waiting for transfers between devices  58 us (29%)
  starting transfers between devices  36.4 us (18%)
  between operations  14.3 us (7%)
  matrix products  13.7 us (7%)
  local copies, waits for them, and re-layouts  11.9 us (6%)
  other arithmetic  4.18 us (2%)
    pallas_call x7, Pallas kernels, call(): pl.pallas_call(kernel, out_shape=outs, in_specs=spaces or [vmem] * len(ar...  63.9 us
    all_to_all x5, waiting for transfers between devices, exchange(): return lax.all_to_all(value, axes, 0, 0, tiled=True)  57.5 us
    all_to_all x5, starting transfers between devices, exchange(): return lax.all_to_all(value, axes, 0, 0, tiled=True)  35 us
    dot_general x4, matrix products, matmul(): return jnp.dot(left_side, right_side, preferred_element_type=F32)  13.7 us
  transfers between devices with their start and end apart: 7, of which 5 were waited for; matrix products, arithmetic and copies ran while one was open for 13% of the time, Pallas kernels for 16%

profile of v2, /device:TPU:1, one launch (start us, length us, event | category | flops | bytes accessed | tf_op | source)
XLA Modules:
  0.0 202.4 jit_solution(10412446979240935412)
XLA Ops:
  7.2 0.0 copy-start
  7.2 1.3 bitcast_convert_fusion.1.gain_ref
  8.5 0.7 pad_add_fusion.1.place_ref
  9.2 9.6 %project.1 = (bf16[128,72,128]{2,1,0:T(8,128)(2,1)}, bf16[4608,128]{1,0:T(8,128)(2,1)}) custom-call(bf16[4608,128]{1,0:T(8,128)(2,1)} %bitcast.51, f32[1,128]{1,0:T(1,128)} %bitcast_convert_fusion.1.gain_ref, bf16[128,128]{1,0:T(8,128)(2,1)} %pl_hbm.1, bf16[128,128]{1,0:T(8,128)(2,1)} %pr_hbm.1, bf16[128,128]{1,0:T(8,128)(2,1)} %gl_hbm.1, ...), custom_call_target="tpu_custom_call" | custom-call | flops 805306368 | bytes 5000000 | tf_op jit(solution)/shard_map/project/pallas_call | solution.py:53
  18.7 0.0 copy-start.3
  18.8 0.0 copy-start.4
  18.8 0.0 copy-start.5
  18.8 0.0 copy-start.10
  18.8 11.9 %all-to-all-start = ((bf16[128,72,128]{2,1,0:T(8,128)(2,1)}), bf16[128,72,128]{2,1,0:T(8,128)(2,1)}, u32[]{:S(2)}, u32[]{:S(2)}) async-start(bf16[128,72,128]{2,1,0:T(8,128)(2,1)} %get-tuple-element.18), calls=%async_computation | async-start | bytes 4718592 | tf_op jit(solution)/shard_map/all_to_all | solution.py:551
  30.7 0.0 copy-done.3
  30.7 0.8 copy.32.wq_ref
  31.5 0.0 copy-done.4
  31.5 0.8 copy.33.wk_ref
  32.3 0.0 copy-done.5
  32.4 0.8 copy.34.wv_ref
  33.2 0.0 copy-done.10
  33.2 0.6 reshape.84.gain_ref
  33.8 12.8 %tokens.1 = (bf16[3,2,768,128]{3,2,1,0:T(8,128)(2,1)}, bf16[3,2,768,128]{3,2,1,0:T(8,128)(2,1)}) custom-call(bf16[3,768,768]{2,1,0:T(8,128)(2,1)} %tokens_ref.1, bf16[3,768,768]{2,1,0:T(8,128)(2,1)} %grad_ref.1, f32[1,768]{1,0:T(1,128)} %reshape.84.gain_ref, bf16[768,96]{1,0:T(8,128)(2,1)} %copy.32.wq_ref, bf16[768,96]{1,0:T(8,128)(2,1)} %copy.33.wk_ref, ...), custom_call_target="tpu_custom_call" | custom-call | flops 1811939328 | bytes 12000000 | tf_op jit(solution)/shard_map/tokens/pallas_call | solution.py:53
  46.6 15.0 %all-to-all-done = bf16[128,72,128]{2,1,0:T(8,128)(2,1)} async-done(((bf16[128,72,128]{2,1,0:T(8,128)(2,1)}), bf16[128,72,128]{2,1,0:T(8,128)(2,1)}, u32[]{:S(2)}, u32[]{:S(2)}) %all-to-all-start) | async-done | bytes 2359328 | tf_op jit(solution)/shard_map/all_to_all | solution.py:551
  61.6 4.9 %product.1 = bf16[16,8,40,128]{3,2,1,0:T(8,128)(2,1)} custom-call(bf16[16,8,72,128]{3,2,1,0:T(8,128)(2,1)} %bitcast.6.in_hbm), custom_call_target="tpu_custom_call" | custom-call | flops 905969664 | bytes 4000000 | tf_op jit(solution)/shard_map/product/pallas_call | solution.py:53
  66.5 0.0 copy-start.8
  66.5 0.0 copy-start.13
  66.5 6.4 %all-to-all-start.1 = ((bf16[128,40,128]{2,1,0:T(8,128)(2,1)}), bf16[128,40,128]{2,1,0:T(8,128)(2,1)}, u32[]{:S(2)}, u32[]{:S(2)}) async-start(bf16[128,40,128]{2,1,0:T(8,128)(2,1)} %bitcast.41), calls=%async_computation.1 | async-start | bytes 2621440 | tf_op jit(solution)/shard_map/all_to_all | solution.py:551
  72.9 1.2 collective-permute-start
  74.1 0.0 copy-done.8
  74.1 0.6 copy.39
  74.7 1.8 constant_dynamic-slice_fusion
  76.5 0.0 copy-done.13
  76.5 0.5 bitcast_convert_fusion.bias_gain_ref
  77.0 3.5 %fusion.2 = f32[4608,128]{1,0:T(8,128)} fusion(bf16[4608,128]{1,0:T(8,128)(2,1)} %get-tuple-element.24, bf16[128,128]{1,0:T(8,128)(2,1)} %param.35), kind=kOutput, calls=%fused_computation.3 | convolution fusion | flops 152764416 | bytes 3571712 | tf_op jit(solution)/shard_map/dot_general | solution.py:31
  80.5 0.0 collective-permute-done.recv_hbm
  80.5 12.5 %all-to-all-done.1.t_hbm = bf16[128,40,128]{2,1,0:T(8,128)(2,1)} async-done(((bf16[128,40,128]{2,1,0:T(8,128)(2,1)}), bf16[128,40,128]{2,1,0:T(8,128)(2,1)}, u32[]{:S(2)}, u32[]{:S(2)}) %all-to-all-start.1) | async-done | bytes 1310752 | tf_op jit(solution)/shard_map/all_to_all | solution.py:551
  93.0 0.7 broadcast_in_dim.31.tri_gain_ref
  93.7 10.9 %update.1 = (f32[48,96,128]{2,1,0:T(8,128)}, bf16[8,16,40,128]{3,2,1,0:T(8,128)(2,1)}) custom-call(bf16[128,40,128]{2,1,0:T(8,128)(2,1)} %all-to-all-done.1.t_hbm, bf16[48,96,128]{2,1,0:T(8,128)(2,1)} %pair_hbm.1, f32[48,96,128]{2,1,0:T(8,128)} %bitcast.48, bf16[128,128]{1,0:T(8,128)(2,1)} %w_ref.1, f32[128,128]{1,0:T(8,128)} %broadcast_in_dim.31.tri_gain_ref, ...), custom_call_target="tpu_custom_call" | custom-call | flops 167772160 | bytes 9000000 | tf_op jit(solution)/shard_map/update/pallas_call | solution.py:53
  104.6 0.0 copy-start.7
  104.6 6.1 %all-to-all-start.2 = ((bf16[128,40,128]{2,1,0:T(8,128)(2,1)}), bf16[128,40,128]{2,1,0:T(8,128)(2,1)}, u32[]{:S(2)}, u32[]{:S(2)}) async-start(bf16[128,40,128]{2,1,0:T(8,128)(2,1)} %bitcast.50), calls=%async_computation.2 | async-start | bytes 2621440 | tf_op jit(solution)/shard_map/all_to_all | solution.py:551
  110.7 0.2 all-gather.2.cloned.1.call-start
  110.9 0.5 all-gather.2.cloned.1.call-update
  111.5 0.1 reshape_broadcast_in_dim.3
  111.5 0.9 broadcast_in_dim.38.chain_row_ref
  112.5 0.1 slice.13
  112.5 0.1 reshape.77
  112.6 0.1 reshape.76
  112.7 0.6 pad_add_fusion.chain_col_ref
  113.3 17.6 %all-to-all-done.2 = bf16[128,40,128]{2,1,0:T(8,128)(2,1)} async-done(((bf16[128,40,128]{2,1,0:T(8,128)(2,1)}), bf16[128,40,128]{2,1,0:T(8,128)(2,1)}, u32[]{:S(2)}, u32[]{:S(2)}) %all-to-all-start.2) | async-done | bytes 1310752 | tf_op jit(solution)/shard_map/all_to_all | solution.py:551
  130.8 11.4 %forward.1 = (bf16[16,3,48,128]{3,2,1,0:T(8,128)(2,1)}, f32[768,768]{1,0:T(8,128)}, f32[768,128]{1,0:T(8,128)}) custom-call(bf16[16,8,40,128]{3,2,1,0:T(8,128)(2,1)} %bitcast.16.bias_hbm, bf16[3,2,768,128]{3,2,1,0:T(8,128)(2,1)} %get-tuple-element.28.keep_hbm, bf16[3,2,768,128]{3,2,1,0:T(8,128)(2,1)} %copy-done.12, s32[768,1]{1,0:T(8,128)} %broadcast_in_dim.38.chain_row_ref, ...), custom_call_target="tpu_custom_call" | custom-call | flops 1811939328 | bytes 12000000 | tf_op jit(solution)/shard_map/forward/pallas_call | solution.py:53
  142.3 5.1 %all-to-all-start.3 = ((bf16[16,3,48,128]{3,2,1,0:T(8,128)(2,1)}), bf16[16,3,48,128]{3,2,1,0:T(8,128)(2,1)S(1)}, u32[]{:S(2)}, u32[]{:S(2)}) async-start(bf16[16,3,48,128]{3,2,1,0:T(8,128)(2,1)} %get-tuple-element.30), calls=%async_computation.3 | async-start | bytes 1179648 | tf_op jit(solution)/shard_map/all_to_all | solution.py:551
  147.4 0.0 copy-done.9
  147.4 0.6 pad_maximum_fusion.1.w_ref
  148.0 9.0 %backward.1 = bf16[16,8,40,128]{3,2,1,0:T(8,128)(2,1)} custom-call(f32[768,768]{1,0:T(8,128)} %get-tuple-element.31.full_hbm, f32[768,128]{1,0:T(8,128)} %get-tuple-element.32.stats_hbm, bf16[3,2,768,128]{3,2,1,0:T(8,128)(2,1)} %get-tuple-element.28.keep_hbm, bf16[3,2,768,128]{3,2,1,0:T(8,128)(2,1)} %copy-done.12), custom_call_target="tpu_custom_call" | custom-call | flops 1811939328 | bytes 12000000 | tf_op jit(solution)/shard_map/backward/pallas_call | solution.py:53
  157.0 7.6 %all-to-all-done.3 = bf16[16,3,48,128]{3,2,1,0:T(8,128)(2,1)S(1)} async-done(((bf16[16,3,48,128]{3,2,1,0:T(8,128)(2,1)}), bf16[16,3,48,128]{3,2,1,0:T(8,128)(2,1)S(1)}, u32[]{:S(2)}, u32[]{:S(2)}) %all-to-all-start.3) | async-done | bytes 589856 | tf_op jit(solution)/shard_map/all_to_all | solution.py:551
  164.6 5.5 %all-to-all-start.4 = ((bf16[128,40,128]{2,1,0:T(8,128)(2,1)}), bf16[128,40,128]{2,1,0:T(8,128)(2,1)}, u32[]{:S(2)}, u32[]{:S(2)}) async-start(bf16[128,40,128]{2,1,0:T(8,128)(2,1)} %bitcast.49), calls=%async_computation.4 | async-start | bytes 2621440 | tf_op jit(solution)/shard_map/all_to_all | solution.py:551
  170.1 0.2 fusion.17
  170.4 0.2 pad_maximum_fusion
  170.6 1.5 copy.37
  172.1 2.1 %reshape.79 = bf16[288,768]{0,1:T(8,128)(2,1)S(1)} reshape(bf16[3,96,8,2,48]{1,0,4,3,2:T(4,128)(2,1)} %bitcast.47) | data formatting | bytes 884736 | tf_op jit(solution)/shard_map/reshape | solution.py:750
  174.2 0.0 all-gather.2.cloned.1.call-done
  174.2 2.1 %fusion.15 = (f32[288]{0:T(512)S(1)}, f32[288,768]{1,0:T(8,128)S(1)}) fusion(bf16[288,768]{1,0:T(8,128)(2,1)} %bitcast.43, bf16[288,768]{0,1:T(8,128)(2,1)S(1)} %reshape.79, bf16[768,768]{1,0:T(8,128)(2,1)} %all-gather.2.cloned.1.call-done), kind=kOutput, calls=%fused_computation.19 | convolution fusion | flops 340401888 | bytes 2950272 | tf_op jit(solution)/shard_map/dot_general | solution.py:31
  176.3 0.3 multiply_reduce_fusion
  176.6 0.6 copy-done.2
  177.2 2.2 %fusion.5 = f32[288,1536]{1,0:T(8,128)} fusion(bf16[768,1536]{1,0:T(8,128)(2,1)S(1)} %copy-done, f32[768]{0:T(1024)S(1)} %convert_element_type.24, f32[288]{0:T(512)S(1)} %add_rsqrt_fusion, f32[288]{0:T(512)S(1)} %broadcast_multiply_fusion, f32[288,768]{1,0:T(8,128)S(1)} %get-tuple-element.36, bf16[288,768]{1,0:T(8,128)(2,1)S(1)} %bitcast.45), kind=kOutput, calls=%fused_computation.12 | convolution fusion | flops 680804352 | bytes 5461248 | tf_op jit(solution)/shard_map/dot_general | solution.py:31
  179.4 6.1 %convolution_add_fusion = f32[288,768]{1,0:T(8,128)} fusion(bf16[1536,768]{1,0:T(8,128)(2,1)} %param.49, bf16[768,1536]{1,0:T(8,128)(2,1)} %param.48, f32[288,1536]{1,0:T(8,128)} %fusion.5, f32[768]{0:T(1024)S(1)} %convert_element_type.24, f32[288]{0:T(512)S(1)} %add_rsqrt_fusion, f32[288]{0:T(512)S(1)} %broadcast_multiply_fusion, f32[288,768]{1,0:T(8,128)} %copy-done.2, ...), kind=kOutput, calls=%fused_computation.6 | convolution fusion | flops 1363599360 | bytes 8705280 | tf_op jit(solution)/shard_map/dot_general | solution.py:31
  185.4 4.8 %all-to-all-done.4 = bf16[128,40,128]{2,1,0:T(8,128)(2,1)} async-done(((bf16[128,40,128]{2,1,0:T(8,128)(2,1)}), bf16[128,40,128]{2,1,0:T(8,128)(2,1)}, u32[]{:S(2)}, u32[]{:S(2)}) %all-to-all-start.4) | async-done | bytes 1310752 | tf_op jit(solution)/shard_map/all_to_all | solution.py:551
  190.3 5.3 %pair_grad.1 = f32[48,96,128]{2,1,0:T(8,128)} custom-call(bf16[8,16,40,128]{3,2,1,0:T(8,128)(2,1)} %bitcast.21.in_hbm, bf16[48,128]{1,0:T(8,128)(2,1)} %pad_maximum_fusion.1.w_ref), custom_call_target="tpu_custom_call" | custom-call | flops 62914560 | bytes 4000000 | tf_op jit(solution)/shard_map/pair_grad/pallas_call | solution.py:53
  (15 shorter events, 0.0 us)
Async XLA Ops:
  7.2 170.0 %copy-start = (bf16[768,1536]{1,0:T(8,128)(2,1)S(1)}, bf16[768,1536]{1,0:T(8,128)(2,1)}, u32[]{:S(2)}) copy-start(bf16[768,1536]{1,0:T(8,128)(2,1)} %param.47) | copy-start | bytes 7077892
  18.7 12.0 %copy-start.3 = (bf16[768,96]{0,1:T(8,128)(2,1)S(1)}, bf16[768,96]{0,1:T(8,128)(2,1)}, u32[]{:S(2)}) copy-start(bf16[768,96]{0,1:T(8,128)(2,1)} %param.42) | copy-start | bytes 442372
  18.8 12.8 %copy-start.4 = (bf16[768,96]{0,1:T(8,128)(2,1)S(1)}, bf16[768,96]{0,1:T(8,128)(2,1)}, u32[]{:S(2)}) copy-start(bf16[768,96]{0,1:T(8,128)(2,1)} %param.43) | copy-start | bytes 442372
  18.8 13.6 %copy-start.5 = (bf16[768,96]{0,1:T(8,128)(2,1)S(1)}, bf16[768,96]{0,1:T(8,128)(2,1)}, u32[]{:S(2)}) copy-start(bf16[768,96]{0,1:T(8,128)(2,1)} %param.44) | copy-start | bytes 442372
  18.8 14.4 %copy-start.10 = (bf16[768]{0:T(1024)(128)(2,1)S(1)}, bf16[768]{0:T(1024)(128)(2,1)}, u32[]{:S(2)}) copy-start(bf16[768]{0:T(1024)(128)(2,1)} %param.41) | copy-start | bytes 4612
  18.8 42.8 %all-to-all-start = ((bf16[128,72,128]{2,1,0:T(8,128)(2,1)}), bf16[128,72,128]{2,1,0:T(8,128)(2,1)}, u32[]{:S(2)}, u32[]{:S(2)}) async-start(bf16[128,72,128]{2,1,0:T(8,128)(2,1)} %get-tuple-element.18), calls=%async_computation | async-start | bytes 4718592 | tf_op jit(solution)/shard_map/all_to_all | solution.py:551
  66.5 7.6 %copy-start.8 = (bf16[128,16]{0,1:T(8,128)(2,1)S(1)}, bf16[128,16]{0,1:T(8,128)(2,1)}, u32[]{:S(2)}) copy-start(bf16[128,16]{0,1:T(8,128)(2,1)} %param.39) | copy-start | bytes 12292
  66.5 10.0 %copy-start.13 = (bf16[128]{0:T(256)(128)(2,1)S(1)}, bf16[128]{0:T(256)(128)(2,1)}, u32[]{:S(2)}) copy-start(bf16[128]{0:T(256)(128)(2,1)} %param.38) | copy-start | bytes 772
  66.5 26.5 %all-to-all-start.1 = ((bf16[128,40,128]{2,1,0:T(8,128)(2,1)}), bf16[128,40,128]{2,1,0:T(8,128)(2,1)}, u32[]{:S(2)}, u32[]{:S(2)}) async-start(bf16[128,40,128]{2,1,0:T(8,128)(2,1)} %bitcast.41), calls=%async_computation.1 | async-start | bytes 2621440 | tf_op jit(solution)/shard_map/all_to_all | solution.py:551
  72.9 7.6 %collective-permute-start = (bf16[3,2,768,128]{3,2,1,0:T(8,128)(2,1)}, bf16[3,2,768,128]{3,2,1,0:T(8,128)(2,1)S(1)}, u32[]{:S(2)}, u32[]{:S(2)}) collective-permute-start(bf16[3,2,768,128]{3,2,1,0:T(8,128)(2,1)} %get-tuple-element.22), channel_id=1, source_target_pairs={{0,8},{8,0},{1,9},{9,1},{2,10},{10,2},{3,11},{11,3},{4,12},{12,4},... | collective-permute-start | bytes 3538952 | tf_op jit(solution)/shard_map/ppermute | solution.py:639
  77.0 16.0 %copy-start.11 = (bf16[128]{0:T(256)(128)(2,1)S(1)}, bf16[128]{0:T(256)(128)(2,1)}, u32[]{:S(2)}) copy-start(bf16[128]{0:T(256)(128)(2,1)} %param.36) | copy-start | bytes 772
  80.5 13.2 %copy-start.12 = (bf16[3,2,768,128]{3,2,1,0:T(8,128)(2,1)}, bf16[3,2,768,128]{3,2,1,0:T(8,128)(2,1)S(1)}, u32[]{:S(2)}) copy-start(bf16[3,2,768,128]{3,2,1,0:T(8,128)(2,1)S(1)} %collective-permute-done.recv_hbm) | copy-start | bytes 3538948
  104.6 6.8 %copy-start.7 = (s32[768]{0:T(1024)S(1)}, s32[768]{0:T(1024)}, u32[]{:S(2)}) copy-start(s32[768]{0:T(1024)} %param.27) | copy-start | bytes 9220
  104.6 26.2 %all-to-all-start.2 = ((bf16[128,40,128]{2,1,0:T(8,128)(2,1)}), bf16[128,40,128]{2,1,0:T(8,128)(2,1)}, u32[]{:S(2)}, u32[]{:S(2)}) async-start(bf16[128,40,128]{2,1,0:T(8,128)(2,1)} %bitcast.50), calls=%async_computation.2 | async-start | bytes 2621440 | tf_op jit(solution)/shard_map/all_to_all | solution.py:551
  110.7 63.5 %all-gather.2.cloned.1.call-start = ((), (), s32[]{:S(2)}) async-start(), calls=%async_computation.5 | async-start | bytes 1327104 | tf_op jit(solution)/shard_map/all_gather | solution.py:640
  130.8 16.6 %copy-start.9 = (bf16[768]{0:T(1024)(128)(2,1)S(1)}, bf16[768]{0:T(1024)(128)(2,1)}, u32[]{:S(2)}) copy-start(bf16[768]{0:T(1024)(128)(2,1)} %param.46) | copy-start | bytes 4612
  130.8 16.6 %copy-start.6 = (bf16[8,2,128]{2,0,1:T(8,128)(2,1)S(1)}, bf16[8,2,128]{2,0,1:T(8,128)(2,1)}, u32[]{:S(2)}) copy-start(bf16[8,2,128]{2,0,1:T(8,128)(2,1)} %copy.39) | copy-start | bytes 12292
  142.3 22.3 %all-to-all-start.3 = ((bf16[16,3,48,128]{3,2,1,0:T(8,128)(2,1)}), bf16[16,3,48,128]{3,2,1,0:T(8,128)(2,1)S(1)}, u32[]{:S(2)}, u32[]{:S(2)}) async-start(bf16[16,3,48,128]{3,2,1,0:T(8,128)(2,1)} %get-tuple-element.30), calls=%async_computation.3 | async-start | bytes 1179648 | tf_op jit(solution)/shard_map/all_to_all | solution.py:551
  164.6 25.7 %all-to-all-start.4 = ((bf16[128,40,128]{2,1,0:T(8,128)(2,1)}), bf16[128,40,128]{2,1,0:T(8,128)(2,1)}, u32[]{:S(2)}, u32[]{:S(2)}) async-start(bf16[128,40,128]{2,1,0:T(8,128)(2,1)} %bitcast.49), calls=%async_computation.4 | async-start | bytes 2621440 | tf_op jit(solution)/shard_map/all_to_all | solution.py:551
  174.2 2.1 %copy-start.1 = (bf16[3,96,768]{2,1,0:T(8,128)(2,1)S(1)}, bf16[3,96,768]{2,1,0:T(8,128)(2,1)}, u32[]{:S(2)}) copy-start(bf16[3,96,768]{2,1,0:T(8,128)(2,1)} %constant_dynamic-slice_fusion) | copy-start | bytes 1327108
  176.3 0.9 copy-start.2
Sparse Core Ops, SparseCore 0:
  113.9 52.4 all-gather.1

commit v3 on v2

--- a/solution.py
+++ b/solution.py
@@ -14,10 +14,10 @@
 ALL = ROWS + COLS
 LOG2E = 1.4426950408889634
 SCALE = HD ** (-0.5) * LOG2E
-VMEM_LIMIT = 60 * 1024 * 1024
-FORWARD_ROWS = 384
-PROJECT_PAR = 2
-UPDATE_PAR = 4
+FORWARD_ROWS = 768
+PROJECT_PAR = 12
+UPDATE_PAR = 12
+THIN_PAR = 16
 BACKWARD_ROWS = 192
 
 
@@ -48,7 +48,7 @@
     return value if shift == 0 else pltpu.roll(value, shift, 1)
 
 
-def call(kernel, outs, args, scratch, name, flops=0, nbytes=0, spaces=None, grid=None, out_specs=None):
+def call(kernel, outs, args, scratch, name, flops=0, nbytes=0, spaces=None, grid=None, out_specs=None, mib=60):
     vmem = pl.BlockSpec(memory_space=pltpu.VMEM)
     return pl.pallas_call(
         kernel,
@@ -56,7 +56,7 @@
         in_specs=spaces or [vmem] * len(args),
         out_specs=out_specs or jax.tree.map(lambda _: vmem, outs),
         scratch_shapes=scratch,
-        compiler_params=pltpu.CompilerParams(vmem_limit_bytes=VMEM_LIMIT),
+        compiler_params=pltpu.CompilerParams(vmem_limit_bytes=mib * 1024 * 1024),
         cost_estimate=pl.CostEstimate(flops=flops, bytes_accessed=nbytes, transcendentals=0),
         name=name,
         **({} if grid is None else {"grid": grid}),
@@ -274,6 +274,52 @@
         out_ref[pl.ds(first, count), q] = piece.astype(BF16)
 
 
+def transition_kernel(
+    mixed_hbm, ring_hbm, far_hbm, place_ref, token_hbm, gain_ref, gate_hbm, up_hbm, down_hbm, out_hbm,
+    mixed_ref, wo_ref, token_ref, gate_ref, up_ref, down_ref, x_ref, out_ref, sems, wo_sems, out_sems,
+):
+    pairs = ((mixed_hbm, mixed_ref), (token_hbm, token_ref), (gate_hbm, gate_ref), (up_hbm, up_ref), (down_hbm, down_ref))
+    wo_copies = []
+    for far, src in ((0, ring_hbm), (1, far_hbm)):
+        for n in range(8):
+            core = lax.rem(place_ref[2] + far, 2)
+            high = lax.rem(place_ref[4] + n // 4, 2)
+            block = core * 8 + high * 4 + lax.rem(place_ref[5] + n, 4)
+            wo_copies.append(
+                pltpu.make_async_copy(src.at[n], wo_ref.at[block, pl.ds(0, 48)], wo_sems.at[8 * far + n])
+            )
+    start_all(wo_copies)
+    copies = start_all([pltpu.make_async_copy(src, dst, sems.at[n]) for n, (src, dst) in enumerate(pairs)])
+    wo_ref[:, 48:64, :] = jnp.zeros((16, 16, 768), BF16)
+    copies[0].wait()
+    low = lanes_of(144) < 64
+    for n in range(8):
+        first = mixed_ref[2 * n].reshape(144, 128).astype(F32)
+        second = mixed_ref[2 * n + 1].reshape(144, 128).astype(F32)
+        top, bottom = unpack_wide(first, second, low)
+        x_ref[0:144, 128 * n : 128 * n + 128] = top.astype(BF16)
+        x_ref[144:288, 128 * n : 128 * n + 128] = bottom.astype(BF16)
+    wait_all(wo_copies)
+    attn = matmul(x_ref[...], wo_ref[...].reshape(1024, 768))
+    copies[1].wait()
+    token = jnp.concatenate([token_ref[s, 48 * half : 48 * half + 48] for half in range(2) for s in range(3)], axis=0)
+    state = token.astype(F32) + attn
+    fed = layer_norm(state, gain_ref[...]).astype(BF16)
+    wait_all(copies[2:])
+    refined = state
+    for n in range(3):
+        cols = slice(512 * n, 512 * n + 512)
+        hidden = jax.nn.silu(matmul(fed, gate_ref[:, cols])) * matmul(fed, up_ref[:, cols])
+        refined = refined + matmul(hidden.astype(BF16), down_ref[cols, :])
+    for half in range(2):
+        for s in range(3):
+            at = 144 * half + 48 * s
+            out_ref[s, 48 * half : 48 * half + 48] = refined[at : at + 48]
+    copy = pltpu.make_async_copy(out_ref, out_hbm, out_sems.at[0])
+    copy.start()
+    copy.wait()
+
+
 def wide_places(i):
     return [(i, 0, 64), (i + 24, 0, 64)]
 
@@ -330,14 +376,14 @@
         for n, position in enumerate(positions):
             b_scr[pl.ds(position, 16, stride=40), :] = bias[:, 128 * n : 128 * n + 128]
 
-    par = UPDATE_PAR
+    par, par2 = UPDATE_PAR, THIN_PAR
 
     def wide(i, carry):
         group([par * i + n for n in range(par)], [wide_places(par * i + n) for n in range(par)])
         return carry
 
     def thin(i, carry):
-        group([24 + par * i + n for n in range(par)], [thin_places(par * i + n) for n in range(par)])
+        group([24 + par2 * i + n for n in range(par2)], [thin_places(par2 * i + n) for n in range(par2)])
         return carry
 
     lax.fori_loop(0, 24 // par, wide, 0)
@@ -346,7 +392,7 @@
         for k, (c, n) in enumerate(((0, 64), (64, 32)))
     ]
     out_copies[0].start()
-    lax.fori_loop(0, 16 // par, thin, 0)
+    lax.fori_loop(0, 16 // par2, thin, 0)
     out_copies[1].start()
     bias_ref[...] = b_scr[...].reshape(16, 40, 128).astype(BF16)
     out_copies += start_all(
@@ -518,14 +564,14 @@
                 out_ref[row, pl.ds(start, size), :] = rows[at : at + size]
                 at += size
 
-    par = UPDATE_PAR
+    par, par2 = UPDATE_PAR, THIN_PAR
 
     def wide(i, carry):
         group([par * i + n for n in range(par)], [wide_places(par * i + n) for n in range(par)])
         return carry
 
     def thin(i, carry):
-        group([24 + par * i + n for n in range(par)], [thin_places(par * i + n) for n in range(par)])
+        group([24 + par2 * i + n for n in range(par2)], [thin_places(par2 * i + n) for n in range(par2)])
         return carry
 
     lax.fori_loop(0, 24 // par, wide, 0)
@@ -534,7 +580,7 @@
         for k, (c, n) in enumerate(((0, 64), (64, 32)))
     ]
     out_copies[0].start()
-    lax.fori_loop(0, 16 // par, thin, 0)
+    lax.fori_loop(0, 16 // par2, thin, 0)
     out_copies[1].start()
     wait_all(out_copies)
 
@@ -547,8 +593,217 @@
     return jnp.concatenate([wide, thin], axis=axis)
 
 
+def memory(space):
+    return pl.BlockSpec(memory_space=space)
+
+
+VMEM, SMEM, HBM = memory(pltpu.VMEM), memory(pltpu.SMEM), memory(pltpu.HBM)
+TILE = (48, 96, 128)
+PACKED = (16, 8, 40, 128)
+
+
+def shape(dims, dtype=BF16):
+    return jax.ShapeDtypeStruct(dims, dtype)
+
+
+def dma(count):
+    return pltpu.SemaphoreType.DMA((count,))
+
+
+def run_project(*args):
+    return call(
+        project_kernel,
+        (shape((128, 72, 128)), shape((4608, 128))),
+        args,
+        [
+            pltpu.VMEM((128 * 72, 128), F32),
+            pltpu.VMEM((4608, 128), BF16),
+            pltpu.VMEM((4608, 128), BF16),
+            pltpu.VMEM((4, 128, 128), BF16),
+            pltpu.VMEM((128, 72, 128), BF16),
+            pltpu.SMEM((768,), jnp.int32),
+            dma(9),
+            dma(5),
+            dma(17),
+        ],
+        "project",
+        flops=2 * 512 * 128 * 6144,
+        nbytes=5_000_000,
+        spaces=[HBM, VMEM] + [HBM] * 5 + [SMEM],
+        out_specs=(HBM, HBM),
+    )
+
+
+def run_tokens(samples, *args):
+    part = shape((samples, 2, 768, 128))
+    token_block = pl.BlockSpec((1, 768, 768), lambda s: (s, 0, 0))
+    part_block = pl.BlockSpec((1, 2, 768, 128), lambda s: (s, 0, 0, 0))
+    return call(
+        token_kernel,
+        (part, part),
+        args,
+        [pltpu.VMEM((768, 384), BF16), pltpu.VMEM((128, 768), BF16), pltpu.VMEM((768, 768), BF16)],
+        "tokens",
+        flops=2 * 2304 * 768 * 512,
+        nbytes=12_000_000,
+        spaces=[token_block, token_block] + [VMEM] * 5 + [SMEM],
+        grid=(samples,),
+        out_specs=(part_block, part_block),
+    )
+
+
+def run_product(*args):
+    return call(
+        product_kernel,
+        shape(PACKED),
+        args,
+        [
+            pltpu.VMEM((16, 8, 72, 128), BF16),
+            pltpu.VMEM(PACKED, BF16),
+            pltpu.VMEM((768, 768), BF16),
+            pltpu.VMEM((768, 768), BF16),
+            dma(2),
+            dma(4),
+        ],
+        "product",
+        flops=2 * 768**3,
+        nbytes=4_000_000,
+        spaces=[HBM],
+        out_specs=HBM,
+        mib=50,
+    )
+
+
+def run_update(*args):
+    return call(
+        update_kernel,
+        (shape(TILE, F32), shape((8, 16, 40, 128))),
+        args,
+        [
+            pltpu.VMEM((128 * 40, 128), F32),
+            pltpu.VMEM((16 * 40, 128), F32),
+            pltpu.VMEM((128, 40, 128), BF16),
+            pltpu.VMEM(TILE, BF16),
+            pltpu.VMEM(TILE, F32),
+            pltpu.VMEM(TILE, F32),
+            pltpu.VMEM((16, 40, 128), BF16),
+            dma(4),
+            dma(2),
+            dma(10),
+        ],
+        "update",
+        flops=2 * 128 * 128 * 5120,
+        nbytes=9_000_000,
+        spaces=[HBM, HBM, HBM] + [VMEM] * 4,
+        out_specs=(HBM, HBM),
+        mib=52,
+    )
+
+
+def run_forward(*args):
+    return call(
+        forward_kernel,
+        (shape((16, 3, 48, 128)), shape((768, 768), F32), shape((768, 128), F32)),
+        args,
+        [
+            pltpu.VMEM((6, 2, 768, 128), BF16),
+            pltpu.VMEM(PACKED, BF16),
+            pltpu.VMEM((16, 3, 48, 128), BF16),
+            pltpu.VMEM((768, 768), F32),
+            pltpu.VMEM((768, 128), F32),
+            dma(2),
+            dma(2),
+            dma(4),
+        ],
+        "forward",
+        flops=6 * 4 * 768 * 768 * 128,
+        nbytes=12_000_000,
+        spaces=[HBM, HBM, HBM, VMEM, VMEM, SMEM, SMEM],
+        out_specs=(HBM, HBM, HBM),
+        mib=51,
+    )
+
+
+def run_backward(*args):
+    return call(
+        backward_kernel,
+        shape(PACKED),
+        args,
+        [
+            pltpu.VMEM((6, 2, 768, 128), BF16),
+            pltpu.VMEM((768, 768), F32),
+            pltpu.VMEM((768, 128), F32),
+            pltpu.VMEM(PACKED, BF16),
+            dma(2),
+            dma(2),
+            dma(768 // BACKWARD_ROWS),
+        ],
+        "backward",
+        flops=6 * 4 * 768 * 768 * 128,
+        nbytes=12_000_000,
+        spaces=[HBM] * 4,
+        out_specs=HBM,
+    )
+
+
+def run_pair_grad(*args):
+    return call(
+        pair_grad_kernel,
+        shape(TILE, F32),
+        args,
+        [
+            pltpu.VMEM((16 * 40, 128), F32),
+            pltpu.VMEM((8, 16, 40, 128), BF16),
+            pltpu.VMEM(TILE, F32),
+            dma(8),
+            dma(2),
+        ],
+        "pair_grad",
+        flops=2 * 48 * 128 * 5120,
+        nbytes=4_000_000,
+        spaces=[HBM, VMEM],
+        out_specs=HBM,
+        mib=52,
+    )
+
+
+def run_transition(*args):
+    return call(
+        transition_kernel,
+        shape((3, 96, 768), F32),
+        args,
+        [
+            pltpu.VMEM((16, 3, 48, 128), BF16),
+            pltpu.VMEM((16, 64, 768), BF16),
+            pltpu.VMEM((3, 96, 768), BF16),
+            pltpu.VMEM((768, 1536), BF16),
+            pltpu.VMEM((768, 1536), BF16),
+            pltpu.VMEM((1536, 768), BF16),
+            pltpu.VMEM((288, 1024), BF16),
+            pltpu.VMEM((3, 96, 768), F32),
+            dma(5),
+            dma(16),
+            dma(1),
+        ],
+        "transition",
+        flops=2 * 288 * 768 * (1024 + 3 * 1536),
+        nbytes=12_000_000,
+        spaces=[HBM] * 3 + [SMEM, HBM, VMEM] + [HBM] * 3,
+        out_specs=HBM,
+        mib=51,
+    )
+
+
 def exchange(value, axes):
     return lax.all_to_all(value, axes, 0, 0, tiled=True)
+
+
+SWAP = [(0, 1), (1, 0)]
+
+
+def gather_ring(half):
+    ring = [half] + [lax.ppermute(half, "z", [(i, (i - k) % 4) for i in range(4)]) for k in range(1, 4)]
+    return jnp.stack(ring)
 
 
 def body(
@@ -585,191 +840,71 @@
     col_start = col_index * tile_cols
     pair_flat = pair_state.reshape(tile_size, channels)
 
-    vmem = pl.BlockSpec(memory_space=pltpu.VMEM)
-    smem = pl.BlockSpec(memory_space=pltpu.SMEM)
-    hbm = pl.BlockSpec(memory_space=pltpu.HBM)
     core_index = lax.axis_index("core")
-    place = jnp.stack([row_start, col_start, core_index, 2 * col_index + core_index]).astype(jnp.int32)
-
-    sides, normed = call(
-        project_kernel,
-        (jax.ShapeDtypeStruct((128, 72, 128), BF16), jax.ShapeDtypeStruct((tile_size, 128), BF16)),
-        (
-            pair_flat, norm_pair.astype(F32)[None], proj_left, proj_right, gate_left, gate_right,
-            pair_mask, place,
-        ),
-        [
-            pltpu.VMEM((128 * 72, 128), F32),
-            pltpu.VMEM((tile_size, 128), BF16),
-            pltpu.VMEM((tile_size, 128), BF16),
-            pltpu.VMEM((4, 128, 128), BF16),
-            pltpu.VMEM((128, 72, 128), BF16),
-            pltpu.SMEM((768,), jnp.int32),
-            pltpu.SemaphoreType.DMA((9,)),
-            pltpu.SemaphoreType.DMA((5,)),
-            pltpu.SemaphoreType.DMA((17,)),
-        ],
-        "project",
-        flops=2 * 512 * 128 * 6144,
-        nbytes=5_000_000,
-        spaces=[hbm, vmem] + [hbm] * 5 + [smem],
-        out_specs=(hbm, hbm),
+    place = jnp.stack(
+        [row_start, col_start, core_index, 2 * col_index + core_index, lax.axis_index("xh"), lax.axis_index("z")]
+    ).astype(jnp.int32)
+
+    sides, normed = run_project(
+        pair_flat, norm_pair.astype(F32)[None], proj_left, proj_right, gate_left, gate_right, pair_mask, place
     )
     sides_in = exchange(sides, ALL)
 
     samples, seq_len, model_width = tokens.shape
-    part = jax.ShapeDtypeStruct((samples, 2, seq_len, 128), BF16)
-    token_block = pl.BlockSpec((1, seq_len, model_width), lambda s: (s, 0, 0))
-    part_block = pl.BlockSpec((1, 2, seq_len, 128), lambda s: (s, 0, 0, 0))
-    keep, send = call(
-        token_kernel,
-        (part, part),
-        (
-            tokens, grad_attn, norm_tokens.astype(F32)[None], w_query, w_key, w_value, w_out, place[2:3],
-        ),
-        [pltpu.VMEM((768, 384), BF16), pltpu.VMEM((128, 768), BF16), pltpu.VMEM((768, 768), BF16)],
-        "tokens",
-        flops=2 * 2304 * 768 * 512,
-        nbytes=12_000_000,
-        spaces=[token_block, token_block] + [vmem] * 5 + [smem],
-        grid=(samples,),
-        out_specs=(part_block, part_block),
-    )
-    sides_in, keep, send = lax.optimization_barrier((sides_in, keep, send))
-    recv = lax.ppermute(send, "core", [(0, 1), (1, 0)])
-    w_out_all = lax.all_gather(w_out, COLS, axis=0, tiled=True)
-
-    products = call(
-        product_kernel,
-        jax.ShapeDtypeStruct((16, 8, 40, 128), BF16),
-        (sides_in.reshape(16, 8, 72, 128),),
-        [
-            pltpu.VMEM((16, 8, 72, 128), BF16),
-            pltpu.VMEM((16, 8, 40, 128), BF16),
-            pltpu.VMEM((768, 768), BF16),
-            pltpu.VMEM((768, 768), BF16),
-            pltpu.SemaphoreType.DMA((2,)),
-            pltpu.SemaphoreType.DMA((4,)),
-        ],
-        "product",
-        flops=2 * 768**3,
-        nbytes=4_000_000,
-        spaces=[hbm],
-        out_specs=hbm,
-    )
+    keep, send = run_tokens(
+        samples, tokens, grad_attn, norm_tokens.astype(F32)[None], w_query, w_key, w_value, w_out, place[2:3]
+    )
+    keep, send, w_out_late = lax.optimization_barrier((keep, send, w_out))
+    ring = gather_ring(lax.dynamic_slice_in_dim(w_out_late, core_index * HD, HD, 0))
+    sides_in, keep, send, ring = lax.optimization_barrier((sides_in, keep, send, ring))
+    recv = lax.ppermute(send, "core", SWAP)
+    products = run_product(sides_in.reshape(16, 8, 72, 128))
+    rings = jnp.concatenate([ring, lax.ppermute(ring, "xh", SWAP)], axis=0)
+    products, rings = lax.optimization_barrier((products, rings))
     tri_in = exchange(products.reshape(128, 40, 128), ALL)
     share_len = seq_len // 8
     token_share = lax.dynamic_slice_in_dim(tokens, col_index * share_len, share_len, 1)
-    tri_in, recv, token_share = lax.optimization_barrier((tri_in, recv, token_share))
-
-    gate = jax.nn.sigmoid(matmul(normed, gate_out))
+    gate = jax.nn.sigmoid(matmul(normed, gate_out)).reshape(pair_state.shape)
     heads_first = jnp.transpose(bias_proj.T.reshape(8, 2, 128), (1, 0, 2)).reshape(16, 128)
-    pair_out, bias = call(
-        update_kernel,
-        (jax.ShapeDtypeStruct(pair_state.shape, F32), jax.ShapeDtypeStruct((8, 16, 40, 128), BF16)),
+    tri_gain = jnp.broadcast_to(norm_tri.astype(F32)[:, None], (128, 128))
+    bias_gain = norm_bias.astype(F32)[None]
+    ff_gain = norm_ff.astype(F32)[None]
+    triple = jnp.concatenate([heads_first] * 3, axis=0)
+    chain_row, chain_col = chain_ids[:, None], column_order(chain_ids[None], 1)
+    (
+        tri_in, recv, token_share, gate, heads_first, tri_gain, bias_gain, ff_gain, triple, chain_row, chain_col
+    ) = lax.optimization_barrier(
         (
-            tri_in,
-            pair_state,
-            gate.reshape(pair_state.shape),
-            tri_out,
-            jnp.broadcast_to(norm_tri.astype(F32)[:, None], (128, 128)),
-            norm_bias.astype(F32)[None],
-            heads_first,
-        ),
-        [
-            pltpu.VMEM((128 * 40, 128), F32),
-            pltpu.VMEM((16 * 40, 128), F32),
-            pltpu.VMEM((128, 40, 128), BF16),
-            pltpu.VMEM(pair_state.shape, BF16),
-            pltpu.VMEM(pair_state.shape, F32),
-            pltpu.VMEM(pair_state.shape, F32),
-            pltpu.VMEM((16, 40, 128), BF16),
-            pltpu.SemaphoreType.DMA((4,)),
-            pltpu.SemaphoreType.DMA((2,)),
-            pltpu.SemaphoreType.DMA((10,)),
-        ],
-        "update",
-        flops=2 * 128 * 128 * 5120,
-        nbytes=9_000_000,
-        spaces=[hbm, hbm, hbm] + [vmem] * 4,
-        out_specs=(hbm, hbm),
-    )
-    bias_in = exchange(bias.reshape(128, 40, 128), ALL).reshape(16, 8, 40, 128)
-
-    pair_scratch = pltpu.VMEM((2 * samples, 2, seq_len, 128), BF16)
-    mixed, full_bias, stats = call(
-        forward_kernel,
-        (
-            jax.ShapeDtypeStruct((16, samples, 48, 128), BF16),
-            jax.ShapeDtypeStruct((seq_len, seq_len), F32),
-            jax.ShapeDtypeStruct((seq_len, 128), F32),
-        ),
-        (
-            bias_in, keep, recv, chain_ids[:, None], column_order(chain_ids[None], 1), place, chain_weight,
-        ),
-        [
-            pair_scratch,
-            pltpu.VMEM((16, 8, 40, 128), BF16),
-            pltpu.VMEM((16, samples, 48, 128), BF16),
-            pltpu.VMEM((seq_len, seq_len), F32),
-            pltpu.VMEM((seq_len, 128), F32),
-            pltpu.SemaphoreType.DMA((2,)),
-            pltpu.SemaphoreType.DMA((2,)),
-            pltpu.SemaphoreType.DMA((4,)),
-        ],
-        "forward",
-        flops=6 * 4 * 768 * 768 * 128,
-        nbytes=12_000_000,
-        spaces=[hbm, hbm, hbm, vmem, vmem, smem, smem],
-        out_specs=(hbm, hbm, hbm),
+            tri_in, recv, token_share, gate, heads_first, tri_gain, bias_gain, ff_gain, triple, chain_row, chain_col
+        )
+    )
+
+    pair_out, bias = run_update(
+        tri_in,
+        pair_state,
+        gate,
+        tri_out,
+        tri_gain,
+        bias_gain,
+        heads_first,
+    )
+    bias_in = exchange(bias.reshape(128, 40, 128), ALL).reshape(PACKED)
+
+    bias_in, rings = lax.optimization_barrier((bias_in, rings))
+    far_rings = lax.ppermute(rings, "core", SWAP)
+
+    mixed, full_bias, stats = run_forward(
+        bias_in, keep, recv, chain_row, chain_col, place, chain_weight
     )
     mixed_in = exchange(mixed, ("core",) + COLS)
-    bias_grad = call(
-        backward_kernel,
-        jax.ShapeDtypeStruct((16, 8, 40, 128), BF16),
-        (full_bias, stats, keep, recv),
-        [
-            pair_scratch,
-            pltpu.VMEM((seq_len, seq_len), F32),
-            pltpu.VMEM((seq_len, 128), F32),
-            pltpu.VMEM((16, 8, 40, 128), BF16),
-            pltpu.SemaphoreType.DMA((2,)),
-            pltpu.SemaphoreType.DMA((2,)),
-            pltpu.SemaphoreType.DMA((768 // BACKWARD_ROWS,)),
-        ],
-        "backward",
-        flops=6 * 4 * 768 * 768 * 128,
-        nbytes=12_000_000,
-        spaces=[hbm] * 4,
-        out_specs=hbm,
-    )
+    bias_grad = run_backward(full_bias, stats, keep, recv)
     grad_in = exchange(bias_grad.reshape(128, 40, 128), ALL).reshape(8, 16, 40, 128)
 
-    mixed_rows = jnp.concatenate([mixed_in[..., 0:HD], mixed_in[..., 64 : 64 + HD]], axis=2)
-    mixed_rows = jnp.transpose(mixed_rows.reshape(2, 8, samples, share_len, HD), (2, 3, 1, 0, 4))
-    attn = matmul(mixed_rows.reshape(samples * share_len, model_width), w_out_all)
-    state = token_share.reshape(samples * share_len, model_width).astype(F32) + attn
-    ff_in = layer_norm(state, norm_ff).astype(BF16)
-    hidden = (jax.nn.silu(matmul(ff_in, ff_gate)) * matmul(ff_in, ff_up)).astype(BF16)
-    refined = (state + matmul(hidden, ff_down)).reshape(samples, share_len, model_width)
-
-    pair_grad = call(
-        pair_grad_kernel,
-        jax.ShapeDtypeStruct(pair_state.shape, F32),
-        (grad_in, jnp.concatenate([heads_first] * 3, axis=0)),
-        [
-            pltpu.VMEM((16 * 40, 128), F32),
-            pltpu.VMEM((8, 16, 40, 128), BF16),
-            pltpu.VMEM(pair_state.shape, F32),
-            pltpu.SemaphoreType.DMA((8,)),
-            pltpu.SemaphoreType.DMA((2,)),
-        ],
-        "pair_grad",
-        flops=2 * 48 * 128 * 5120,
-        nbytes=4_000_000,
-        spaces=[hbm, vmem],
-        out_specs=hbm,
-    )
+    refined = run_transition(
+        mixed_in, rings, far_rings, place, token_share, ff_gain, ff_gate, ff_up, ff_down
+    )
+
+    pair_grad = run_pair_grad(grad_in, triple)
     return (pair_out, refined, pair_grad)
 
 

time: 203 us -> 184 us (0.906)
  between operations: 14.3 us -> 1.15 us
  starting transfers between devices: 36.4 us -> 47.3 us
  matrix products: 13.7 us -> 3.54 us
  local copies, waits for them, and re-layouts: 11.9 us -> 7.2 us
  other arithmetic: 4.18 us -> 1.27 us
    ppermute x1 -> x6, waiting for transfers between devices: 0.01 us -> 13.4 us  [the longest x3 10.7 us: gather_ring(): lax.ppermute(half, 'z', [(i, (i - k) % 4) for i in range(4)])]
    all_to_all x5, waiting for transfers between devices: 57.5 us -> 45.6 us  [exchange(): return lax.all_to_all(value, axes, 0, 0, tiled=True)]
    ppermute x1 -> x6, starting transfers between devices: 1.21 us -> 12 us  [the longest x3 6.03 us: gather_ring(): lax.ppermute(half, 'z', [(i, (i - k) % 4) for i in range(4)])]
    dot_general x4 -> x1, matrix products: 13.7 us -> 3.54 us  [matmul(): return jnp.dot(left_side, right_side, preferred_element_type=F32)]
    reshape x2 -> x0, local copies, waits for them, and re-layouts: 3.56 us -> none  [the longest x1 2.1 us: body(): mixed_rows.reshape(samples * share_len, model_width)]
    unnamed x31 -> x39, local copies, waits for them, and re-layouts: 3.12 us -> 4.34 us
    pallas_call x7 -> x8, Pallas kernels: 63.9 us -> 63.6 us  [call(): pl.pallas_call(kernel, out_shape=outs, in_specs=spaces or [vmem] * len(ar...]
  transfers between devices with their start and end apart: 7 -> 11, of which waited for: 5 -> 8; matrix products, arithmetic and copies ran while one was open for 13% -> 4% of each run, Pallas kernels for 16% -> 20%
where the time goes in v3:
time: 184 us; the launch traced here: 183 us
  Pallas kernels  63.6 us (35%)
  waiting for transfers between devices  59 us (32%)
  starting transfers between devices  47.3 us (26%)
  local copies, waits for them, and re-layouts  7.2 us (4%)
  matrix products  3.54 us (2%)
    pallas_call x8, Pallas kernels, call(): pl.pallas_call(kernel, out_shape=outs, in_specs=spaces or [vmem] * len(ar...  63.6 us
    all_to_all x5, waiting for transfers between devices, exchange(): return lax.all_to_all(value, axes, 0, 0, tiled=True)  45.6 us
    all_to_all x5, starting transfers between devices, exchange(): return lax.all_to_all(value, axes, 0, 0, tiled=True)  35.3 us
    ppermute x3, waiting for transfers between devices, gather_ring(): lax.ppermute(half, 'z', [(i, (i - k) % 4) for i in range(4)])  10.7 us
    ppermute x3, starting transfers between devices, gather_ring(): lax.ppermute(half, 'z', [(i, (i - k) % 4) for i in range(4)])  6.03 us
    unnamed x39, local copies, waits for them, and re-layouts  4.34 us
  transfers between devices with their start and end apart: 11, of which 8 were waited for; matrix products, arithmetic and copies ran while one was open for 4% of the time, Pallas kernels for 20%

profile of v3, /device:TPU:1, one launch (start us, length us, event | category | flops | bytes accessed | tf_op | source)
XLA Modules:
  0.0 183.0 jit_solution(2101907327304240990)
XLA Ops:
  0.6 0.0 copy-start
  0.7 1.2 bitcast_convert_fusion.1.gain_ref
  1.8 0.6 stack.42.place_ref
  2.5 7.7 %project.1 = (bf16[128,72,128]{2,1,0:T(8,128)(2,1)}, bf16[4608,128]{1,0:T(8,128)(2,1)}) custom-call(bf16[4608,128]{1,0:T(8,128)(2,1)} %bitcast.39, f32[1,128]{1,0:T(1,128)} %bitcast_convert_fusion.1.gain_ref, bf16[128,128]{1,0:T(8,128)(2,1)} %pl_hbm.1, bf16[128,128]{1,0:T(8,128)(2,1)} %pr_hbm.1, bf16[128,128]{1,0:T(8,128)(2,1)} %gl_hbm.1, ...), custom_call_target="tpu_custom_call" | custom-call | flops 805306368 | bytes 5000000 | tf_op jit(solution)/shard_map/project/pallas_call | solution.py:53
  10.2 0.0 copy-start.9
  10.2 0.0 copy-start.10
  10.2 0.0 copy-start.11
  10.2 0.0 copy-start.14
  10.2 11.5 %all-to-all-start = ((bf16[128,72,128]{2,1,0:T(8,128)(2,1)}), bf16[128,72,128]{2,1,0:T(8,128)(2,1)S(1)}, u32[]{:S(2)}, u32[]{:S(2)}) async-start(bf16[128,72,128]{2,1,0:T(8,128)(2,1)} %get-tuple-element.34), calls=%async_computation | async-start | bytes 4718592 | tf_op jit(solution)/shard_map/all_to_all | solution.py:798
  21.7 0.0 copy-done.9
  21.8 0.8 copy.32.wq_ref
  22.6 0.8 copy.33.wk_ref
  23.4 0.8 copy.34.wv_ref
  24.2 0.0 copy-done.14
  24.2 0.6 reshape.56.gain_ref
  24.8 13.3 %tokens.1 = (bf16[3,2,768,128]{3,2,1,0:T(8,128)(2,1)}, bf16[3,2,768,128]{3,2,1,0:T(8,128)(2,1)}) custom-call(bf16[3,768,768]{2,1,0:T(8,128)(2,1)} %tokens_ref.1, bf16[3,768,768]{2,1,0:T(8,128)(2,1)} %grad_ref.1, f32[1,768]{1,0:T(1,128)} %reshape.56.gain_ref, bf16[768,96]{1,0:T(8,128)(2,1)} %copy.32.wq_ref, bf16[768,96]{1,0:T(8,128)(2,1)} %copy.33.wk_ref, ...), custom_call_target="tpu_custom_call" | custom-call | flops 1811939328 | bytes 12000000 | tf_op jit(solution)/shard_map/tokens/pallas_call | solution.py:53
  38.1 3.4 %collective-permute-start.1 = (bf16[48,768]{1,0:T(8,128)(2,1)S(1)}, bf16[48,768]{1,0:T(8,128)(2,1)S(1)}, u32[]{:S(2)}, u32[]{:S(2)}) collective-permute-start(bf16[48,768]{1,0:T(8,128)(2,1)S(1)} %constant_dynamic-slice_fusion.1), channel_id=1, source_target_pairs={{0,2},{1,3},{2,0},{3,1},{4,6},{5,7},{6,4},{7,5},{8,10},{9,11},{10,... | collective-permute-start | bytes 221192 | tf_op jit(solution)/shard_map/ppermute | solution.py:805
  41.5 0.6 collective-permute-start.2
  42.0 2.1 %collective-permute-start = (bf16[48,768]{1,0:T(8,128)(2,1)S(1)}, bf16[48,768]{1,0:T(8,128)(2,1)S(1)}, u32[]{:S(2)}, u32[]{:S(2)}) collective-permute-start(bf16[48,768]{1,0:T(8,128)(2,1)S(1)} %constant_dynamic-slice_fusion.1), channel_id=1, source_target_pairs={{0,3},{1,0},{2,1},{3,2},{4,7},{5,4},{6,5},{7,6},{8,11},{9,8},{10,9... | collective-permute-start | bytes 221192 | tf_op jit(solution)/shard_map/ppermute | solution.py:805
  44.1 9.4 %collective-permute-done.1 = bf16[48,768]{1,0:T(8,128)(2,1)S(1)} collective-permute-done((bf16[48,768]{1,0:T(8,128)(2,1)S(1)}, bf16[48,768]{1,0:T(8,128)(2,1)S(1)}, u32[]{:S(2)}, u32[]{:S(2)}) %collective-permute-start.1) | collective-permute-done | bytes 73760 | tf_op jit(solution)/shard_map/ppermute | solution.py:805
  53.5 1.3 collective-permute-done.2
  54.8 0.0 collective-permute-done
  54.9 0.0 all-to-all-done
  54.9 3.5 %collective-permute-start.3 = (bf16[4,48,768]{2,1,0:T(8,128)(2,1)S(1)}, bf16[4,48,768]{2,1,0:T(8,128)(2,1)S(1)}, u32[]{:S(2)}, u32[]{:S(2)}) collective-permute-start(bf16[4,48,768]{2,1,0:T(8,128)(2,1)S(1)} %pad_maximum_fusion.1), channel_id=1, source_target_pairs={{0,4},{4,0},{1,5},{5,1},{2,6},{6,2},{3,7},{7,3},{8,12},{12,8},{9,1... | collective-permute-start | bytes 884744 | tf_op jit(solution)/shard_map/ppermute | solution.py:862
  58.3 4.6 %product.1 = bf16[16,8,40,128]{3,2,1,0:T(8,128)(2,1)S(1)} custom-call(bf16[16,8,72,128]{3,2,1,0:T(8,128)(2,1)S(1)} %bitcast.36), custom_call_target="tpu_custom_call" | custom-call | flops 905969664 | bytes 4000000 | tf_op jit(solution)/shard_map/product/pallas_call | solution.py:53
  62.9 0.0 copy-start.1
  62.9 1.0 copy-done.1
  64.0 1.1 collective-permute-done.3
  65.1 0.1 pad_maximum_fusion.ring_hbm
  65.1 8.0 %all-to-all-start.1 = ((bf16[128,40,128]{2,1,0:T(8,128)(2,1)}), bf16[128,40,128]{2,1,0:T(8,128)(2,1)}, u32[]{:S(2)}, u32[]{:S(2)}) async-start(bf16[128,40,128]{2,1,0:T(8,128)(2,1)} %bitcast.37), calls=%async_computation.1 | async-start | bytes 2621440 | tf_op jit(solution)/shard_map/all_to_all | solution.py:798
  73.1 1.4 collective-permute-start.4
  74.5 0.0 copy-done.12
  74.5 0.1 reshape_broadcast_in_dim.3
  74.6 0.1 slice.7
  74.6 0.1 reshape.50
  74.7 0.1 reshape.49
  74.8 1.1 constant_dynamic-slice_fusion.token_hbm
  75.9 0.0 copy-done
  75.9 0.0 copy-start.16
  75.9 0.0 copy-start.2
  76.0 0.0 copy-start.3
  76.0 3.5 %fusion.2 = f32[4608,128]{1,0:T(8,128)} fusion(bf16[4608,128]{1,0:T(8,128)(2,1)} %get-tuple-element.44, bf16[128,128]{1,0:T(8,128)(2,1)S(1)} %copy-done), kind=kOutput, calls=%fused_computation.3 | convolution fusion | flops 152764416 | bytes 3571712 | tf_op jit(solution)/shard_map/dot_general | solution.py:31
  79.5 0.0 collective-permute-done.4.recv_hbm
  79.5 13.7 %all-to-all-done.1.t_hbm = bf16[128,40,128]{2,1,0:T(8,128)(2,1)} async-done(((bf16[128,40,128]{2,1,0:T(8,128)(2,1)}), bf16[128,40,128]{2,1,0:T(8,128)(2,1)}, u32[]{:S(2)}, u32[]{:S(2)}) %all-to-all-start.1) | async-done | bytes 1310752 | tf_op jit(solution)/shard_map/all_to_all | solution.py:798
  93.2 0.0 copy-done.16
  93.2 0.1 broadcast_in_dim.35.tri_gain_ref
  93.3 0.0 copy-done.2
  93.3 6.4 %update.1 = (f32[48,96,128]{2,1,0:T(8,128)}, bf16[8,16,40,128]{3,2,1,0:T(8,128)(2,1)}) custom-call(bf16[128,40,128]{2,1,0:T(8,128)(2,1)} %all-to-all-done.1.t_hbm, bf16[48,96,128]{2,1,0:T(8,128)(2,1)S(1)} %copy-done.2, f32[48,96,128]{2,1,0:T(8,128)} %bitcast.42, bf16[128,128]{1,0:T(8,128)(2,1)S(1)} %copy-done.3, ...), custom_call_target="tpu_custom_call" | custom-call | flops 167772160 | bytes 9000000 | tf_op jit(solution)/shard_map/update/pallas_call | solution.py:53
  99.8 0.0 copy-start.6
  99.8 6.1 %all-to-all-start.2 = ((bf16[128,40,128]{2,1,0:T(8,128)(2,1)}), bf16[128,40,128]{2,1,0:T(8,128)(2,1)}, u32[]{:S(2)}, u32[]{:S(2)}) async-start(bf16[128,40,128]{2,1,0:T(8,128)(2,1)} %bitcast.44), calls=%async_computation.2 | async-start | bytes 2621440 | tf_op jit(solution)/shard_map/all_to_all | solution.py:798
  105.9 0.2 copy.36.chain_row_ref
  106.1 19.9 %all-to-all-done.2 = bf16[128,40,128]{2,1,0:T(8,128)(2,1)} async-done(((bf16[128,40,128]{2,1,0:T(8,128)(2,1)}), bf16[128,40,128]{2,1,0:T(8,128)(2,1)}, u32[]{:S(2)}, u32[]{:S(2)}) %all-to-all-start.2) | async-done | bytes 1310752 | tf_op jit(solution)/shard_map/all_to_all | solution.py:798
  126.0 0.0 copy-done.4
  126.0 9.1 %forward.1 = (bf16[16,3,48,128]{3,2,1,0:T(8,128)(2,1)}, f32[768,768]{1,0:T(8,128)}, f32[768,128]{1,0:T(8,128)S(1)}) custom-call(bf16[16,8,40,128]{3,2,1,0:T(8,128)(2,1)} %bitcast.22.bias_hbm, bf16[3,2,768,128]{3,2,1,0:T(8,128)(2,1)S(1)} %copy-done.5, bf16[3,2,768,128]{3,2,1,0:T(8,128)(2,1)} %collective-permute-done.4.recv_hbm, ...), custom_call_target="tpu_custom_call" | custom-call | flops 1811939328 | bytes 12000000 | tf_op jit(solution)/shard_map/forward/pallas_call | solution.py:53
  135.1 0.8 copy-done.7
  135.9 5.1 %all-to-all-start.3 = ((bf16[16,3,48,128]{3,2,1,0:T(8,128)(2,1)}), bf16[16,3,48,128]{3,2,1,0:T(8,128)(2,1)S(1)}, u32[]{:S(2)}, u32[]{:S(2)}) async-start(bf16[16,3,48,128]{3,2,1,0:T(8,128)(2,1)} %get-tuple-element.58), calls=%async_computation.3 | async-start | bytes 1179648 | tf_op jit(solution)/shard_map/all_to_all | solution.py:798
  141.0 9.0 %backward.1 = bf16[16,8,40,128]{3,2,1,0:T(8,128)(2,1)} custom-call(f32[768,768]{1,0:T(8,128)} %get-tuple-element.62.full_hbm, f32[768,128]{1,0:T(8,128)} %copy-done.7, bf16[3,2,768,128]{3,2,1,0:T(8,128)(2,1)} %get-tuple-element.54.keep_hbm, bf16[3,2,768,128]{3,2,1,0:T(8,128)(2,1)} %collective-permute-done.4.recv_hbm), custom_call_target="tpu_custom_call" | custom-call | flops 1811939328 | bytes 12000000 | tf_op jit(solution)/shard_map/backward/pallas_call | solution.py:53
  149.9 3.8 %all-to-all-done.3.mixed_hbm = bf16[16,3,48,128]{3,2,1,0:T(8,128)(2,1)S(1)} async-done(((bf16[16,3,48,128]{3,2,1,0:T(8,128)(2,1)}), bf16[16,3,48,128]{3,2,1,0:T(8,128)(2,1)S(1)}, u32[]{:S(2)}, u32[]{:S(2)}) %all-to-all-start.3) | async-done | bytes 589856 | tf_op jit(solution)/shard_map/all_to_all | solution.py:798
  153.7 4.6 %all-to-all-start.4 = ((bf16[128,40,128]{2,1,0:T(8,128)(2,1)}), bf16[128,40,128]{2,1,0:T(8,128)(2,1)S(1)}, u32[]{:S(2)}, u32[]{:S(2)}) async-start(bf16[128,40,128]{2,1,0:T(8,128)(2,1)} %bitcast.43), calls=%async_computation.4 | async-start | bytes 2621440 | tf_op jit(solution)/shard_map/all_to_all | solution.py:798
  158.4 1.1 collective-permute-start.5
  159.5 1.6 collective-permute-done.5.far_hbm
  161.1 9.5 %transition.1 = f32[3,96,768]{2,1,0:T(8,128)} custom-call(bf16[16,3,48,128]{3,2,1,0:T(8,128)(2,1)S(1)} %all-to-all-done.3.mixed_hbm, bf16[8,48,768]{2,1,0:T(8,128)(2,1)S(1)} %pad_maximum_fusion.ring_hbm, bf16[8,48,768]{2,1,0:T(8,128)(2,1)S(1)} %collective-permute-done.5.far_hbm, s32[6]{0:T(128)S(1)} %copy-done.4, ...), custom_call_target="tpu_custom_call" | custom-call | flops 2491416576 | bytes 12000000 | tf_op jit(solution)/shard_map/transition/pallas_call | solution.py:53
  170.6 8.2 %all-to-all-done.4 = bf16[128,40,128]{2,1,0:T(8,128)(2,1)S(1)} async-done(((bf16[128,40,128]{2,1,0:T(8,128)(2,1)}), bf16[128,40,128]{2,1,0:T(8,128)(2,1)S(1)}, u32[]{:S(2)}, u32[]{:S(2)}) %all-to-all-start.4) | async-done | bytes 1310752 | tf_op jit(solution)/shard_map/all_to_all | solution.py:798
  178.8 4.1 %pair_grad.1 = f32[48,96,128]{2,1,0:T(8,128)} custom-call(bf16[8,16,40,128]{3,2,1,0:T(8,128)(2,1)S(1)} %bitcast.38, bf16[48,128]{1,0:T(8,128)(2,1)S(1)} %pad_maximum_fusion.2.w_ref), custom_call_target="tpu_custom_call" | custom-call | flops 62914560 | bytes 4000000 | tf_op jit(solution)/shard_map/pair_grad/pallas_call | solution.py:53
  (26 shorter events, 0.1 us)
Async XLA Ops:
  0.6 75.3 %copy-start = (bf16[128,128]{1,0:T(8,128)(2,1)S(1)}, bf16[128,128]{1,0:T(8,128)(2,1)}, u32[]{:S(2)}) copy-start(bf16[128,128]{1,0:T(8,128)(2,1)} %param.35) | copy-start | bytes 98308
  10.2 11.6 %copy-start.9 = (bf16[768,96]{0,1:T(8,128)(2,1)S(1)}, bf16[768,96]{0,1:T(8,128)(2,1)}, u32[]{:S(2)}) copy-start(bf16[768,96]{0,1:T(8,128)(2,1)} %param.42) | copy-start | bytes 442372
  10.2 12.4 %copy-start.10 = (bf16[768,96]{0,1:T(8,128)(2,1)S(1)}, bf16[768,96]{0,1:T(8,128)(2,1)}, u32[]{:S(2)}) copy-start(bf16[768,96]{0,1:T(8,128)(2,1)} %param.43) | copy-start | bytes 442372
  10.2 13.2 %copy-start.11 = (bf16[768,96]{0,1:T(8,128)(2,1)S(1)}, bf16[768,96]{0,1:T(8,128)(2,1)}, u32[]{:S(2)}) copy-start(bf16[768,96]{0,1:T(8,128)(2,1)} %param.44) | copy-start | bytes 442372
  10.2 14.0 %copy-start.14 = (bf16[768]{0:T(1024)(128)(2,1)S(1)}, bf16[768]{0:T(1024)(128)(2,1)}, u32[]{:S(2)}) copy-start(bf16[768]{0:T(1024)(128)(2,1)} %param.41) | copy-start | bytes 4612
  10.2 44.6 %all-to-all-start = ((bf16[128,72,128]{2,1,0:T(8,128)(2,1)}), bf16[128,72,128]{2,1,0:T(8,128)(2,1)S(1)}, u32[]{:S(2)}, u32[]{:S(2)}) async-start(bf16[128,72,128]{2,1,0:T(8,128)(2,1)} %get-tuple-element.34), calls=%async_computation | async-start | bytes 4718592 | tf_op jit(solution)/shard_map/all_to_all | solution.py:798
  24.8 13.3 %copy-start.8 = (bf16[96,768]{1,0:T(8,128)(2,1)S(1)}, bf16[96,768]{1,0:T(8,128)(2,1)}, u32[]{:S(2)}) copy-start(bf16[96,768]{1,0:T(8,128)(2,1)} %wo_ref.1) | copy-start | bytes 442372
  38.1 15.4 %collective-permute-start.1 = (bf16[48,768]{1,0:T(8,128)(2,1)S(1)}, bf16[48,768]{1,0:T(8,128)(2,1)S(1)}, u32[]{:S(2)}, u32[]{:S(2)}) collective-permute-start(bf16[48,768]{1,0:T(8,128)(2,1)S(1)} %constant_dynamic-slice_fusion.1), channel_id=1, source_target_pairs={{0,2},{1,3},{2,0},{3,1},{4,6},{5,7},{6,4},{7,5},{8,10},{9,11},{10,... | collective-permute-start | bytes 221192 | tf_op jit(solution)/shard_map/ppermute | solution.py:805
  41.5 13.4 %collective-permute-start.2 = (bf16[48,768]{1,0:T(8,128)(2,1)S(1)}, bf16[48,768]{1,0:T(8,128)(2,1)S(1)}, u32[]{:S(2)}, u32[]{:S(2)}) collective-permute-start(bf16[48,768]{1,0:T(8,128)(2,1)S(1)} %constant_dynamic-slice_fusion.1), channel_id=1, source_target_pairs={{0,1},{1,2},{2,3},{3,0},{4,5},{5,6},{6,7},{7,4},{8,9},{9,10},{10,1... | collective-permute-start | bytes 221192 | tf_op jit(solution)/shard_map/ppermute | solution.py:805
  42.0 12.8 %collective-permute-start = (bf16[48,768]{1,0:T(8,128)(2,1)S(1)}, bf16[48,768]{1,0:T(8,128)(2,1)S(1)}, u32[]{:S(2)}, u32[]{:S(2)}) collective-permute-start(bf16[48,768]{1,0:T(8,128)(2,1)S(1)} %constant_dynamic-slice_fusion.1), channel_id=1, source_target_pairs={{0,3},{1,0},{2,1},{3,2},{4,7},{5,4},{6,5},{7,6},{8,11},{9,8},{10,9... | collective-permute-start | bytes 221192 | tf_op jit(solution)/shard_map/ppermute | solution.py:805
  54.9 10.2 %collective-permute-start.3 = (bf16[4,48,768]{2,1,0:T(8,128)(2,1)S(1)}, bf16[4,48,768]{2,1,0:T(8,128)(2,1)S(1)}, u32[]{:S(2)}, u32[]{:S(2)}) collective-permute-start(bf16[4,48,768]{2,1,0:T(8,128)(2,1)S(1)} %pad_maximum_fusion.1), channel_id=1, source_target_pairs={{0,4},{4,0},{1,5},{5,1},{2,6},{6,2},{3,7},{7,3},{8,12},{12,8},{9,1... | collective-permute-start | bytes 884744 | tf_op jit(solution)/shard_map/ppermute | solution.py:862
  62.9 1.1 copy-start.1
  64.0 10.5 %copy-start.12 = (s32[768]{0:T(1024)S(1)}, s32[768]{0:T(1024)}, u32[]{:S(2)}) copy-start(s32[768]{0:T(1024)} %param.27) | copy-start | bytes 9220
  64.0 10.8 %copy-start.13 = (bf16[128,16]{0,1:T(8,128)(2,1)S(1)}, bf16[128,16]{0,1:T(8,128)(2,1)}, u32[]{:S(2)}) copy-start(bf16[128,16]{0,1:T(8,128)(2,1)} %param.39) | copy-start | bytes 12292
  64.0 10.8 %copy-start.15 = (bf16[768]{0:T(1024)(128)(2,1)S(1)}, bf16[768]{0:T(1024)(128)(2,1)}, u32[]{:S(2)}) copy-start(bf16[768]{0:T(1024)(128)(2,1)} %param.46) | copy-start | bytes 4612
  64.0 11.9 %copy-start.17 = (bf16[128]{0:T(256)(128)(2,1)S(1)}, bf16[128]{0:T(256)(128)(2,1)}, u32[]{:S(2)}) copy-start(bf16[128]{0:T(256)(128)(2,1)} %param.38) | copy-start | bytes 772
  65.1 28.1 %all-to-all-start.1 = ((bf16[128,40,128]{2,1,0:T(8,128)(2,1)}), bf16[128,40,128]{2,1,0:T(8,128)(2,1)}, u32[]{:S(2)}, u32[]{:S(2)}) async-start(bf16[128,40,128]{2,1,0:T(8,128)(2,1)} %bitcast.37), calls=%async_computation.1 | async-start | bytes 2621440 | tf_op jit(solution)/shard_map/all_to_all | solution.py:798
  73.1 6.4 %collective-permute-start.4 = (bf16[3,2,768,128]{3,2,1,0:T(8,128)(2,1)}, bf16[3,2,768,128]{3,2,1,0:T(8,128)(2,1)}, u32[]{:S(2)}, u32[]{:S(2)}) collective-permute-start(bf16[3,2,768,128]{3,2,1,0:T(8,128)(2,1)} %get-tuple-element.43), channel_id=1, source_target_pairs={{0,8},{8,0},{1,9},{9,1},{2,10},{10,2},{3,11},{11,3},{4,12},{12,4},... | collective-permute-start | bytes 3538952 | tf_op jit(solution)/shard_map/ppermute | solution.py:860
  75.9 17.3 %copy-start.16 = (bf16[128]{0:T(256)(128)(2,1)S(1)}, bf16[128]{0:T(256)(128)(2,1)}, u32[]{:S(2)}) copy-start(bf16[128]{0:T(256)(128)(2,1)} %param.36) | copy-start | bytes 772
  75.9 17.4 %copy-start.2 = (bf16[48,96,128]{2,1,0:T(8,128)(2,1)S(1)}, bf16[48,96,128]{2,1,0:T(8,128)(2,1)}, u32[]{:S(2)}) copy-start(bf16[48,96,128]{2,1,0:T(8,128)(2,1)} %pair_hbm.1) | copy-start | bytes 3538948
  76.0 17.4 %copy-start.3 = (bf16[128,128]{1,0:T(8,128)(2,1)S(1)}, bf16[128,128]{1,0:T(8,128)(2,1)}, u32[]{:S(2)}) copy-start(bf16[128,128]{1,0:T(8,128)(2,1)} %w_ref.1) | copy-start | bytes 98308
  99.8 26.2 %copy-start.4 = (s32[6]{0:T(128)S(1)}, s32[6]{0:T(128)}, u32[]{:S(2)}) copy-start(s32[6]{0:T(128)} %stack.42.place_ref) | copy-start | bytes 76
  99.8 26.2 %copy-start.5 = (bf16[3,2,768,128]{3,2,1,0:T(8,128)(2,1)S(1)}, bf16[3,2,768,128]{3,2,1,0:T(8,128)(2,1)}, u32[]{:S(2)}) copy-start(bf16[3,2,768,128]{3,2,1,0:T(8,128)(2,1)} %get-tuple-element.54.keep_hbm) | copy-start | bytes 3538948
  99.8 26.2 %copy-start.6 = (f32[16]{0:T(128)S(1)}, f32[16]{0:T(128)}, u32[]{:S(2)}) copy-start(f32[16]{0:T(128)} %weight_ref.1) | copy-start | bytes 196
  99.8 26.2 %all-to-all-start.2 = ((bf16[128,40,128]{2,1,0:T(8,128)(2,1)}), bf16[128,40,128]{2,1,0:T(8,128)(2,1)}, u32[]{:S(2)}, u32[]{:S(2)}) async-start(bf16[128,40,128]{2,1,0:T(8,128)(2,1)} %bitcast.44), calls=%async_computation.2 | async-start | bytes 2621440 | tf_op jit(solution)/shard_map/all_to_all | solution.py:798
  135.1 0.8 copy-start.7
  135.9 17.9 %all-to-all-start.3 = ((bf16[16,3,48,128]{3,2,1,0:T(8,128)(2,1)}), bf16[16,3,48,128]{3,2,1,0:T(8,128)(2,1)S(1)}, u32[]{:S(2)}, u32[]{:S(2)}) async-start(bf16[16,3,48,128]{3,2,1,0:T(8,128)(2,1)} %get-tuple-element.58), calls=%async_computation.3 | async-start | bytes 1179648 | tf_op jit(solution)/shard_map/all_to_all | solution.py:798
  153.7 25.1 %all-to-all-start.4 = ((bf16[128,40,128]{2,1,0:T(8,128)(2,1)}), bf16[128,40,128]{2,1,0:T(8,128)(2,1)S(1)}, u32[]{:S(2)}, u32[]{:S(2)}) async-start(bf16[128,40,128]{2,1,0:T(8,128)(2,1)} %bitcast.43), calls=%async_computation.4 | async-start | bytes 2621440 | tf_op jit(solution)/shard_map/all_to_all | solution.py:798
  158.4 2.8 %collective-permute-start.5 = (bf16[8,48,768]{2,1,0:T(8,128)(2,1)S(1)}, bf16[8,48,768]{2,1,0:T(8,128)(2,1)S(1)}, u32[]{:S(2)}, u32[]{:S(2)}) collective-permute-start(bf16[8,48,768]{2,1,0:T(8,128)(2,1)S(1)} %pad_maximum_fusion.ring_hbm), channel_id=1, source_target_pairs={{0,8},{8,0},{1,9},{9,1},{2,10},{10,2},{3,11},{11,3},{4,12},{12,4},... | collective-permute-start | bytes 1769480 | tf_op jit(solution)/shard_map/ppermute | solution.py:894

commit v4 on v3

--- a/solution.py
+++ b/solution.py
@@ -15,10 +15,9 @@
 LOG2E = 1.4426950408889634
 SCALE = HD ** (-0.5) * LOG2E
 FORWARD_ROWS = 768
-PROJECT_PAR = 12
 UPDATE_PAR = 12
 THIN_PAR = 16
-BACKWARD_ROWS = 192
+BACKWARD_ROWS = 384
 
 
 def layer_norm(value_rows, gain_vec):
@@ -56,7 +55,7 @@
         in_specs=spaces or [vmem] * len(args),
         out_specs=out_specs or jax.tree.map(lambda _: vmem, outs),
         scratch_shapes=scratch,
-        compiler_params=pltpu.CompilerParams(vmem_limit_bytes=mib * 1024 * 1024),
+        compiler_params=pltpu.CompilerParams(vmem_limit_bytes=int(mib * 1024 * 1024)),
         cost_estimate=pl.CostEstimate(flops=flops, bytes_accessed=nbytes, transcendentals=0),
         name=name,
         **({} if grid is None else {"grid": grid}),
@@ -75,10 +74,10 @@
 
 
 def project_kernel(
-    pair_hbm, gain_ref, pl_hbm, pr_hbm, gl_hbm, gr_hbm, mask_hbm, place_ref, out_hbm, normed_hbm,
+    pair_hbm, gain_ref, pl_hbm, pr_hbm, gl_hbm, gr_hbm, mask_hbm, out_hbm, normed_hbm,
     scr, pair_ref, normed_ref, w_ref, out_ref, mask_ref, pair_sems, w_sems, out_sems,
 ):
-    blocks = [pl.ds(512 * n, 512) for n in range(9)]
+    blocks = [pl.ds(2304 * (n % 2) + 576 * (n // 2), 576) for n in range(8)]
     pair_copies = start_all(
         [pltpu.make_async_copy(pair_hbm.at[b], pair_ref.at[b], pair_sems.at[n]) for n, b in enumerate(blocks)]
     )
@@ -89,18 +88,23 @@
         ]
         + [pltpu.make_async_copy(mask_hbm, mask_ref, w_sems.at[4])]
     )
-    gain = gain_ref[...]
+    gain = gain_ref[...].astype(F32).reshape(1, 128)
     normed_copies = []
-    for n, block in enumerate(blocks):
+
+    def norm_block(n):
+        block = blocks[n]
         pair_copies[n].wait()
         normed_ref[block, :] = layer_norm(pair_ref[block, :].astype(F32), gain).astype(BF16)
         copy = pltpu.make_async_copy(normed_ref.at[block], normed_hbm.at[block], out_sems.at[n])
         copy.start()
         normed_copies.append(copy)
+
+    norm_block(0)
+    norm_block(1)
     wait_all(w_copies)
     lane = lanes_of(1)
-    row_start = place_ref[0]
-    col_start = place_ref[1]
+    row_start = lax.axis_index(ROWS) * 48
+    col_start = lax.axis_index(COLS) * 96
     wide_cols = jnp.zeros((1, 128), F32)
     thin_cols = jnp.zeros((1, 128), F32)
     for k in range(64):
@@ -129,12 +133,12 @@
         scr[pl.ds(i + 24, 128, stride=72), :] = right * wide_mask
         scr[pl.ds(i + 48, 128, stride=72), :] = both_p * jax.nn.sigmoid(both_g) * thin_mask
 
-    def chunk(i, carry):
-        for k in range(PROJECT_PAR):
-            one(PROJECT_PAR * i + k)
-        return carry
-
-    lax.fori_loop(0, 24 // PROJECT_PAR, chunk, 0)
+    for m in range(4):
+        if m < 3:
+            norm_block(2 * m + 2)
+            norm_block(2 * m + 3)
+        for k in range(6):
+            one(6 * m + k)
     out_copies = []
     for n in range(8):
         part = scr[1152 * n : 1152 * n + 1152, :].reshape(16, 72, 128)
@@ -435,7 +439,7 @@
 
 def forward_kernel(
     bias_hbm, keep_hbm, recv_hbm, chain_row_ref, chain_col_ref, place_ref, weight_ref,
-    mixed_hbm, full_hbm, stats_hbm, pairs, bias_ref, mixed_ref, full_ref, stats_ref, sems, in_sems, out_sems,
+    mixed_hbm, full_hbm, pairs, bias_ref, mixed_ref, full_ref, sems, in_sems, out_sems,
 ):
     bias_copies = start_all(
         [
@@ -456,9 +460,10 @@
         )
 
     unpack_bias(bias_ref, bias_copies, put)
-    full_copy = pltpu.make_async_copy(full_ref, full_hbm, out_sems.at[0])
+    stats = slice(768, 896)
+    full_copy = pltpu.make_async_copy(full_ref.at[:, 0:768], full_hbm.at[:, 0:768], out_sems.at[0])
     full_copy.start()
-    stats_ref[...] = jnp.zeros_like(stats_ref)
+    full_ref[:, stats] = jnp.zeros((768, 128), F32)
     wait_all(copies)
     low_all = lanes_of(768) < 64
     lane = lanes_of(FORWARD_ROWS)
@@ -472,12 +477,12 @@
         keys = jnp.where(low_all, both, jnp.zeros_like(both))
         rows = pl.ds(pl.multiple_of(b * FORWARD_ROWS, 32), FORWARD_ROWS)
         asked = pairs[s, 0, rows, :]
-        weights = jnp.exp2(dot_nt(asked, keys) * SCALE + full_ref[rows, :])
+        weights = jnp.exp2(dot_nt(asked, keys) * SCALE + full_ref[rows, 0:768])
         inverse = 1.0 / jnp.sum(weights, axis=-1, keepdims=True)
         mixed = matmul((weights * inverse).astype(BF16), both)
         center = jnp.sum(jnp.where(low, 0.0, asked.astype(F32) * mixed), axis=-1, keepdims=True)
-        stats_ref[rows, :] = jnp.where(
-            lane == s, inverse, jnp.where(lane == s + 64, center, stats_ref[rows, :])
+        full_ref[rows, stats] = jnp.where(
+            lane == s, inverse, jnp.where(lane == s + 64, center, full_ref[rows, stats])
         )
         for n in range(shares):
             mixed_ref[owner * 8 + b * shares + n, slot] = jnp.where(
@@ -499,7 +504,7 @@
     mixed_copy(core, 1).start()
     lax.fori_loop(blocks, 2 * blocks, step, 0)
     mixed_copy(1 - core, 2).start()
-    stats_copy = pltpu.make_async_copy(stats_ref, stats_hbm, out_sems.at[3])
+    stats_copy = pltpu.make_async_copy(full_ref.at[:, stats], full_hbm.at[:, stats], out_sems.at[3])
     stats_copy.start()
     mixed_copy(core, 1).wait()
     mixed_copy(1 - core, 2).wait()
@@ -507,16 +512,20 @@
     stats_copy.wait()
 
 
-def backward_kernel(
-    full_hbm, stats_hbm, keep_hbm, recv_hbm, grad_hbm, pairs, full_ref, stats_ref, grad_ref, sems, in_sems, out_sems
-):
+def backward_kernel(full_hbm, keep_hbm, recv_hbm, grad_hbm, pairs, full_ref, grad_ref, sems, in_sems, out_sems):
     copies = pair_copies(keep_hbm, recv_hbm, pairs, sems)
-    copies += start_all([pltpu.make_async_copy(stats_hbm, stats_ref, in_sems.at[0])])
-    copies += start_all([pltpu.make_async_copy(full_hbm, full_ref, in_sems.at[1])])
+    blocks = 768 // BACKWARD_ROWS
+
+    def full_copy(b):
+        rows = pl.ds(pl.multiple_of(b * BACKWARD_ROWS, 32), BACKWARD_ROWS)
+        return pltpu.make_async_copy(full_hbm.at[rows], full_ref.at[rows], in_sems.at[b])
+
+    start_all([full_copy(b) for b in range(blocks)])
     wait_all(copies)
     low_all = lanes_of(768) < 64
 
     def row_block(b, carry):
+        full_copy(b).wait()
         rows = pl.ds(pl.multiple_of(b * BACKWARD_ROWS, 32), BACKWARD_ROWS)
         total = None
         for s in range(6):
@@ -524,9 +533,9 @@
             keys = jnp.where(low_all, both, jnp.zeros_like(both))
             values = jnp.where(low_all, jnp.zeros_like(both), both)
             asked = pairs[s, 0, rows, :]
-            inverse = stats_ref[rows, s : s + 1]
-            center = stats_ref[rows, s + 64 : s + 65]
-            probs = jnp.exp2(dot_nt(asked, keys) * SCALE + full_ref[rows, :]) * inverse
+            inverse = full_ref[rows, 768 + s : 769 + s]
+            center = full_ref[rows, 832 + s : 833 + s]
+            probs = jnp.exp2(dot_nt(asked, keys) * SCALE + full_ref[rows, 0:768]) * inverse
             score_grad = probs * (dot_nt(asked, values) - center)
             total = score_grad if total is None else total + score_grad
         pack_rows(total, grad_ref, b * (BACKWARD_ROWS // 48), BACKWARD_ROWS // 48)
@@ -537,8 +546,8 @@
         part = pl.ds(b * (BACKWARD_ROWS // 48), BACKWARD_ROWS // 48)
         return pltpu.make_async_copy(grad_ref.at[part], grad_hbm.at[part], out_sems.at[b])
 
-    lax.fori_loop(0, 768 // BACKWARD_ROWS, row_block, 0)
-    wait_all([grad_copy(b) for b in range(768 // BACKWARD_ROWS)])
+    lax.fori_loop(0, blocks, row_block, 0)
+    wait_all([grad_copy(b) for b in range(blocks)])
 
 
 def pair_grad_kernel(in_hbm, w_ref, out_hbm, scr, in_ref, out_ref, in_sems, out_sems):
@@ -629,7 +638,7 @@
         "project",
         flops=2 * 512 * 128 * 6144,
         nbytes=5_000_000,
-        spaces=[HBM, VMEM] + [HBM] * 5 + [SMEM],
+        spaces=[HBM, VMEM] + [HBM] * 5,
         out_specs=(HBM, HBM),
     )
 
@@ -670,7 +679,7 @@
         nbytes=4_000_000,
         spaces=[HBM],
         out_specs=HBM,
-        mib=50,
+        mib=50.5,
     )
 
 
@@ -703,14 +712,13 @@
 def run_forward(*args):
     return call(
         forward_kernel,
-        (shape((16, 3, 48, 128)), shape((768, 768), F32), shape((768, 128), F32)),
+        (shape((16, 3, 48, 128)), shape((768, 896), F32)),
         args,
         [
             pltpu.VMEM((6, 2, 768, 128), BF16),
             pltpu.VMEM(PACKED, BF16),
             pltpu.VMEM((16, 3, 48, 128), BF16),
-            pltpu.VMEM((768, 768), F32),
-            pltpu.VMEM((768, 128), F32),
+            pltpu.VMEM((768, 896), F32),
             dma(2),
             dma(2),
             dma(4),
@@ -719,7 +727,7 @@
         flops=6 * 4 * 768 * 768 * 128,
         nbytes=12_000_000,
         spaces=[HBM, HBM, HBM, VMEM, VMEM, SMEM, SMEM],
-        out_specs=(HBM, HBM, HBM),
+        out_specs=(HBM, HBM),
         mib=51,
     )
 
@@ -731,17 +739,16 @@
         args,
         [
             pltpu.VMEM((6, 2, 768, 128), BF16),
-            pltpu.VMEM((768, 768), F32),
-            pltpu.VMEM((768, 128), F32),
+            pltpu.VMEM((768, 896), F32),
             pltpu.VMEM(PACKED, BF16),
             dma(2),
-            dma(2),
+            dma(768 // BACKWARD_ROWS),
             dma(768 // BACKWARD_ROWS),
         ],
         "backward",
         flops=6 * 4 * 768 * 768 * 128,
         nbytes=12_000_000,
-        spaces=[HBM] * 4,
+        spaces=[HBM] * 3,
         out_specs=HBM,
     )
 
@@ -846,7 +853,7 @@
     ).astype(jnp.int32)
 
     sides, normed = run_project(
-        pair_flat, norm_pair.astype(F32)[None], proj_left, proj_right, gate_left, gate_right, pair_mask, place
+        pair_flat, norm_pair, proj_left, proj_right, gate_left, gate_right, pair_mask
     )
     sides_in = exchange(sides, ALL)
 
@@ -893,11 +900,11 @@
     bias_in, rings = lax.optimization_barrier((bias_in, rings))
     far_rings = lax.ppermute(rings, "core", SWAP)
 
-    mixed, full_bias, stats = run_forward(
+    mixed, full_bias = run_forward(
         bias_in, keep, recv, chain_row, chain_col, place, chain_weight
     )
     mixed_in = exchange(mixed, ("core",) + COLS)
-    bias_grad = run_backward(full_bias, stats, keep, recv)
+    bias_grad = run_backward(full_bias, keep, recv)
     grad_in = exchange(bias_grad.reshape(128, 40, 128), ALL).reshape(8, 16, 40, 128)
 
     refined = run_transition(

time: 184 us -> 180 us (0.978)
  waiting for transfers between devices: 59 us -> 62.2 us
  starting transfers between devices: 47.3 us -> 44.8 us
  local copies, waits for them, and re-layouts: 7.2 us -> 4.85 us
    ppermute x3, waiting for transfers between devices: 10.7 us -> 12.6 us  [gather_ring(): lax.ppermute(half, 'z', [(i, (i - k) % 4) for i in range(4)])]
    unnamed x39 -> x35, local copies, waits for them, and re-layouts: 4.34 us -> 2.53 us
  transfers between devices with their start and end apart: 11 -> 11, of which waited for: 8 -> 9; matrix products, arithmetic and copies ran while one was open for 4% -> 5% of each run, Pallas kernels for 20% -> 20%
where the time goes in v4:
time: 180 us; the launch traced here: 179 us
  Pallas kernels  62.6 us (35%)
  waiting for transfers between devices  62.2 us (35%)
  starting transfers between devices  44.8 us (25%)
  local copies, waits for them, and re-layouts  4.85 us (3%)
  matrix products  3.54 us (2%)
    pallas_call x8, Pallas kernels, call(): pl.pallas_call(kernel, out_shape=outs, in_specs=spaces or [vmem] * len(ar...  62.6 us
    all_to_all x5, waiting for transfers between devices, exchange(): return lax.all_to_all(value, axes, 0, 0, tiled=True)  46.3 us
    all_to_all x5, starting transfers between devices, exchange(): return lax.all_to_all(value, axes, 0, 0, tiled=True)  34.6 us
    ppermute x3, waiting for transfers between devices, gather_ring(): lax.ppermute(half, 'z', [(i, (i - k) % 4) for i in range(4)])  12.6 us
    ppermute x3, starting transfers between devices, gather_ring(): lax.ppermute(half, 'z', [(i, (i - k) % 4) for i in range(4)])  4.21 us
  transfers between devices with their start and end apart: 11, of which 9 were waited for; matrix products, arithmetic and copies ran while one was open for 5% of the time, Pallas kernels for 20%

profile of v4, /device:TPU:1, one launch (start us, length us, event | category | flops | bytes accessed | tf_op | source)
XLA Modules:
  0.0 179.3 jit_solution(7424035068803924441)
XLA Ops:
  0.6 0.0 copy-start
  0.6 7.0 %project.1 = (bf16[128,72,128]{2,1,0:T(8,128)(2,1)}, bf16[4608,128]{1,0:T(8,128)(2,1)}) custom-call(bf16[4608,128]{1,0:T(8,128)(2,1)} %bitcast.34, bf16[128]{0:T(256)(128)(2,1)} %gain_ref.1, bf16[128,128]{1,0:T(8,128)(2,1)} %pl_hbm.1, bf16[128,128]{1,0:T(8,128)(2,1)} %pr_hbm.1, bf16[128,128]{1,0:T(8,128)(2,1)} %gl_hbm.1, bf16[128,128]{1,0:T(8,128)(2,1)} %gr_hbm.1, ...), custom_call_target="tpu_custom_call" | custom-call | flops 805306368 | bytes 5000000 | tf_op jit(solution)/shard_map/project/pallas_call | solution.py:52
  7.6 0.0 copy-start.7
  7.6 0.0 copy-start.8
  7.6 0.0 copy-start.9
  7.6 0.0 copy-start.12
  7.7 11.5 %all-to-all-start = ((bf16[128,72,128]{2,1,0:T(8,128)(2,1)}), bf16[128,72,128]{2,1,0:T(8,128)(2,1)S(1)}, u32[]{:S(2)}, u32[]{:S(2)}) async-start(bf16[128,72,128]{2,1,0:T(8,128)(2,1)} %get-tuple-element.33), calls=%async_computation | async-start | bytes 4718592 | tf_op jit(solution)/shard_map/all_to_all | solution.py:805
  19.2 0.8 copy.32.wq_ref
  20.0 0.0 copy-done.8
  20.0 0.8 copy.33.wk_ref
  20.8 0.8 copy.34.wv_ref
  21.6 0.6 reshape.55.gain_ref
  22.2 13.3 %tokens.1 = (bf16[3,2,768,128]{3,2,1,0:T(8,128)(2,1)}, bf16[3,2,768,128]{3,2,1,0:T(8,128)(2,1)}) custom-call(bf16[3,768,768]{2,1,0:T(8,128)(2,1)} %tokens_ref.1, bf16[3,768,768]{2,1,0:T(8,128)(2,1)} %grad_ref.1, f32[1,768]{1,0:T(1,128)} %reshape.55.gain_ref, bf16[768,96]{1,0:T(8,128)(2,1)} %copy.32.wq_ref, bf16[768,96]{1,0:T(8,128)(2,1)} %copy.33.wk_ref, ...), custom_call_target="tpu_custom_call" | custom-call | flops 1811939328 | bytes 12000000 | tf_op jit(solution)/shard_map/tokens/pallas_call | solution.py:52
  35.5 3.3 %collective-permute-start = (bf16[48,768]{1,0:T(8,128)(2,1)S(1)}, bf16[48,768]{1,0:T(8,128)(2,1)S(1)}, u32[]{:S(2)}, u32[]{:S(2)}) collective-permute-start(bf16[48,768]{1,0:T(8,128)(2,1)S(1)} %constant_dynamic-slice_fusion.1), channel_id=1, source_target_pairs={{0,3},{1,0},{2,1},{3,2},{4,7},{5,4},{6,5},{7,6},{8,11},{9,8},{10,9... | collective-permute-start | bytes 221192 | tf_op jit(solution)/shard_map/ppermute | solution.py:812
  38.9 0.1 collective-permute-start.1
  39.0 0.8 collective-permute-start.2
  39.8 9.3 %collective-permute-done = bf16[48,768]{1,0:T(8,128)(2,1)S(1)} collective-permute-done((bf16[48,768]{1,0:T(8,128)(2,1)S(1)}, bf16[48,768]{1,0:T(8,128)(2,1)S(1)}, u32[]{:S(2)}, u32[]{:S(2)}) %collective-permute-start) | collective-permute-done | bytes 73760 | tf_op jit(solution)/shard_map/ppermute | solution.py:812
  49.0 2.0 %collective-permute-done.1 = bf16[48,768]{1,0:T(8,128)(2,1)S(1)} collective-permute-done((bf16[48,768]{1,0:T(8,128)(2,1)S(1)}, bf16[48,768]{1,0:T(8,128)(2,1)S(1)}, u32[]{:S(2)}, u32[]{:S(2)}) %collective-permute-start.1) | collective-permute-done | bytes 73760 | tf_op jit(solution)/shard_map/ppermute | solution.py:812
  51.0 1.3 collective-permute-done.2
  52.4 0.0 all-to-all-done
  52.4 0.0 copy-start.5
  52.4 3.4 %collective-permute-start.3 = (bf16[4,48,768]{2,1,0:T(8,128)(2,1)S(1)}, bf16[4,48,768]{2,1,0:T(8,128)(2,1)S(1)}, u32[]{:S(2)}, u32[]{:S(2)}) collective-permute-start(bf16[4,48,768]{2,1,0:T(8,128)(2,1)S(1)} %pad_maximum_fusion.1), channel_id=1, source_target_pairs={{0,4},{4,0},{1,5},{5,1},{2,6},{6,2},{3,7},{7,3},{8,12},{12,8},{9,1... | collective-permute-start | bytes 884744 | tf_op jit(solution)/shard_map/ppermute | solution.py:869
  55.8 4.9 %product.1 = bf16[16,8,40,128]{3,2,1,0:T(8,128)(2,1)} custom-call(bf16[16,8,72,128]{3,2,1,0:T(8,128)(2,1)} %bitcast.37), custom_call_target="tpu_custom_call" | custom-call | flops 905969664 | bytes 4000000 | tf_op jit(solution)/shard_map/product/pallas_call | solution.py:52
  60.7 0.0 copy-start.10
  60.7 0.0 copy-start.11
  60.8 0.0 copy-start.13
  60.8 0.0 copy-start.15
  60.8 1.7 collective-permute-done.3
  62.4 0.1 pad_maximum_fusion.ring_hbm
  62.5 7.6 %all-to-all-start.1 = ((bf16[128,40,128]{2,1,0:T(8,128)(2,1)}), bf16[128,40,128]{2,1,0:T(8,128)(2,1)}, u32[]{:S(2)}, u32[]{:S(2)}) async-start(bf16[128,40,128]{2,1,0:T(8,128)(2,1)} %bitcast.7), calls=%async_computation.1 | async-start | bytes 2621440 | tf_op jit(solution)/shard_map/all_to_all | solution.py:805
  70.1 1.4 collective-permute-start.4
  71.5 0.0 copy-done.10
  71.5 0.1 reshape_broadcast_in_dim.3
  71.5 0.1 slice.7
  71.6 0.1 reshape.50
  71.7 0.1 reshape.49
  71.8 1.1 constant_dynamic-slice_fusion.token_hbm
  72.9 0.0 copy-done
  72.9 0.0 copy-start.14
  72.9 0.0 copy-start.1
  72.9 0.0 copy-start.2
  72.9 3.5 %fusion.2 = f32[4608,128]{1,0:T(8,128)} fusion(bf16[4608,128]{1,0:T(8,128)(2,1)} %get-tuple-element.43, bf16[128,128]{1,0:T(8,128)(2,1)S(1)} %copy-done), kind=kOutput, calls=%fused_computation.3 | convolution fusion | flops 152764416 | bytes 3571712 | tf_op jit(solution)/shard_map/dot_general | solution.py:30
  76.5 0.0 collective-permute-done.4.recv_hbm
  76.5 13.7 %all-to-all-done.1.t_hbm = bf16[128,40,128]{2,1,0:T(8,128)(2,1)} async-done(((bf16[128,40,128]{2,1,0:T(8,128)(2,1)}), bf16[128,40,128]{2,1,0:T(8,128)(2,1)}, u32[]{:S(2)}, u32[]{:S(2)}) %all-to-all-start.1) | async-done | bytes 1310752 | tf_op jit(solution)/shard_map/all_to_all | solution.py:805
  90.2 0.0 copy-done.14
  90.2 0.1 broadcast_in_dim.28.tri_gain_ref
  90.3 0.0 copy-done.1
  90.3 6.4 %update.1 = (f32[48,96,128]{2,1,0:T(8,128)}, bf16[8,16,40,128]{3,2,1,0:T(8,128)(2,1)}) custom-call(bf16[128,40,128]{2,1,0:T(8,128)(2,1)} %all-to-all-done.1.t_hbm, bf16[48,96,128]{2,1,0:T(8,128)(2,1)S(1)} %copy-done.1, f32[48,96,128]{2,1,0:T(8,128)} %bitcast.38, bf16[128,128]{1,0:T(8,128)(2,1)S(1)} %copy-done.2, ...), custom_call_target="tpu_custom_call" | custom-call | flops 167772160 | bytes 9000000 | tf_op jit(solution)/shard_map/update/pallas_call | solution.py:52
  96.7 0.0 copy-start.4
  96.7 6.1 %all-to-all-start.2 = ((bf16[128,40,128]{2,1,0:T(8,128)(2,1)}), bf16[128,40,128]{2,1,0:T(8,128)(2,1)}, u32[]{:S(2)}, u32[]{:S(2)}) async-start(bf16[128,40,128]{2,1,0:T(8,128)(2,1)} %bitcast.39), calls=%async_computation.2 | async-start | bytes 2621440 | tf_op jit(solution)/shard_map/all_to_all | solution.py:805
  102.8 0.1 stack.47.place_ref
  102.9 0.2 copy.36.chain_row_ref
  103.1 19.8 %all-to-all-done.2 = bf16[128,40,128]{2,1,0:T(8,128)(2,1)} async-done(((bf16[128,40,128]{2,1,0:T(8,128)(2,1)}), bf16[128,40,128]{2,1,0:T(8,128)(2,1)}, u32[]{:S(2)}, u32[]{:S(2)}) %all-to-all-start.2) | async-done | bytes 1310752 | tf_op jit(solution)/shard_map/all_to_all | solution.py:805
  122.9 0.0 copy-done.3
  123.0 9.4 %forward.1 = (bf16[16,3,48,128]{3,2,1,0:T(8,128)(2,1)}, f32[768,896]{1,0:T(8,128)}) custom-call(bf16[16,8,40,128]{3,2,1,0:T(8,128)(2,1)} %bitcast.16.bias_hbm, bf16[3,2,768,128]{3,2,1,0:T(8,128)(2,1)S(1)} %copy-done.3, bf16[3,2,768,128]{3,2,1,0:T(8,128)(2,1)} %collective-permute-done.4.recv_hbm, s32[768,1]{1,0:T(8,128)S(1)} %copy.36.chain_row_ref, ...), custom_call_target="tpu_custom_call" | custom-call | flops 1811939328 | bytes 12000000 | tf_op jit(solution)/shard_map/forward/pallas_call | solution.py:52
  132.3 5.1 %all-to-all-start.3 = ((bf16[16,3,48,128]{3,2,1,0:T(8,128)(2,1)}), bf16[16,3,48,128]{3,2,1,0:T(8,128)(2,1)S(1)}, u32[]{:S(2)}, u32[]{:S(2)}) async-start(bf16[16,3,48,128]{3,2,1,0:T(8,128)(2,1)} %get-tuple-element.57), calls=%async_computation.3 | async-start | bytes 1179648 | tf_op jit(solution)/shard_map/all_to_all | solution.py:805
  137.4 8.1 %backward.1 = bf16[16,8,40,128]{3,2,1,0:T(8,128)(2,1)} custom-call(f32[768,896]{1,0:T(8,128)} %get-tuple-element.61.full_hbm, bf16[3,2,768,128]{3,2,1,0:T(8,128)(2,1)} %get-tuple-element.53.keep_hbm, bf16[3,2,768,128]{3,2,1,0:T(8,128)(2,1)} %collective-permute-done.4.recv_hbm), custom_call_target="tpu_custom_call" | custom-call | flops 1811939328 | bytes 12000000 | tf_op jit(solution)/shard_map/backward/pallas_call | solution.py:52
  145.6 4.6 %all-to-all-done.3.mixed_hbm = bf16[16,3,48,128]{3,2,1,0:T(8,128)(2,1)S(1)} async-done(((bf16[16,3,48,128]{3,2,1,0:T(8,128)(2,1)}), bf16[16,3,48,128]{3,2,1,0:T(8,128)(2,1)S(1)}, u32[]{:S(2)}, u32[]{:S(2)}) %all-to-all-start.3) | async-done | bytes 589856 | tf_op jit(solution)/shard_map/all_to_all | solution.py:805
  150.2 4.4 %all-to-all-start.4 = ((bf16[128,40,128]{2,1,0:T(8,128)(2,1)}), bf16[128,40,128]{2,1,0:T(8,128)(2,1)S(1)}, u32[]{:S(2)}, u32[]{:S(2)}) async-start(bf16[128,40,128]{2,1,0:T(8,128)(2,1)} %bitcast.40), calls=%async_computation.4 | async-start | bytes 2621440 | tf_op jit(solution)/shard_map/all_to_all | solution.py:805
  154.6 1.1 collective-permute-start.5
  155.8 1.6 collective-permute-done.5.far_hbm
  157.4 9.5 %transition.1 = f32[3,96,768]{2,1,0:T(8,128)} custom-call(bf16[16,3,48,128]{3,2,1,0:T(8,128)(2,1)S(1)} %all-to-all-done.3.mixed_hbm, bf16[8,48,768]{2,1,0:T(8,128)(2,1)S(1)} %pad_maximum_fusion.ring_hbm, bf16[8,48,768]{2,1,0:T(8,128)(2,1)S(1)} %collective-permute-done.5.far_hbm, s32[6]{0:T(128)S(1)} %stack.47.place_ref, ...), custom_call_target="tpu_custom_call" | custom-call | flops 2491416576 | bytes 12000000 | tf_op jit(solution)/shard_map/transition/pallas_call | solution.py:52
  166.9 8.2 %all-to-all-done.4 = bf16[128,40,128]{2,1,0:T(8,128)(2,1)S(1)} async-done(((bf16[128,40,128]{2,1,0:T(8,128)(2,1)}), bf16[128,40,128]{2,1,0:T(8,128)(2,1)S(1)}, u32[]{:S(2)}, u32[]{:S(2)}) %all-to-all-start.4) | async-done | bytes 1310752 | tf_op jit(solution)/shard_map/all_to_all | solution.py:805
  175.0 4.1 %pair_grad.1 = f32[48,96,128]{2,1,0:T(8,128)} custom-call(bf16[8,16,40,128]{3,2,1,0:T(8,128)(2,1)S(1)} %bitcast.33, bf16[48,128]{1,0:T(8,128)(2,1)S(1)} %pad_maximum_fusion.2.w_ref), custom_call_target="tpu_custom_call" | custom-call | flops 62914560 | bytes 4000000 | tf_op jit(solution)/shard_map/pair_grad/pallas_call | solution.py:52
  (21 shorter events, 0.1 us)
Async XLA Ops:
  0.6 72.3 %copy-start = (bf16[128,128]{1,0:T(8,128)(2,1)S(1)}, bf16[128,128]{1,0:T(8,128)(2,1)}, u32[]{:S(2)}) copy-start(bf16[128,128]{1,0:T(8,128)(2,1)} %param.35) | copy-start | bytes 98308
  7.6 11.6 %copy-start.7 = (bf16[768,96]{0,1:T(8,128)(2,1)S(1)}, bf16[768,96]{0,1:T(8,128)(2,1)}, u32[]{:S(2)}) copy-start(bf16[768,96]{0,1:T(8,128)(2,1)} %param.42) | copy-start | bytes 442372
  7.6 12.4 %copy-start.8 = (bf16[768,96]{0,1:T(8,128)(2,1)S(1)}, bf16[768,96]{0,1:T(8,128)(2,1)}, u32[]{:S(2)}) copy-start(bf16[768,96]{0,1:T(8,128)(2,1)} %param.43) | copy-start | bytes 442372
  7.6 13.2 %copy-start.9 = (bf16[768,96]{0,1:T(8,128)(2,1)S(1)}, bf16[768,96]{0,1:T(8,128)(2,1)}, u32[]{:S(2)}) copy-start(bf16[768,96]{0,1:T(8,128)(2,1)} %param.44) | copy-start | bytes 442372
  7.6 14.0 %copy-start.12 = (bf16[768]{0:T(1024)(128)(2,1)S(1)}, bf16[768]{0:T(1024)(128)(2,1)}, u32[]{:S(2)}) copy-start(bf16[768]{0:T(1024)(128)(2,1)} %param.41) | copy-start | bytes 4612
  7.7 44.7 %all-to-all-start = ((bf16[128,72,128]{2,1,0:T(8,128)(2,1)}), bf16[128,72,128]{2,1,0:T(8,128)(2,1)S(1)}, u32[]{:S(2)}, u32[]{:S(2)}) async-start(bf16[128,72,128]{2,1,0:T(8,128)(2,1)} %get-tuple-element.33), calls=%async_computation | async-start | bytes 4718592 | tf_op jit(solution)/shard_map/all_to_all | solution.py:805
  22.2 13.3 %copy-start.6 = (bf16[96,768]{1,0:T(8,128)(2,1)S(1)}, bf16[96,768]{1,0:T(8,128)(2,1)}, u32[]{:S(2)}) copy-start(bf16[96,768]{1,0:T(8,128)(2,1)} %wo_ref.1) | copy-start | bytes 442372
  35.5 13.5 %collective-permute-start = (bf16[48,768]{1,0:T(8,128)(2,1)S(1)}, bf16[48,768]{1,0:T(8,128)(2,1)S(1)}, u32[]{:S(2)}, u32[]{:S(2)}) collective-permute-start(bf16[48,768]{1,0:T(8,128)(2,1)S(1)} %constant_dynamic-slice_fusion.1), channel_id=1, source_target_pairs={{0,3},{1,0},{2,1},{3,2},{4,7},{5,4},{6,5},{7,6},{8,11},{9,8},{10,9... | collective-permute-start | bytes 221192 | tf_op jit(solution)/shard_map/ppermute | solution.py:812
  38.9 12.2 %collective-permute-start.1 = (bf16[48,768]{1,0:T(8,128)(2,1)S(1)}, bf16[48,768]{1,0:T(8,128)(2,1)S(1)}, u32[]{:S(2)}, u32[]{:S(2)}) collective-permute-start(bf16[48,768]{1,0:T(8,128)(2,1)S(1)} %constant_dynamic-slice_fusion.1), channel_id=1, source_target_pairs={{0,2},{1,3},{2,0},{3,1},{4,6},{5,7},{6,4},{7,5},{8,10},{9,11},{10,... | collective-permute-start | bytes 221192 | tf_op jit(solution)/shard_map/ppermute | solution.py:812
  39.0 13.4 %collective-permute-start.2 = (bf16[48,768]{1,0:T(8,128)(2,1)S(1)}, bf16[48,768]{1,0:T(8,128)(2,1)S(1)}, u32[]{:S(2)}, u32[]{:S(2)}) collective-permute-start(bf16[48,768]{1,0:T(8,128)(2,1)S(1)} %constant_dynamic-slice_fusion.1), channel_id=1, source_target_pairs={{0,1},{1,2},{2,3},{3,0},{4,5},{5,6},{6,7},{7,4},{8,9},{9,10},{10,1... | collective-permute-start | bytes 221192 | tf_op jit(solution)/shard_map/ppermute | solution.py:812
  52.4 3.4 %copy-start.5 = (bf16[128,72,128]{2,1,0:T(8,128)(2,1)}, bf16[128,72,128]{2,1,0:T(8,128)(2,1)S(1)}, u32[]{:S(2)}) copy-start(bf16[128,72,128]{2,1,0:T(8,128)(2,1)S(1)} %all-to-all-done) | copy-start | bytes 7077892
  52.4 10.0 %collective-permute-start.3 = (bf16[4,48,768]{2,1,0:T(8,128)(2,1)S(1)}, bf16[4,48,768]{2,1,0:T(8,128)(2,1)S(1)}, u32[]{:S(2)}, u32[]{:S(2)}) collective-permute-start(bf16[4,48,768]{2,1,0:T(8,128)(2,1)S(1)} %pad_maximum_fusion.1), channel_id=1, source_target_pairs={{0,4},{4,0},{1,5},{5,1},{2,6},{6,2},{3,7},{7,3},{8,12},{12,8},{9,1... | collective-permute-start | bytes 884744 | tf_op jit(solution)/shard_map/ppermute | solution.py:869
  60.7 10.7 %copy-start.10 = (s32[768]{0:T(1024)S(1)}, s32[768]{0:T(1024)}, u32[]{:S(2)}) copy-start(s32[768]{0:T(1024)} %param.27) | copy-start | bytes 9220
  60.7 11.0 %copy-start.11 = (bf16[128,16]{0,1:T(8,128)(2,1)S(1)}, bf16[128,16]{0,1:T(8,128)(2,1)}, u32[]{:S(2)}) copy-start(bf16[128,16]{0,1:T(8,128)(2,1)} %param.39) | copy-start | bytes 12292
  60.8 11.0 %copy-start.13 = (bf16[768]{0:T(1024)(128)(2,1)S(1)}, bf16[768]{0:T(1024)(128)(2,1)}, u32[]{:S(2)}) copy-start(bf16[768]{0:T(1024)(128)(2,1)} %param.46) | copy-start | bytes 4612
  60.8 12.1 %copy-start.15 = (bf16[128]{0:T(256)(128)(2,1)S(1)}, bf16[128]{0:T(256)(128)(2,1)}, u32[]{:S(2)}) copy-start(bf16[128]{0:T(256)(128)(2,1)} %param.38) | copy-start | bytes 772
  62.5 27.7 %all-to-all-start.1 = ((bf16[128,40,128]{2,1,0:T(8,128)(2,1)}), bf16[128,40,128]{2,1,0:T(8,128)(2,1)}, u32[]{:S(2)}, u32[]{:S(2)}) async-start(bf16[128,40,128]{2,1,0:T(8,128)(2,1)} %bitcast.7), calls=%async_computation.1 | async-start | bytes 2621440 | tf_op jit(solution)/shard_map/all_to_all | solution.py:805
  70.1 6.4 %collective-permute-start.4 = (bf16[3,2,768,128]{3,2,1,0:T(8,128)(2,1)}, bf16[3,2,768,128]{3,2,1,0:T(8,128)(2,1)}, u32[]{:S(2)}, u32[]{:S(2)}) collective-permute-start(bf16[3,2,768,128]{3,2,1,0:T(8,128)(2,1)} %get-tuple-element.42), channel_id=1, source_target_pairs={{0,8},{8,0},{1,9},{9,1},{2,10},{10,2},{3,11},{11,3},{4,12},{12,4},... | collective-permute-start | bytes 3538952 | tf_op jit(solution)/shard_map/ppermute | solution.py:867
  72.9 17.3 %copy-start.14 = (bf16[128]{0:T(256)(128)(2,1)S(1)}, bf16[128]{0:T(256)(128)(2,1)}, u32[]{:S(2)}) copy-start(bf16[128]{0:T(256)(128)(2,1)} %param.36) | copy-start | bytes 772
  72.9 17.4 %copy-start.1 = (bf16[48,96,128]{2,1,0:T(8,128)(2,1)S(1)}, bf16[48,96,128]{2,1,0:T(8,128)(2,1)}, u32[]{:S(2)}) copy-start(bf16[48,96,128]{2,1,0:T(8,128)(2,1)} %pair_hbm.1) | copy-start | bytes 3538948
  72.9 17.4 %copy-start.2 = (bf16[128,128]{1,0:T(8,128)(2,1)S(1)}, bf16[128,128]{1,0:T(8,128)(2,1)}, u32[]{:S(2)}) copy-start(bf16[128,128]{1,0:T(8,128)(2,1)} %w_ref.1) | copy-start | bytes 98308
  96.7 26.2 %copy-start.3 = (bf16[3,2,768,128]{3,2,1,0:T(8,128)(2,1)S(1)}, bf16[3,2,768,128]{3,2,1,0:T(8,128)(2,1)}, u32[]{:S(2)}) copy-start(bf16[3,2,768,128]{3,2,1,0:T(8,128)(2,1)} %get-tuple-element.53.keep_hbm) | copy-start | bytes 3538948
  96.7 26.2 %copy-start.4 = (f32[16]{0:T(128)S(1)}, f32[16]{0:T(128)}, u32[]{:S(2)}) copy-start(f32[16]{0:T(128)} %weight_ref.1) | copy-start | bytes 196
  96.7 26.2 %all-to-all-start.2 = ((bf16[128,40,128]{2,1,0:T(8,128)(2,1)}), bf16[128,40,128]{2,1,0:T(8,128)(2,1)}, u32[]{:S(2)}, u32[]{:S(2)}) async-start(bf16[128,40,128]{2,1,0:T(8,128)(2,1)} %bitcast.39), calls=%async_computation.2 | async-start | bytes 2621440 | tf_op jit(solution)/shard_map/all_to_all | solution.py:805
  132.3 17.9 %all-to-all-start.3 = ((bf16[16,3,48,128]{3,2,1,0:T(8,128)(2,1)}), bf16[16,3,48,128]{3,2,1,0:T(8,128)(2,1)S(1)}, u32[]{:S(2)}, u32[]{:S(2)}) async-start(bf16[16,3,48,128]{3,2,1,0:T(8,128)(2,1)} %get-tuple-element.57), calls=%async_computation.3 | async-start | bytes 1179648 | tf_op jit(solution)/shard_map/all_to_all | solution.py:805
  150.2 24.8 %all-to-all-start.4 = ((bf16[128,40,128]{2,1,0:T(8,128)(2,1)}), bf16[128,40,128]{2,1,0:T(8,128)(2,1)S(1)}, u32[]{:S(2)}, u32[]{:S(2)}) async-start(bf16[128,40,128]{2,1,0:T(8,128)(2,1)} %bitcast.40), calls=%async_computation.4 | async-start | bytes 2621440 | tf_op jit(solution)/shard_map/all_to_all | solution.py:805
  154.6 2.8 %collective-permute-start.5 = (bf16[8,48,768]{2,1,0:T(8,128)(2,1)S(1)}, bf16[8,48,768]{2,1,0:T(8,128)(2,1)S(1)}, u32[]{:S(2)}, u32[]{:S(2)}) collective-permute-start(bf16[8,48,768]{2,1,0:T(8,128)(2,1)S(1)} %pad_maximum_fusion.ring_hbm), channel_id=1, source_target_pairs={{0,8},{8,0},{1,9},{9,1},{2,10},{10,2},{3,11},{11,3},{4,12},{12,4},... | collective-permute-start | bytes 1769480 | tf_op jit(solution)/shard_map/ppermute | solution.py:901

commit v5 on v4

--- a/solution.py
+++ b/solution.py
@@ -679,7 +679,7 @@
         nbytes=4_000_000,
         spaces=[HBM],
         out_specs=HBM,
-        mib=50.5,
+        mib=50,
     )
 
 
@@ -866,8 +866,6 @@
     sides_in, keep, send, ring = lax.optimization_barrier((sides_in, keep, send, ring))
     recv = lax.ppermute(send, "core", SWAP)
     products = run_product(sides_in.reshape(16, 8, 72, 128))
-    rings = jnp.concatenate([ring, lax.ppermute(ring, "xh", SWAP)], axis=0)
-    products, rings = lax.optimization_barrier((products, rings))
     tri_in = exchange(products.reshape(128, 40, 128), ALL)
     share_len = seq_len // 8
     token_share = lax.dynamic_slice_in_dim(tokens, col_index * share_len, share_len, 1)
@@ -897,12 +895,14 @@
     )
     bias_in = exchange(bias.reshape(128, 40, 128), ALL).reshape(PACKED)
 
-    bias_in, rings = lax.optimization_barrier((bias_in, rings))
-    far_rings = lax.ppermute(rings, "core", SWAP)
+    bias_in, ring = lax.optimization_barrier((bias_in, ring))
+    rings = jnp.concatenate([ring, lax.ppermute(ring, "xh", SWAP)], axis=0)
 
     mixed, full_bias = run_forward(
         bias_in, keep, recv, chain_row, chain_col, place, chain_weight
     )
+    mixed, rings = lax.optimization_barrier((mixed, rings))
+    far_rings = lax.ppermute(rings, "core", SWAP)
     mixed_in = exchange(mixed, ("core",) + COLS)
     bias_grad = run_backward(full_bias, keep, recv)
     grad_in = exchange(bias_grad.reshape(128, 40, 128), ALL).reshape(8, 16, 40, 128)

time: 180 us -> 177 us (0.983)
  blocking collectives: 0 us -> 26.2 us
  waiting for transfers between devices: 62.2 us -> 40.7 us
  starting transfers between devices: 44.8 us -> 36.7 us
    all_to_all x0 -> x1, blocking collectives: none -> 26.2 us  [exchange(): return lax.all_to_all(value, axes, 0, 0, tiled=True)]
    all_to_all x5 -> x4, waiting for transfers between devices: 46.3 us -> 26.5 us  [exchange(): return lax.all_to_all(value, axes, 0, 0, tiled=True)]
    all_to_all x5 -> x4, starting transfers between devices: 34.6 us -> 27.3 us  [exchange(): return lax.all_to_all(value, axes, 0, 0, tiled=True)]
  transfers between devices with their start and end apart: 11 -> 10, of which waited for: 9 -> 7; matrix products, arithmetic and copies ran while one was open for 5% -> 5% of each run, Pallas kernels for 20% -> 23%
where the time goes in v5:
time: 177 us
  Pallas kernels  62.3 us (35%)
  waiting for transfers between devices  40.7 us (23%)
  starting transfers between devices  36.7 us (21%)
  blocking collectives  26.2 us (15%)
  local copies, waits for them, and re-layouts  5.89 us (3%)
  matrix products  3.55 us (2%)
    pallas_call x8, Pallas kernels, call(): pl.pallas_call(kernel, out_shape=outs, in_specs=spaces or [vmem] * len(ar...  62.3 us
    all_to_all x4, starting transfers between devices, exchange(): return lax.all_to_all(value, axes, 0, 0, tiled=True)  27.3 us
    all_to_all x4, waiting for transfers between devices, exchange(): return lax.all_to_all(value, axes, 0, 0, tiled=True)  26.5 us
    all_to_all x1, blocking collectives, exchange(): return lax.all_to_all(value, axes, 0, 0, tiled=True)  26.2 us
    ppermute x3, waiting for transfers between devices, gather_ring(): lax.ppermute(half, 'z', [(i, (i - k) % 4) for i in range(4)])  12.6 us
    ppermute x3, starting transfers between devices, gather_ring(): lax.ppermute(half, 'z', [(i, (i - k) % 4) for i in range(4)])  4.21 us
    unnamed x35, local copies, waits for them, and re-layouts  3.57 us
    dot_general x1, matrix products, matmul(): return jnp.dot(left_side, right_side, preferred_element_type=F32)  3.55 us
  transfers between devices with their start and end apart: 10, of which 7 were waited for; matrix products, arithmetic and copies ran while one was open for 5% of the time, Pallas kernels for 23%

profile of v5, /device:TPU:1, one launch (start us, length us, event | category | flops | bytes accessed | tf_op | source)
XLA Modules:
  0.0 176.6 jit_solution(6722002026845279719)
XLA Ops:
  0.6 0.0 copy-start
  0.6 7.0 %project.1 = (bf16[128,72,128]{2,1,0:T(8,128)(2,1)}, bf16[4608,128]{1,0:T(8,128)(2,1)}) custom-call(bf16[4608,128]{1,0:T(8,128)(2,1)} %bitcast.36, bf16[128]{0:T(256)(128)(2,1)} %gain_ref.1, bf16[128,128]{1,0:T(8,128)(2,1)} %pl_hbm.1, bf16[128,128]{1,0:T(8,128)(2,1)} %pr_hbm.1, bf16[128,128]{1,0:T(8,128)(2,1)} %gl_hbm.1, bf16[128,128]{1,0:T(8,128)(2,1)} %gr_hbm.1, ...), custom_call_target="tpu_custom_call" | custom-call | flops 805306368 | bytes 5000000 | tf_op jit(solution)/shard_map/project/pallas_call | solution.py:52
  7.6 0.0 copy-start.7
  7.6 0.0 copy-start.8
  7.6 0.0 copy-start.9
  7.6 0.0 copy-start.12
  7.7 11.5 %all-to-all-start = ((bf16[128,72,128]{2,1,0:T(8,128)(2,1)}), bf16[128,72,128]{2,1,0:T(8,128)(2,1)S(1)}, u32[]{:S(2)}, u32[]{:S(2)}) async-start(bf16[128,72,128]{2,1,0:T(8,128)(2,1)} %get-tuple-element.33), calls=%async_computation | async-start | bytes 4718592 | tf_op jit(solution)/shard_map/all_to_all | solution.py:805
  19.2 0.0 copy-done.7
  19.2 0.8 copy.32.wq_ref
  20.0 0.0 copy-done.8
  20.0 0.8 copy.33.wk_ref
  20.8 0.0 copy-done.9
  20.8 0.8 copy.34.wv_ref
  21.6 0.0 copy-done.12
  21.6 0.6 reshape.55.gain_ref
  22.2 13.3 %tokens.1 = (bf16[3,2,768,128]{3,2,1,0:T(8,128)(2,1)}, bf16[3,2,768,128]{3,2,1,0:T(8,128)(2,1)}) custom-call(bf16[3,768,768]{2,1,0:T(8,128)(2,1)} %tokens_ref.1, bf16[3,768,768]{2,1,0:T(8,128)(2,1)} %grad_ref.1, f32[1,768]{1,0:T(1,128)} %reshape.55.gain_ref, bf16[768,96]{1,0:T(8,128)(2,1)} %copy.32.wq_ref, bf16[768,96]{1,0:T(8,128)(2,1)} %copy.33.wk_ref, ...), custom_call_target="tpu_custom_call" | custom-call | flops 1811939328 | bytes 12000000 | tf_op jit(solution)/shard_map/tokens/pallas_call | solution.py:52
  35.5 3.3 %collective-permute-start = (bf16[48,768]{1,0:T(8,128)(2,1)S(1)}, bf16[48,768]{1,0:T(8,128)(2,1)S(1)}, u32[]{:S(2)}, u32[]{:S(2)}) collective-permute-start(bf16[48,768]{1,0:T(8,128)(2,1)S(1)} %constant_dynamic-slice_fusion.1), channel_id=1, source_target_pairs={{0,3},{1,0},{2,1},{3,2},{4,7},{5,4},{6,5},{7,6},{8,11},{9,8},{10,9... | collective-permute-start | bytes 221192 | tf_op jit(solution)/shard_map/ppermute | solution.py:812
  38.9 0.1 collective-permute-start.1
  39.0 0.8 collective-permute-start.2
  39.8 9.3 %collective-permute-done = bf16[48,768]{1,0:T(8,128)(2,1)S(1)} collective-permute-done((bf16[48,768]{1,0:T(8,128)(2,1)S(1)}, bf16[48,768]{1,0:T(8,128)(2,1)S(1)}, u32[]{:S(2)}, u32[]{:S(2)}) %collective-permute-start) | collective-permute-done | bytes 73760 | tf_op jit(solution)/shard_map/ppermute | solution.py:812
  49.0 2.0 %collective-permute-done.1 = bf16[48,768]{1,0:T(8,128)(2,1)S(1)} collective-permute-done((bf16[48,768]{1,0:T(8,128)(2,1)S(1)}, bf16[48,768]{1,0:T(8,128)(2,1)S(1)}, u32[]{:S(2)}, u32[]{:S(2)}) %collective-permute-start.1) | collective-permute-done | bytes 73760 | tf_op jit(solution)/shard_map/ppermute | solution.py:812
  51.0 1.3 collective-permute-done.2
  52.4 0.0 all-to-all-done
  52.4 0.0 copy-start.10
  52.4 0.0 copy-start.11
  52.4 0.0 copy-start.13
  52.4 4.6 %product.1 = bf16[16,8,40,128]{3,2,1,0:T(8,128)(2,1)S(1)} custom-call(bf16[16,8,72,128]{3,2,1,0:T(8,128)(2,1)S(1)} %bitcast.33), custom_call_target="tpu_custom_call" | custom-call | flops 905969664 | bytes 4000000 | tf_op jit(solution)/shard_map/product/pallas_call | solution.py:52
  57.0 0.0 copy-start.1
  57.0 1.0 copy-done.1
  58.1 7.0 %all-to-all-start.1 = ((bf16[128,40,128]{2,1,0:T(8,128)(2,1)}), bf16[128,40,128]{2,1,0:T(8,128)(2,1)}, u32[]{:S(2)}, u32[]{:S(2)}) async-start(bf16[128,40,128]{2,1,0:T(8,128)(2,1)} %bitcast.34), calls=%async_computation.1 | async-start | bytes 2621440 | tf_op jit(solution)/shard_map/all_to_all | solution.py:805
  65.1 1.4 collective-permute-start.3
  66.5 0.0 copy-done.10
  66.5 0.1 reshape_broadcast_in_dim.3
  66.5 0.1 slice.7
  66.6 0.1 reshape.50
  66.7 0.1 reshape.49
  66.8 1.1 constant_dynamic-slice_fusion.token_hbm
  67.9 0.0 copy-start.14
  67.9 0.0 copy-start.2
  67.9 0.0 copy-start.3
  67.9 3.5 %fusion.2 = f32[4608,128]{1,0:T(8,128)} fusion(bf16[4608,128]{1,0:T(8,128)(2,1)} %get-tuple-element.41, bf16[128,128]{1,0:T(8,128)(2,1)S(1)} %copy-done), kind=kOutput, calls=%fused_computation.3 | convolution fusion | flops 152764416 | bytes 3571712 | tf_op jit(solution)/shard_map/dot_general | solution.py:30
  71.5 0.0 collective-permute-done.3.recv_hbm
  71.5 13.7 %all-to-all-done.1.t_hbm = bf16[128,40,128]{2,1,0:T(8,128)(2,1)} async-done(((bf16[128,40,128]{2,1,0:T(8,128)(2,1)}), bf16[128,40,128]{2,1,0:T(8,128)(2,1)}, u32[]{:S(2)}, u32[]{:S(2)}) %all-to-all-start.1) | async-done | bytes 1310752 | tf_op jit(solution)/shard_map/all_to_all | solution.py:805
  85.2 0.0 copy-done.14
  85.2 0.1 broadcast_in_dim.28.tri_gain_ref
  85.3 0.0 copy-done.2
  85.3 6.4 %update.1 = (f32[48,96,128]{2,1,0:T(8,128)}, bf16[8,16,40,128]{3,2,1,0:T(8,128)(2,1)}) custom-call(bf16[128,40,128]{2,1,0:T(8,128)(2,1)} %all-to-all-done.1.t_hbm, bf16[48,96,128]{2,1,0:T(8,128)(2,1)S(1)} %copy-done.2, f32[48,96,128]{2,1,0:T(8,128)} %bitcast.39, bf16[128,128]{1,0:T(8,128)(2,1)S(1)} %copy-done.3, ...), custom_call_target="tpu_custom_call" | custom-call | flops 167772160 | bytes 9000000 | tf_op jit(solution)/shard_map/update/pallas_call | solution.py:52
  91.7 0.0 copy-start.5
  91.7 26.2 %all_to_all.25 = bf16[128,40,128]{2,1,0:T(8,128)(2,1)} all-to-all(bf16[128,40,128]{2,1,0:T(8,128)(2,1)} %bitcast.42), channel_id=1, replica_groups=mesh['grp'=2,'y'=4,'core'=2,'xh'=2,'z'=4] {'grp','y','core','xh','z'}, dimensions={0} | all-to-all | bytes 2621440 | tf_op jit(solution)/shard_map/all_to_all | solution.py:805
  118.0 2.5 %collective-permute-start.4 = (bf16[4,48,768]{2,1,0:T(8,128)(2,1)S(1)}, bf16[4,48,768]{2,1,0:T(8,128)(2,1)S(1)}, u32[]{:S(2)}, u32[]{:S(2)}) collective-permute-start(bf16[4,48,768]{2,1,0:T(8,128)(2,1)S(1)} %pad_maximum_fusion.1), channel_id=1, source_target_pairs={{0,4},{4,0},{1,5},{5,1},{2,6},{6,2},{3,7},{7,3},{8,12},{12,8},{9,1... | collective-permute-start | bytes 884744 | tf_op jit(solution)/shard_map/ppermute | solution.py:899
  120.5 0.1 stack.47.place_ref
  120.6 0.2 copy.36.chain_row_ref
  120.8 9.4 %forward.1 = (bf16[16,3,48,128]{3,2,1,0:T(8,128)(2,1)}, f32[768,896]{1,0:T(8,128)}) custom-call(bf16[16,8,40,128]{3,2,1,0:T(8,128)(2,1)} %bitcast.40, bf16[3,2,768,128]{3,2,1,0:T(8,128)(2,1)S(1)} %copy-done.4, bf16[3,2,768,128]{3,2,1,0:T(8,128)(2,1)} %collective-permute-done.3.recv_hbm, s32[768,1]{1,0:T(8,128)S(1)} %copy.36.chain_row_ref, ...), custom_call_target="tpu_custom_call" | custom-call | flops 1811939328 | bytes 12000000 | tf_op jit(solution)/shard_map/forward/pallas_call | solution.py:52
  130.2 0.0 collective-permute-done.4
  130.2 0.1 pad_maximum_fusion.ring_hbm
  130.3 5.2 %all-to-all-start.3 = ((bf16[16,3,48,128]{3,2,1,0:T(8,128)(2,1)}), bf16[16,3,48,128]{3,2,1,0:T(8,128)(2,1)S(1)}, u32[]{:S(2)}, u32[]{:S(2)}) async-start(bf16[16,3,48,128]{3,2,1,0:T(8,128)(2,1)} %get-tuple-element.57), calls=%async_computation.3 | async-start | bytes 1179648 | tf_op jit(solution)/shard_map/all_to_all | solution.py:805
  135.4 8.1 %backward.1 = bf16[16,8,40,128]{3,2,1,0:T(8,128)(2,1)} custom-call(f32[768,896]{1,0:T(8,128)} %get-tuple-element.61.full_hbm, bf16[3,2,768,128]{3,2,1,0:T(8,128)(2,1)} %get-tuple-element.51.keep_hbm, bf16[3,2,768,128]{3,2,1,0:T(8,128)(2,1)} %collective-permute-done.3.recv_hbm), custom_call_target="tpu_custom_call" | custom-call | flops 1811939328 | bytes 12000000 | tf_op jit(solution)/shard_map/backward/pallas_call | solution.py:52
  143.6 4.6 %all-to-all-done.3.mixed_hbm = bf16[16,3,48,128]{3,2,1,0:T(8,128)(2,1)S(1)} async-done(((bf16[16,3,48,128]{3,2,1,0:T(8,128)(2,1)}), bf16[16,3,48,128]{3,2,1,0:T(8,128)(2,1)S(1)}, u32[]{:S(2)}, u32[]{:S(2)}) %all-to-all-start.3) | async-done | bytes 589856 | tf_op jit(solution)/shard_map/all_to_all | solution.py:805
  148.2 3.6 %all-to-all-start.4 = ((bf16[128,40,128]{2,1,0:T(8,128)(2,1)}), bf16[128,40,128]{2,1,0:T(8,128)(2,1)S(1)}, u32[]{:S(2)}, u32[]{:S(2)}) async-start(bf16[128,40,128]{2,1,0:T(8,128)(2,1)} %bitcast.41), calls=%async_computation.4 | async-start | bytes 2621440 | tf_op jit(solution)/shard_map/all_to_all | solution.py:805
  151.8 1.3 collective-permute-start.5
  153.1 1.6 collective-permute-done.5.far_hbm
  154.7 9.5 %transition.1 = f32[3,96,768]{2,1,0:T(8,128)} custom-call(bf16[16,3,48,128]{3,2,1,0:T(8,128)(2,1)S(1)} %all-to-all-done.3.mixed_hbm, bf16[8,48,768]{2,1,0:T(8,128)(2,1)S(1)} %pad_maximum_fusion.ring_hbm, bf16[8,48,768]{2,1,0:T(8,128)(2,1)S(1)} %collective-permute-done.5.far_hbm, s32[6]{0:T(128)S(1)} %stack.47.place_ref, ...), custom_call_target="tpu_custom_call" | custom-call | flops 2491416576 | bytes 12000000 | tf_op jit(solution)/shard_map/transition/pallas_call | solution.py:52
  164.2 8.2 %all-to-all-done.4 = bf16[128,40,128]{2,1,0:T(8,128)(2,1)S(1)} async-done(((bf16[128,40,128]{2,1,0:T(8,128)(2,1)}), bf16[128,40,128]{2,1,0:T(8,128)(2,1)S(1)}, u32[]{:S(2)}, u32[]{:S(2)}) %all-to-all-start.4) | async-done | bytes 1310752 | tf_op jit(solution)/shard_map/all_to_all | solution.py:805
  172.4 4.1 %pair_grad.1 = f32[48,96,128]{2,1,0:T(8,128)} custom-call(bf16[8,16,40,128]{3,2,1,0:T(8,128)(2,1)S(1)} %bitcast.35, bf16[48,128]{1,0:T(8,128)(2,1)S(1)} %pad_maximum_fusion.2.w_ref), custom_call_target="tpu_custom_call" | custom-call | flops 62914560 | bytes 4000000 | tf_op jit(solution)/shard_map/pair_grad/pallas_call | solution.py:52
  (20 shorter events, 0.1 us)
Async XLA Ops:
  0.6 67.3 %copy-start = (bf16[128,128]{1,0:T(8,128)(2,1)S(1)}, bf16[128,128]{1,0:T(8,128)(2,1)}, u32[]{:S(2)}) copy-start(bf16[128,128]{1,0:T(8,128)(2,1)} %param.35) | copy-start | bytes 98308
  7.6 11.6 %copy-start.7 = (bf16[768,96]{0,1:T(8,128)(2,1)S(1)}, bf16[768,96]{0,1:T(8,128)(2,1)}, u32[]{:S(2)}) copy-start(bf16[768,96]{0,1:T(8,128)(2,1)} %param.42) | copy-start | bytes 442372
  7.6 12.4 %copy-start.8 = (bf16[768,96]{0,1:T(8,128)(2,1)S(1)}, bf16[768,96]{0,1:T(8,128)(2,1)}, u32[]{:S(2)}) copy-start(bf16[768,96]{0,1:T(8,128)(2,1)} %param.43) | copy-start | bytes 442372
  7.6 13.2 %copy-start.9 = (bf16[768,96]{0,1:T(8,128)(2,1)S(1)}, bf16[768,96]{0,1:T(8,128)(2,1)}, u32[]{:S(2)}) copy-start(bf16[768,96]{0,1:T(8,128)(2,1)} %param.44) | copy-start | bytes 442372
  7.6 14.0 %copy-start.12 = (bf16[768]{0:T(1024)(128)(2,1)S(1)}, bf16[768]{0:T(1024)(128)(2,1)}, u32[]{:S(2)}) copy-start(bf16[768]{0:T(1024)(128)(2,1)} %param.41) | copy-start | bytes 4612
  7.7 44.7 %all-to-all-start = ((bf16[128,72,128]{2,1,0:T(8,128)(2,1)}), bf16[128,72,128]{2,1,0:T(8,128)(2,1)S(1)}, u32[]{:S(2)}, u32[]{:S(2)}) async-start(bf16[128,72,128]{2,1,0:T(8,128)(2,1)} %get-tuple-element.33), calls=%async_computation | async-start | bytes 4718592 | tf_op jit(solution)/shard_map/all_to_all | solution.py:805
  22.2 13.3 %copy-start.6 = (bf16[96,768]{1,0:T(8,128)(2,1)S(1)}, bf16[96,768]{1,0:T(8,128)(2,1)}, u32[]{:S(2)}) copy-start(bf16[96,768]{1,0:T(8,128)(2,1)} %wo_ref.1) | copy-start | bytes 442372
  35.5 13.5 %collective-permute-start = (bf16[48,768]{1,0:T(8,128)(2,1)S(1)}, bf16[48,768]{1,0:T(8,128)(2,1)S(1)}, u32[]{:S(2)}, u32[]{:S(2)}) collective-permute-start(bf16[48,768]{1,0:T(8,128)(2,1)S(1)} %constant_dynamic-slice_fusion.1), channel_id=1, source_target_pairs={{0,3},{1,0},{2,1},{3,2},{4,7},{5,4},{6,5},{7,6},{8,11},{9,8},{10,9... | collective-permute-start | bytes 221192 | tf_op jit(solution)/shard_map/ppermute | solution.py:812
  38.9 12.2 %collective-permute-start.1 = (bf16[48,768]{1,0:T(8,128)(2,1)S(1)}, bf16[48,768]{1,0:T(8,128)(2,1)S(1)}, u32[]{:S(2)}, u32[]{:S(2)}) collective-permute-start(bf16[48,768]{1,0:T(8,128)(2,1)S(1)} %constant_dynamic-slice_fusion.1), channel_id=1, source_target_pairs={{0,2},{1,3},{2,0},{3,1},{4,6},{5,7},{6,4},{7,5},{8,10},{9,11},{10,... | collective-permute-start | bytes 221192 | tf_op jit(solution)/shard_map/ppermute | solution.py:812
  39.0 13.4 %collective-permute-start.2 = (bf16[48,768]{1,0:T(8,128)(2,1)S(1)}, bf16[48,768]{1,0:T(8,128)(2,1)S(1)}, u32[]{:S(2)}, u32[]{:S(2)}) collective-permute-start(bf16[48,768]{1,0:T(8,128)(2,1)S(1)} %constant_dynamic-slice_fusion.1), channel_id=1, source_target_pairs={{0,1},{1,2},{2,3},{3,0},{4,5},{5,6},{6,7},{7,4},{8,9},{9,10},{10,1... | collective-permute-start | bytes 221192 | tf_op jit(solution)/shard_map/ppermute | solution.py:812
  52.4 14.1 %copy-start.10 = (s32[768]{0:T(1024)S(1)}, s32[768]{0:T(1024)}, u32[]{:S(2)}) copy-start(s32[768]{0:T(1024)} %param.27) | copy-start | bytes 9220
  52.4 14.4 %copy-start.11 = (bf16[128,16]{0,1:T(8,128)(2,1)S(1)}, bf16[128,16]{0,1:T(8,128)(2,1)}, u32[]{:S(2)}) copy-start(bf16[128,16]{0,1:T(8,128)(2,1)} %param.39) | copy-start | bytes 12292
  52.4 14.4 %copy-start.13 = (bf16[768]{0:T(1024)(128)(2,1)S(1)}, bf16[768]{0:T(1024)(128)(2,1)}, u32[]{:S(2)}) copy-start(bf16[768]{0:T(1024)(128)(2,1)} %param.46) | copy-start | bytes 4612
  57.0 1.1 copy-start.1
  58.1 9.8 %copy-start.15 = (bf16[128]{0:T(256)(128)(2,1)S(1)}, bf16[128]{0:T(256)(128)(2,1)}, u32[]{:S(2)}) copy-start(bf16[128]{0:T(256)(128)(2,1)} %param.38) | copy-start | bytes 772
  58.1 27.1 %all-to-all-start.1 = ((bf16[128,40,128]{2,1,0:T(8,128)(2,1)}), bf16[128,40,128]{2,1,0:T(8,128)(2,1)}, u32[]{:S(2)}, u32[]{:S(2)}) async-start(bf16[128,40,128]{2,1,0:T(8,128)(2,1)} %bitcast.34), calls=%async_computation.1 | async-start | bytes 2621440 | tf_op jit(solution)/shard_map/all_to_all | solution.py:805
  65.1 6.4 %collective-permute-start.3 = (bf16[3,2,768,128]{3,2,1,0:T(8,128)(2,1)}, bf16[3,2,768,128]{3,2,1,0:T(8,128)(2,1)}, u32[]{:S(2)}, u32[]{:S(2)}) collective-permute-start(bf16[3,2,768,128]{3,2,1,0:T(8,128)(2,1)} %get-tuple-element.40), channel_id=1, source_target_pairs={{0,8},{8,0},{1,9},{9,1},{2,10},{10,2},{3,11},{11,3},{4,12},{12,4},... | collective-permute-start | bytes 3538952 | tf_op jit(solution)/shard_map/ppermute | solution.py:867
  67.9 17.3 %copy-start.14 = (bf16[128]{0:T(256)(128)(2,1)S(1)}, bf16[128]{0:T(256)(128)(2,1)}, u32[]{:S(2)}) copy-start(bf16[128]{0:T(256)(128)(2,1)} %param.36) | copy-start | bytes 772
  67.9 17.4 %copy-start.2 = (bf16[48,96,128]{2,1,0:T(8,128)(2,1)S(1)}, bf16[48,96,128]{2,1,0:T(8,128)(2,1)}, u32[]{:S(2)}) copy-start(bf16[48,96,128]{2,1,0:T(8,128)(2,1)} %pair_hbm.1) | copy-start | bytes 3538948
  67.9 17.4 %copy-start.3 = (bf16[128,128]{1,0:T(8,128)(2,1)S(1)}, bf16[128,128]{1,0:T(8,128)(2,1)}, u32[]{:S(2)}) copy-start(bf16[128,128]{1,0:T(8,128)(2,1)} %w_ref.1) | copy-start | bytes 98308
  91.7 29.0 %copy-start.4 = (bf16[3,2,768,128]{3,2,1,0:T(8,128)(2,1)S(1)}, bf16[3,2,768,128]{3,2,1,0:T(8,128)(2,1)}, u32[]{:S(2)}) copy-start(bf16[3,2,768,128]{3,2,1,0:T(8,128)(2,1)} %get-tuple-element.51.keep_hbm) | copy-start | bytes 3538948
  91.7 29.0 %copy-start.5 = (f32[16]{0:T(128)S(1)}, f32[16]{0:T(128)}, u32[]{:S(2)}) copy-start(f32[16]{0:T(128)} %weight_ref.1) | copy-start | bytes 196
  118.0 12.2 %collective-permute-start.4 = (bf16[4,48,768]{2,1,0:T(8,128)(2,1)S(1)}, bf16[4,48,768]{2,1,0:T(8,128)(2,1)S(1)}, u32[]{:S(2)}, u32[]{:S(2)}) collective-permute-start(bf16[4,48,768]{2,1,0:T(8,128)(2,1)S(1)} %pad_maximum_fusion.1), channel_id=1, source_target_pairs={{0,4},{4,0},{1,5},{5,1},{2,6},{6,2},{3,7},{7,3},{8,12},{12,8},{9,1... | collective-permute-start | bytes 884744 | tf_op jit(solution)/shard_map/ppermute | solution.py:899
  130.3 17.9 %all-to-all-start.3 = ((bf16[16,3,48,128]{3,2,1,0:T(8,128)(2,1)}), bf16[16,3,48,128]{3,2,1,0:T(8,128)(2,1)S(1)}, u32[]{:S(2)}, u32[]{:S(2)}) async-start(bf16[16,3,48,128]{3,2,1,0:T(8,128)(2,1)} %get-tuple-element.57), calls=%async_computation.3 | async-start | bytes 1179648 | tf_op jit(solution)/shard_map/all_to_all | solution.py:805
  148.2 24.2 %all-to-all-start.4 = ((bf16[128,40,128]{2,1,0:T(8,128)(2,1)}), bf16[128,40,128]{2,1,0:T(8,128)(2,1)S(1)}, u32[]{:S(2)}, u32[]{:S(2)}) async-start(bf16[128,40,128]{2,1,0:T(8,128)(2,1)} %bitcast.41), calls=%async_computation.4 | async-start | bytes 2621440 | tf_op jit(solution)/shard_map/all_to_all | solution.py:805
  151.8 2.9 %collective-permute-start.5 = (bf16[8,48,768]{2,1,0:T(8,128)(2,1)S(1)}, bf16[8,48,768]{2,1,0:T(8,128)(2,1)S(1)}, u32[]{:S(2)}, u32[]{:S(2)}) collective-permute-start(bf16[8,48,768]{2,1,0:T(8,128)(2,1)S(1)} %pad_maximum_fusion.ring_hbm), channel_id=1, source_target_pairs={{0,8},{8,0},{1,9},{9,1},{2,10},{10,2},{3,11},{11,3},{4,12},{12,4},... | collective-permute-start | bytes 1769480 | tf_op jit(solution)/shard_map/ppermute | solution.py:905

commit v6 on v5

--- a/solution.py
+++ b/solution.py
@@ -861,7 +861,7 @@
     keep, send = run_tokens(
         samples, tokens, grad_attn, norm_tokens.astype(F32)[None], w_query, w_key, w_value, w_out, place[2:3]
     )
-    keep, send, w_out_late = lax.optimization_barrier((keep, send, w_out))
+    normed, w_out_late = lax.optimization_barrier((normed, w_out))
     ring = gather_ring(lax.dynamic_slice_in_dim(w_out_late, core_index * HD, HD, 0))
     sides_in, keep, send, ring = lax.optimization_barrier((sides_in, keep, send, ring))
     recv = lax.ppermute(send, "core", SWAP)

time: 177 us -> 177 us (level)
    unnamed x35 -> x37, local copies, waits for them, and re-layouts: 3.57 us -> 3.58 us
  transfers between devices with their start and end apart: 10 -> 10, of which waited for: 7 -> 6; matrix products, arithmetic and copies ran while one was open for 5% -> 5% of each run, Pallas kernels for 23% -> 23%
where the time goes in v6:
time: 177 us; the launch traced here: 176 us
  Pallas kernels  62.4 us (35%)
  waiting for transfers between devices  40.1 us (23%)
  starting transfers between devices  37 us (21%)
  blocking collectives  26.2 us (15%)
  local copies, waits for them, and re-layouts  5.89 us (3%)
  matrix products  3.54 us (2%)
    pallas_call x8, Pallas kernels, call(): pl.pallas_call(kernel, out_shape=outs, in_specs=spaces or [vmem] * len(ar...  62.4 us
    all_to_all x4, starting transfers between devices, exchange(): return lax.all_to_all(value, axes, 0, 0, tiled=True)  27.6 us
    all_to_all x4, waiting for transfers between devices, exchange(): return lax.all_to_all(value, axes, 0, 0, tiled=True)  26.5 us
    all_to_all x1, blocking collectives, exchange(): return lax.all_to_all(value, axes, 0, 0, tiled=True)  26.2 us
    ppermute x3, waiting for transfers between devices, gather_ring(): lax.ppermute(half, 'z', [(i, (i - k) % 4) for i in range(4)])  11.9 us
    ppermute x3, starting transfers between devices, gather_ring(): lax.ppermute(half, 'z', [(i, (i - k) % 4) for i in range(4)])  4.21 us
    unnamed x37, local copies, waits for them, and re-layouts  3.58 us
    dot_general x1, matrix products, matmul(): return jnp.dot(left_side, right_side, preferred_element_type=F32)  3.54 us
  transfers between devices with their start and end apart: 10, of which 6 were waited for; matrix products, arithmetic and copies ran while one was open for 5% of the time, Pallas kernels for 23%

profile of v6, /device:TPU:1, one launch (start us, length us, event | category | flops | bytes accessed | tf_op | source)
XLA Modules:
  0.0 176.3 jit_solution(6338117057720648709)
XLA Ops:
  0.6 0.0 copy-start
  0.6 7.0 %project.1 = (bf16[128,72,128]{2,1,0:T(8,128)(2,1)}, bf16[4608,128]{1,0:T(8,128)(2,1)}) custom-call(bf16[4608,128]{1,0:T(8,128)(2,1)} %bitcast.36, bf16[128]{0:T(256)(128)(2,1)} %gain_ref.1, bf16[128,128]{1,0:T(8,128)(2,1)} %pl_hbm.1, bf16[128,128]{1,0:T(8,128)(2,1)} %pr_hbm.1, bf16[128,128]{1,0:T(8,128)(2,1)} %gl_hbm.1, bf16[128,128]{1,0:T(8,128)(2,1)} %gr_hbm.1, ...), custom_call_target="tpu_custom_call" | custom-call | flops 805306368 | bytes 5000000 | tf_op jit(solution)/shard_map/project/pallas_call | solution.py:52
  7.6 0.0 copy-start.6
  7.6 0.0 copy-start.8
  7.6 0.0 copy-start.9
  7.6 0.0 copy-start.10
  7.7 0.0 copy-start.13
  7.7 11.5 %all-to-all-start = ((bf16[128,72,128]{2,1,0:T(8,128)(2,1)}), bf16[128,72,128]{2,1,0:T(8,128)(2,1)S(1)}, u32[]{:S(2)}, u32[]{:S(2)}) async-start(bf16[128,72,128]{2,1,0:T(8,128)(2,1)} %get-tuple-element.32), calls=%async_computation | async-start | bytes 4718592 | tf_op jit(solution)/shard_map/all_to_all | solution.py:805
  19.2 0.0 copy-done.6
  19.2 3.3 %collective-permute-start = (bf16[48,768]{1,0:T(8,128)(2,1)S(1)}, bf16[48,768]{1,0:T(8,128)(2,1)S(1)}, u32[]{:S(2)}, u32[]{:S(2)}) collective-permute-start(bf16[48,768]{1,0:T(8,128)(2,1)S(1)} %constant_dynamic-slice_fusion.1), channel_id=1, source_target_pairs={{0,3},{1,0},{2,1},{3,2},{4,7},{5,4},{6,5},{7,6},{8,11},{9,8},{10,9... | collective-permute-start | bytes 221192 | tf_op jit(solution)/shard_map/ppermute | solution.py:812
  22.6 0.1 collective-permute-start.1
  22.7 0.8 collective-permute-start.2
  23.4 0.8 copy.32.wq_ref
  24.3 0.0 copy-done.9
  24.3 0.8 copy.33.wk_ref
  25.1 0.8 copy.34.wv_ref
  25.9 0.6 reshape.55.gain_ref
  26.5 13.3 %tokens.1 = (bf16[3,2,768,128]{3,2,1,0:T(8,128)(2,1)}, bf16[3,2,768,128]{3,2,1,0:T(8,128)(2,1)}) custom-call(bf16[3,768,768]{2,1,0:T(8,128)(2,1)} %tokens_ref.1, bf16[3,768,768]{2,1,0:T(8,128)(2,1)} %grad_ref.1, f32[1,768]{1,0:T(1,128)} %reshape.55.gain_ref, bf16[768,96]{1,0:T(8,128)(2,1)} %copy.32.wq_ref, bf16[768,96]{1,0:T(8,128)(2,1)} %copy.33.wk_ref, ...), custom_call_target="tpu_custom_call" | custom-call | flops 1811939328 | bytes 12000000 | tf_op jit(solution)/shard_map/tokens/pallas_call | solution.py:52
  39.8 0.0 collective-permute-done
  39.8 10.7 %collective-permute-done.1 = bf16[48,768]{1,0:T(8,128)(2,1)S(1)} collective-permute-done((bf16[48,768]{1,0:T(8,128)(2,1)S(1)}, bf16[48,768]{1,0:T(8,128)(2,1)S(1)}, u32[]{:S(2)}, u32[]{:S(2)}) %collective-permute-start.1) | collective-permute-done | bytes 73760 | tf_op jit(solution)/shard_map/ppermute | solution.py:812
  50.5 1.2 collective-permute-done.2
  51.8 0.0 all-to-all-done
  51.8 0.0 copy-start.11
  51.8 0.0 copy-start.12
  51.8 0.0 copy-start.14
  51.8 4.6 %product.1 = bf16[16,8,40,128]{3,2,1,0:T(8,128)(2,1)S(1)} custom-call(bf16[16,8,72,128]{3,2,1,0:T(8,128)(2,1)S(1)} %bitcast.33), custom_call_target="tpu_custom_call" | custom-call | flops 905969664 | bytes 4000000 | tf_op jit(solution)/shard_map/product/pallas_call | solution.py:52
  56.4 0.0 copy-start.1
  56.4 1.0 copy-done.1
  57.5 7.3 %all-to-all-start.1 = ((bf16[128,40,128]{2,1,0:T(8,128)(2,1)}), bf16[128,40,128]{2,1,0:T(8,128)(2,1)}, u32[]{:S(2)}, u32[]{:S(2)}) async-start(bf16[128,40,128]{2,1,0:T(8,128)(2,1)} %bitcast.34), calls=%async_computation.1 | async-start | bytes 2621440 | tf_op jit(solution)/shard_map/all_to_all | solution.py:805
  64.8 1.4 collective-permute-start.3
  66.2 0.0 copy-done.11
  66.2 0.1 reshape_broadcast_in_dim.3
  66.2 0.1 slice.7
  66.3 0.1 reshape.50
  66.4 0.1 reshape.49
  66.5 1.1 constant_dynamic-slice_fusion.token_hbm
  67.6 0.0 copy-done
  67.6 0.0 copy-start.15
  67.6 0.0 copy-start.2
  67.6 0.0 copy-start.3
  67.6 3.5 %fusion.2 = f32[4608,128]{1,0:T(8,128)} fusion(bf16[4608,128]{1,0:T(8,128)(2,1)} %get-tuple-element.39, bf16[128,128]{1,0:T(8,128)(2,1)S(1)} %copy-done), kind=kOutput, calls=%fused_computation.3 | convolution fusion | flops 152764416 | bytes 3571712 | tf_op jit(solution)/shard_map/dot_general | solution.py:30
  71.2 0.0 collective-permute-done.3.recv_hbm
  71.2 13.7 %all-to-all-done.1.t_hbm = bf16[128,40,128]{2,1,0:T(8,128)(2,1)} async-done(((bf16[128,40,128]{2,1,0:T(8,128)(2,1)}), bf16[128,40,128]{2,1,0:T(8,128)(2,1)}, u32[]{:S(2)}, u32[]{:S(2)}) %all-to-all-start.1) | async-done | bytes 1310752 | tf_op jit(solution)/shard_map/all_to_all | solution.py:805
  84.9 0.0 copy-done.15
  84.9 0.1 broadcast_in_dim.28.tri_gain_ref
  85.0 0.0 copy-done.2
  85.0 6.4 %update.1 = (f32[48,96,128]{2,1,0:T(8,128)}, bf16[8,16,40,128]{3,2,1,0:T(8,128)(2,1)}) custom-call(bf16[128,40,128]{2,1,0:T(8,128)(2,1)} %all-to-all-done.1.t_hbm, bf16[48,96,128]{2,1,0:T(8,128)(2,1)S(1)} %copy-done.2, f32[48,96,128]{2,1,0:T(8,128)} %bitcast.39, bf16[128,128]{1,0:T(8,128)(2,1)S(1)} %copy-done.3, ...), custom_call_target="tpu_custom_call" | custom-call | flops 167772160 | bytes 9000000 | tf_op jit(solution)/shard_map/update/pallas_call | solution.py:52
  91.4 0.0 copy-start.5
  91.5 26.2 %all_to_all.25 = bf16[128,40,128]{2,1,0:T(8,128)(2,1)} all-to-all(bf16[128,40,128]{2,1,0:T(8,128)(2,1)} %bitcast.42), channel_id=1, replica_groups=mesh['grp'=2,'y'=4,'core'=2,'xh'=2,'z'=4] {'grp','y','core','xh','z'}, dimensions={0} | all-to-all | bytes 2621440 | tf_op jit(solution)/shard_map/all_to_all | solution.py:805
  117.7 2.5 %collective-permute-start.4 = (bf16[4,48,768]{2,1,0:T(8,128)(2,1)S(1)}, bf16[4,48,768]{2,1,0:T(8,128)(2,1)S(1)}, u32[]{:S(2)}, u32[]{:S(2)}) collective-permute-start(bf16[4,48,768]{2,1,0:T(8,128)(2,1)S(1)} %pad_maximum_fusion.1), channel_id=1, source_target_pairs={{0,4},{4,0},{1,5},{5,1},{2,6},{6,2},{3,7},{7,3},{8,12},{12,8},{9,1... | collective-permute-start | bytes 884744 | tf_op jit(solution)/shard_map/ppermute | solution.py:899
  120.2 0.1 stack.47.place_ref
  120.3 0.2 copy.36.chain_row_ref
  120.5 9.4 %forward.1 = (bf16[16,3,48,128]{3,2,1,0:T(8,128)(2,1)}, f32[768,896]{1,0:T(8,128)}) custom-call(bf16[16,8,40,128]{3,2,1,0:T(8,128)(2,1)} %bitcast.40, bf16[3,2,768,128]{3,2,1,0:T(8,128)(2,1)S(1)} %copy-done.4, bf16[3,2,768,128]{3,2,1,0:T(8,128)(2,1)} %collective-permute-done.3.recv_hbm, s32[768,1]{1,0:T(8,128)S(1)} %copy.36.chain_row_ref, ...), custom_call_target="tpu_custom_call" | custom-call | flops 1811939328 | bytes 12000000 | tf_op jit(solution)/shard_map/forward/pallas_call | solution.py:52
  129.9 0.0 collective-permute-done.4
  129.9 0.1 pad_maximum_fusion.ring_hbm
  130.0 5.2 %all-to-all-start.3 = ((bf16[16,3,48,128]{3,2,1,0:T(8,128)(2,1)}), bf16[16,3,48,128]{3,2,1,0:T(8,128)(2,1)S(1)}, u32[]{:S(2)}, u32[]{:S(2)}) async-start(bf16[16,3,48,128]{3,2,1,0:T(8,128)(2,1)} %get-tuple-element.55), calls=%async_computation.3 | async-start | bytes 1179648 | tf_op jit(solution)/shard_map/all_to_all | solution.py:805
  135.1 8.1 %backward.1 = bf16[16,8,40,128]{3,2,1,0:T(8,128)(2,1)} custom-call(f32[768,896]{1,0:T(8,128)} %get-tuple-element.59.full_hbm, bf16[3,2,768,128]{3,2,1,0:T(8,128)(2,1)} %get-tuple-element.49.keep_hbm, bf16[3,2,768,128]{3,2,1,0:T(8,128)(2,1)} %collective-permute-done.3.recv_hbm), custom_call_target="tpu_custom_call" | custom-call | flops 1811939328 | bytes 12000000 | tf_op jit(solution)/shard_map/backward/pallas_call | solution.py:52
  143.3 4.6 %all-to-all-done.3.mixed_hbm = bf16[16,3,48,128]{3,2,1,0:T(8,128)(2,1)S(1)} async-done(((bf16[16,3,48,128]{3,2,1,0:T(8,128)(2,1)}), bf16[16,3,48,128]{3,2,1,0:T(8,128)(2,1)S(1)}, u32[]{:S(2)}, u32[]{:S(2)}) %all-to-all-start.3) | async-done | bytes 589856 | tf_op jit(solution)/shard_map/all_to_all | solution.py:805
  147.9 3.6 %all-to-all-start.4 = ((bf16[128,40,128]{2,1,0:T(8,128)(2,1)}), bf16[128,40,128]{2,1,0:T(8,128)(2,1)S(1)}, u32[]{:S(2)}, u32[]{:S(2)}) async-start(bf16[128,40,128]{2,1,0:T(8,128)(2,1)} %bitcast.41), calls=%async_computation.4 | async-start | bytes 2621440 | tf_op jit(solution)/shard_map/all_to_all | solution.py:805
  151.6 1.3 collective-permute-start.5
  152.8 1.6 collective-permute-done.5.far_hbm
  154.5 9.5 %transition.1 = f32[3,96,768]{2,1,0:T(8,128)} custom-call(bf16[16,3,48,128]{3,2,1,0:T(8,128)(2,1)S(1)} %all-to-all-done.3.mixed_hbm, bf16[8,48,768]{2,1,0:T(8,128)(2,1)S(1)} %pad_maximum_fusion.ring_hbm, bf16[8,48,768]{2,1,0:T(8,128)(2,1)S(1)} %collective-permute-done.5.far_hbm, s32[6]{0:T(128)S(1)} %stack.47.place_ref, ...), custom_call_target="tpu_custom_call" | custom-call | flops 2491416576 | bytes 12000000 | tf_op jit(solution)/shard_map/transition/pallas_call | solution.py:52
  163.9 8.2 %all-to-all-done.4 = bf16[128,40,128]{2,1,0:T(8,128)(2,1)S(1)} async-done(((bf16[128,40,128]{2,1,0:T(8,128)(2,1)}), bf16[128,40,128]{2,1,0:T(8,128)(2,1)S(1)}, u32[]{:S(2)}, u32[]{:S(2)}) %all-to-all-start.4) | async-done | bytes 1310752 | tf_op jit(solution)/shard_map/all_to_all | solution.py:805
  172.1 4.1 %pair_grad.1 = f32[48,96,128]{2,1,0:T(8,128)} custom-call(bf16[8,16,40,128]{3,2,1,0:T(8,128)(2,1)S(1)} %bitcast.35, bf16[48,128]{1,0:T(8,128)(2,1)S(1)} %pad_maximum_fusion.2.w_ref), custom_call_target="tpu_custom_call" | custom-call | flops 62914560 | bytes 4000000 | tf_op jit(solution)/shard_map/pair_grad/pallas_call | solution.py:52
  (22 shorter events, 0.1 us)
Async XLA Ops:
  0.6 67.0 %copy-start = (bf16[128,128]{1,0:T(8,128)(2,1)S(1)}, bf16[128,128]{1,0:T(8,128)(2,1)}, u32[]{:S(2)}) copy-start(bf16[128,128]{1,0:T(8,128)(2,1)} %param.35) | copy-start | bytes 98308
  7.6 11.6 %copy-start.6 = (bf16[96,768]{1,0:T(8,128)(2,1)S(1)}, bf16[96,768]{1,0:T(8,128)(2,1)}, u32[]{:S(2)}) copy-start(bf16[96,768]{1,0:T(8,128)(2,1)} %wo_ref.1) | copy-start | bytes 442372
  7.6 15.8 %copy-start.8 = (bf16[768,96]{0,1:T(8,128)(2,1)S(1)}, bf16[768,96]{0,1:T(8,128)(2,1)}, u32[]{:S(2)}) copy-start(bf16[768,96]{0,1:T(8,128)(2,1)} %param.42) | copy-start | bytes 442372
  7.6 16.6 %copy-start.9 = (bf16[768,96]{0,1:T(8,128)(2,1)S(1)}, bf16[768,96]{0,1:T(8,128)(2,1)}, u32[]{:S(2)}) copy-start(bf16[768,96]{0,1:T(8,128)(2,1)} %param.43) | copy-start | bytes 442372
  7.6 17.4 %copy-start.10 = (bf16[768,96]{0,1:T(8,128)(2,1)S(1)}, bf16[768,96]{0,1:T(8,128)(2,1)}, u32[]{:S(2)}) copy-start(bf16[768,96]{0,1:T(8,128)(2,1)} %param.44) | copy-start | bytes 442372
  7.7 18.2 %copy-start.13 = (bf16[768]{0:T(1024)(128)(2,1)S(1)}, bf16[768]{0:T(1024)(128)(2,1)}, u32[]{:S(2)}) copy-start(bf16[768]{0:T(1024)(128)(2,1)} %param.41) | copy-start | bytes 4612
  7.7 44.1 %all-to-all-start = ((bf16[128,72,128]{2,1,0:T(8,128)(2,1)}), bf16[128,72,128]{2,1,0:T(8,128)(2,1)S(1)}, u32[]{:S(2)}, u32[]{:S(2)}) async-start(bf16[128,72,128]{2,1,0:T(8,128)(2,1)} %get-tuple-element.32), calls=%async_computation | async-start | bytes 4718592 | tf_op jit(solution)/shard_map/all_to_all | solution.py:805
  19.2 20.6 %collective-permute-start = (bf16[48,768]{1,0:T(8,128)(2,1)S(1)}, bf16[48,768]{1,0:T(8,128)(2,1)S(1)}, u32[]{:S(2)}, u32[]{:S(2)}) collective-permute-start(bf16[48,768]{1,0:T(8,128)(2,1)S(1)} %constant_dynamic-slice_fusion.1), channel_id=1, source_target_pairs={{0,3},{1,0},{2,1},{3,2},{4,7},{5,4},{6,5},{7,6},{8,11},{9,8},{10,9... | collective-permute-start | bytes 221192 | tf_op jit(solution)/shard_map/ppermute | solution.py:812
  22.6 28.0 %collective-permute-start.1 = (bf16[48,768]{1,0:T(8,128)(2,1)S(1)}, bf16[48,768]{1,0:T(8,128)(2,1)S(1)}, u32[]{:S(2)}, u32[]{:S(2)}) collective-permute-start(bf16[48,768]{1,0:T(8,128)(2,1)S(1)} %constant_dynamic-slice_fusion.1), channel_id=1, source_target_pairs={{0,2},{1,3},{2,0},{3,1},{4,6},{5,7},{6,4},{7,5},{8,10},{9,11},{10,... | collective-permute-start | bytes 221192 | tf_op jit(solution)/shard_map/ppermute | solution.py:812
  22.7 29.1 %collective-permute-start.2 = (bf16[48,768]{1,0:T(8,128)(2,1)S(1)}, bf16[48,768]{1,0:T(8,128)(2,1)S(1)}, u32[]{:S(2)}, u32[]{:S(2)}) collective-permute-start(bf16[48,768]{1,0:T(8,128)(2,1)S(1)} %constant_dynamic-slice_fusion.1), channel_id=1, source_target_pairs={{0,1},{1,2},{2,3},{3,0},{4,5},{5,6},{6,7},{7,4},{8,9},{9,10},{10,1... | collective-permute-start | bytes 221192 | tf_op jit(solution)/shard_map/ppermute | solution.py:812
  26.5 13.3 %copy-start.7 = (bf16[96,768]{1,0:T(8,128)(2,1)S(1)}, bf16[96,768]{1,0:T(8,128)(2,1)}, u32[]{:S(2)}) copy-start(bf16[96,768]{1,0:T(8,128)(2,1)} %wo_ref.1) | copy-start | bytes 442372
  51.8 14.4 %copy-start.11 = (s32[768]{0:T(1024)S(1)}, s32[768]{0:T(1024)}, u32[]{:S(2)}) copy-start(s32[768]{0:T(1024)} %param.27) | copy-start | bytes 9220
  51.8 14.7 %copy-start.12 = (bf16[128,16]{0,1:T(8,128)(2,1)S(1)}, bf16[128,16]{0,1:T(8,128)(2,1)}, u32[]{:S(2)}) copy-start(bf16[128,16]{0,1:T(8,128)(2,1)} %param.39) | copy-start | bytes 12292
  51.8 14.7 %copy-start.14 = (bf16[768]{0:T(1024)(128)(2,1)S(1)}, bf16[768]{0:T(1024)(128)(2,1)}, u32[]{:S(2)}) copy-start(bf16[768]{0:T(1024)(128)(2,1)} %param.46) | copy-start | bytes 4612
  56.4 1.1 copy-start.1
  57.5 10.1 %copy-start.16 = (bf16[128]{0:T(256)(128)(2,1)S(1)}, bf16[128]{0:T(256)(128)(2,1)}, u32[]{:S(2)}) copy-start(bf16[128]{0:T(256)(128)(2,1)} %param.38) | copy-start | bytes 772
  57.5 27.4 %all-to-all-start.1 = ((bf16[128,40,128]{2,1,0:T(8,128)(2,1)}), bf16[128,40,128]{2,1,0:T(8,128)(2,1)}, u32[]{:S(2)}, u32[]{:S(2)}) async-start(bf16[128,40,128]{2,1,0:T(8,128)(2,1)} %bitcast.34), calls=%async_computation.1 | async-start | bytes 2621440 | tf_op jit(solution)/shard_map/all_to_all | solution.py:805
  64.8 6.4 %collective-permute-start.3 = (bf16[3,2,768,128]{3,2,1,0:T(8,128)(2,1)}, bf16[3,2,768,128]{3,2,1,0:T(8,128)(2,1)}, u32[]{:S(2)}, u32[]{:S(2)}) collective-permute-start(bf16[3,2,768,128]{3,2,1,0:T(8,128)(2,1)} %get-tuple-element.38), channel_id=1, source_target_pairs={{0,8},{8,0},{1,9},{9,1},{2,10},{10,2},{3,11},{11,3},{4,12},{12,4},... | collective-permute-start | bytes 3538952 | tf_op jit(solution)/shard_map/ppermute | solution.py:867
  67.6 17.3 %copy-start.15 = (bf16[128]{0:T(256)(128)(2,1)S(1)}, bf16[128]{0:T(256)(128)(2,1)}, u32[]{:S(2)}) copy-start(bf16[128]{0:T(256)(128)(2,1)} %param.36) | copy-start | bytes 772
  67.6 17.4 %copy-start.2 = (bf16[48,96,128]{2,1,0:T(8,128)(2,1)S(1)}, bf16[48,96,128]{2,1,0:T(8,128)(2,1)}, u32[]{:S(2)}) copy-start(bf16[48,96,128]{2,1,0:T(8,128)(2,1)} %pair_hbm.1) | copy-start | bytes 3538948
  67.6 17.4 %copy-start.3 = (bf16[128,128]{1,0:T(8,128)(2,1)S(1)}, bf16[128,128]{1,0:T(8,128)(2,1)}, u32[]{:S(2)}) copy-start(bf16[128,128]{1,0:T(8,128)(2,1)} %w_ref.1) | copy-start | bytes 98308
  91.4 29.0 %copy-start.4 = (bf16[3,2,768,128]{3,2,1,0:T(8,128)(2,1)S(1)}, bf16[3,2,768,128]{3,2,1,0:T(8,128)(2,1)}, u32[]{:S(2)}) copy-start(bf16[3,2,768,128]{3,2,1,0:T(8,128)(2,1)} %get-tuple-element.49.keep_hbm) | copy-start | bytes 3538948
  91.4 29.0 %copy-start.5 = (f32[16]{0:T(128)S(1)}, f32[16]{0:T(128)}, u32[]{:S(2)}) copy-start(f32[16]{0:T(128)} %weight_ref.1) | copy-start | bytes 196
  117.7 12.2 %collective-permute-start.4 = (bf16[4,48,768]{2,1,0:T(8,128)(2,1)S(1)}, bf16[4,48,768]{2,1,0:T(8,128)(2,1)S(1)}, u32[]{:S(2)}, u32[]{:S(2)}) collective-permute-start(bf16[4,48,768]{2,1,0:T(8,128)(2,1)S(1)} %pad_maximum_fusion.1), channel_id=1, source_target_pairs={{0,4},{4,0},{1,5},{5,1},{2,6},{6,2},{3,7},{7,3},{8,12},{12,8},{9,1... | collective-permute-start | bytes 884744 | tf_op jit(solution)/shard_map/ppermute | solution.py:899
  130.0 17.9 %all-to-all-start.3 = ((bf16[16,3,48,128]{3,2,1,0:T(8,128)(2,1)}), bf16[16,3,48,128]{3,2,1,0:T(8,128)(2,1)S(1)}, u32[]{:S(2)}, u32[]{:S(2)}) async-start(bf16[16,3,48,128]{3,2,1,0:T(8,128)(2,1)} %get-tuple-element.55), calls=%async_computation.3 | async-start | bytes 1179648 | tf_op jit(solution)/shard_map/all_to_all | solution.py:805
  147.9 24.2 %all-to-all-start.4 = ((bf16[128,40,128]{2,1,0:T(8,128)(2,1)}), bf16[128,40,128]{2,1,0:T(8,128)(2,1)S(1)}, u32[]{:S(2)}, u32[]{:S(2)}) async-start(bf16[128,40,128]{2,1,0:T(8,128)(2,1)} %bitcast.41), calls=%async_computation.4 | async-start | bytes 2621440 | tf_op jit(solution)/shard_map/all_to_all | solution.py:805
  151.6 2.9 %collective-permute-start.5 = (bf16[8,48,768]{2,1,0:T(8,128)(2,1)S(1)}, bf16[8,48,768]{2,1,0:T(8,128)(2,1)S(1)}, u32[]{:S(2)}, u32[]{:S(2)}) collective-permute-start(bf16[8,48,768]{2,1,0:T(8,128)(2,1)S(1)} %pad_maximum_fusion.ring_hbm), channel_id=1, source_target_pairs={{0,8},{8,0},{1,9},{9,1},{2,10},{10,2},{3,11},{11,3},{4,12},{12,4},... | collective-permute-start | bytes 1769480 | tf_op jit(solution)/shard_map/ppermute | solution.py:905
